TPU v7x, 32 devices: a whole 2x2x4 slice. The times are simulated.
32 devices in a mesh: grp: 2 (over y), seq: 16 (over z, x, core).
Axes of the slice: x: 2, y: 2, z: 4, core: 2. Of those that a mesh axis runs over, the one named last changes fastest.
Arguments:
- queries: bfloat16 [192, 8, 4096], P('seq', 'grp'), parts along dimension 1, may hold values from -7 to 7
- keys: bfloat16 [192, 8, 4096], P('seq', 'grp'), parts along dimension 1, may hold values from -7 to 7
- values: bfloat16 [192, 8, 4096], P('seq', 'grp'), parts along dimension 1, may hold values from -6 to 6
- clip_frames: int32 [8], P('grp'), parts along dimension 0, may hold values from 1 to 8, as said below
Outputs:
- attended: bfloat16 [192, 8, 4096], P('seq', 'grp'), parts along dimension 1
There are 2 independent parts, one for each index of `grp`. A program takes and returns all parts, laid end to end along the dimension named above; each array names one. Nothing has to cross between parts.
Inputs may be any that keep to these rules, and one draw needn't show every extreme that they name: Tokens of clip s at positions clip_frames[s] * 24 and later hold no data; some clip has all 8 frames.
All inputs are finite; a program needn't handle non-finite values.
Results may differ from a plain program's by a relative error of at most 0.0048.
Values may be sent and summed in bfloat16 or wider, within the bound.
No kernel may reach another device: no remote copies, remote signals or barrier semaphores. Data moves between devices by JAX's collectives and lax.ppermute only.
A program may use at most 64 MiB of HBM per device.

v0:
```python
import math

import jax
import jax.numpy as jnp
from jax import lax
from jax.sharding import PartitionSpec as P

HEADS = 32
HDIM = 128
FRAMES = 8


neg_large = -1e30


def attend_block(query_block, key_rows, value_rows, key_bias):
    scores = jnp.einsum("qnd,knd->nqk", query_block, key_rows, preferred_element_type=jnp.float32)
    scores = scores * (1.0 / math.sqrt(HDIM)) + jnp.transpose(key_bias)[:, None, :]
    row_max = jnp.max(scores, axis=2, keepdims=True)
    exponent = jnp.exp(scores - row_max)
    weights = (exponent / jnp.sum(exponent, axis=2, keepdims=True)).astype(jnp.bfloat16)
    combined = jnp.einsum("nqk,knd->qnd", weights, value_rows, preferred_element_type=jnp.float32)
    return combined.astype(jnp.bfloat16)


def attend_all(query_rows, key_rows, value_rows, key_bias):
    length, item_count, head_dim = query_rows.shape
    block_rows = min(512, length)
    blocked = query_rows.reshape(length // block_rows, block_rows, item_count, head_dim)
    combined = lax.map(
        lambda query_block: attend_block(query_block, key_rows, value_rows, key_bias), blocked
    )
    return combined.reshape(length, item_count, head_dim)


def body(queries, keys, values, clip_frames):
    tokens, seq_count, feature_dim = queries.shape
    devices = lax.axis_size("seq")
    device_index = lax.axis_index("seq")
    slot_count = seq_count * HEADS
    per_device = slot_count // devices
    length = tokens * devices
    frame_tokens = length // FRAMES
    query_slots = queries.reshape(tokens, devices, per_device, HDIM)
    key_slots = keys.reshape(tokens, devices, per_device, HDIM)
    value_slots = values.reshape(tokens, devices, per_device, HDIM)
    slot_limit = jnp.repeat(clip_frames * frame_tokens, HEADS)
    query_all, key_all, value_all = (
        lax.all_to_all(query_slots, "seq", split_axis=1, concat_axis=0, tiled=True),
        lax.all_to_all(key_slots, "seq", split_axis=1, concat_axis=0, tiled=True),
        lax.all_to_all(value_slots, "seq", split_axis=1, concat_axis=0, tiled=True),
    )
    own_limit = lax.dynamic_slice_in_dim(slot_limit, device_index * per_device, per_device)
    key_place = jnp.arange(length, dtype=jnp.int32)
    key_bias = jnp.where(key_place[:, None] < own_limit[None, :], 0.0, neg_large).astype(
        jnp.float32
    )
    combined = attend_all(
        query_all.reshape(length, per_device, HDIM),
        key_all.reshape(length, per_device, HDIM),
        value_all.reshape(length, per_device, HDIM),
        key_bias,
    )
    combined = combined.reshape(length, 1, per_device, HDIM)
    returned = lax.all_to_all(combined, "seq", split_axis=0, concat_axis=1, tiled=True)
    return returned.reshape(tokens, seq_count, feature_dim)


def solution(mesh):
    return jax.shard_map(
        body,
        mesh=mesh,
        in_specs=(P("seq", "grp", None), P("seq", "grp", None), P("seq", "grp", None), P("grp")),
        out_specs=P("seq", "grp", None),
        check_vma=False,
    )
```

profile of v0, /device:TPU:0, one launch (start us, length us, event | category | flops | bytes accessed | tf_op | source)
XLA Modules:
  0.0 70.6 jit_solution(1180711210621695569)
XLA Ops:
  0.0 0.0 copy-start
  0.0 1.5 %reshape.47 = bf16[12,16,8,128]{3,2,1,0:T(8,128)(2,1)S(1)} reshape(bf16[12,4,4096]{2,1,0:T(4,128)(2,1)} %param.4) | data formatting | bytes 786432 | tf_op jit(solution)/shard_map/reshape | solution.py:44
  1.5 0.8 %copy.24 = bf16[12,16,8,128]{3,2,0,1:T(8,128)(2,1)} copy(bf16[12,16,8,128]{3,2,1,0:T(8,128)(2,1)S(1)} %reshape.47) | data formatting | bytes 786432 | tf_op jit(solution)/shard_map/reshape | solution.py:44
  2.3 0.0 copy-start.1
  2.3 7.5 %all-to-all-start = ((bf16[12,16,8,128]{3,2,0,1:T(8,128)(2,1)}), bf16[12,16,8,128]{3,2,0,1:T(8,128)(2,1)S(1)}, u32[]{:S(2)}, u32[]{:S(2)}) async-start(bf16[12,16,8,128]{3,2,0,1:T(8,128)(2,1)} %copy.24), calls=%async_computation | async-start | bytes 786432 | tf_op jit(solution)/shard_map/all_to_all | solution.py:49
  9.8 0.0 copy-done
  9.8 0.4 reshape.48
  10.2 0.8 %copy.25 = bf16[12,16,8,128]{3,2,0,1:T(8,128)(2,1)} copy(bf16[12,16,8,128]{3,2,1,0:T(8,128)(2,1)S(1)} %reshape.48) | data formatting | bytes 786432 | tf_op jit(solution)/shard_map/reshape | solution.py:45
  11.0 0.0 copy-start.2
  11.0 11.0 %all-to-all-done = bf16[12,16,8,128]{3,2,0,1:T(8,128)(2,1)S(1)} async-done(((bf16[12,16,8,128]{3,2,0,1:T(8,128)(2,1)}), bf16[12,16,8,128]{3,2,0,1:T(8,128)(2,1)S(1)}, u32[]{:S(2)}, u32[]{:S(2)}) %all-to-all-start) | async-done | bytes 393248 | tf_op jit(solution)/shard_map/all_to_all | solution.py:49
  22.0 3.6 %all-to-all-start.1 = ((bf16[12,16,8,128]{3,2,0,1:T(8,128)(2,1)}), bf16[12,16,8,128]{3,2,0,1:T(8,128)(2,1)S(1)}, u32[]{:S(2)}, u32[]{:S(2)}) async-start(bf16[12,16,8,128]{3,2,0,1:T(8,128)(2,1)} %copy.25), calls=%async_computation.1 | async-start | bytes 786432 | tf_op jit(solution)/shard_map/all_to_all | solution.py:50
  25.5 0.0 copy-done.1
  25.5 0.4 reshape.51
  26.0 0.8 %copy.28 = bf16[12,16,8,128]{3,2,0,1:T(8,128)(2,1)} copy(bf16[12,16,8,128]{3,2,1,0:T(8,128)(2,1)S(1)} %reshape.51) | data formatting | bytes 786432 | tf_op jit(solution)/shard_map/reshape | solution.py:46
  26.8 10.9 %all-to-all-done.1 = bf16[12,16,8,128]{3,2,0,1:T(8,128)(2,1)S(1)} async-done(((bf16[12,16,8,128]{3,2,0,1:T(8,128)(2,1)}), bf16[12,16,8,128]{3,2,0,1:T(8,128)(2,1)S(1)}, u32[]{:S(2)}, u32[]{:S(2)}) %all-to-all-start.1) | async-done | bytes 393248 | tf_op jit(solution)/shard_map/all_to_all | solution.py:50
  37.7 3.6 %all-to-all-start.2 = ((bf16[12,16,8,128]{3,2,0,1:T(8,128)(2,1)}), bf16[12,16,8,128]{3,2,0,1:T(8,128)(2,1)S(1)}, u32[]{:S(2)}, u32[]{:S(2)}) async-start(bf16[12,16,8,128]{3,2,0,1:T(8,128)(2,1)} %copy.28), calls=%async_computation.2 | async-start | bytes 786432 | tf_op jit(solution)/shard_map/all_to_all | solution.py:51
  41.3 0.0 copy-done.2
  41.3 0.1 broadcast_in_dim.23
  41.4 0.1 reshape.50
  41.4 0.1 dynamic_slice.6
  41.5 0.1 fusion.11
  41.6 0.7 fusion.18
  42.3 11.1 %all-to-all-done.2 = bf16[12,16,8,128]{3,2,0,1:T(8,128)(2,1)S(1)} async-done(((bf16[12,16,8,128]{3,2,0,1:T(8,128)(2,1)}), bf16[12,16,8,128]{3,2,0,1:T(8,128)(2,1)S(1)}, u32[]{:S(2)}, u32[]{:S(2)}) %all-to-all-start.2) | async-done | bytes 393248 | tf_op jit(solution)/shard_map/all_to_all | solution.py:51
  53.4 0.5 fusion.3
  53.9 0.3 copy.31
  54.2 15.5 %all_to_all.60 = bf16[192,1,8,128]{3,2,1,0:T(8,128)(2,1)S(1)} all-to-all(bf16[192,1,8,128]{3,2,1,0:T(8,128)(2,1)S(1)} %copy.31), channel_id=1, replica_groups=mesh['grp'=2,'seq'=16] {'seq'}, dimensions={0} | all-to-all | bytes 786432 | tf_op jit(solution)/shard_map/all_to_all | solution.py:65
  69.7 0.1 copy.32
  69.8 0.8 %reshape.53 = bf16[12,4,4096]{2,1,0:T(4,128)(2,1)} reshape(bf16[12,16,1,8,128]{4,3,1,0,2:T(8,128)(2,1)S(1)} %copy.32) | data formatting | bytes 786432 | tf_op jit(solution)/shard_map/reshape | solution.py:66
  (1 shorter events, 0.0 us)
Async XLA Ops:
  0.0 9.8 %copy-start = (bf16[12,4,4096]{2,1,0:T(4,128)(2,1)S(1)}, bf16[12,4,4096]{2,1,0:T(4,128)(2,1)}, u32[]{:S(2)}) copy-start(bf16[12,4,4096]{2,1,0:T(4,128)(2,1)} %param.5) | copy-start | bytes 1179652
  2.3 23.3 %copy-start.1 = (bf16[12,4,4096]{2,1,0:T(4,128)(2,1)S(1)}, bf16[12,4,4096]{2,1,0:T(4,128)(2,1)}, u32[]{:S(2)}) copy-start(bf16[12,4,4096]{2,1,0:T(4,128)(2,1)} %param.6) | copy-start | bytes 1179652
  2.3 19.7 %all-to-all-start = ((bf16[12,16,8,128]{3,2,0,1:T(8,128)(2,1)}), bf16[12,16,8,128]{3,2,0,1:T(8,128)(2,1)S(1)}, u32[]{:S(2)}, u32[]{:S(2)}) async-start(bf16[12,16,8,128]{3,2,0,1:T(8,128)(2,1)} %copy.24), calls=%async_computation | async-start | bytes 786432 | tf_op jit(solution)/shard_map/all_to_all | solution.py:49
  11.0 30.2 %copy-start.2 = (s32[4]{0:T(128)S(1)}, s32[4]{0:T(128)}, u32[]{:S(2)}) copy-start(s32[4]{0:T(128)} %param.7) | copy-start | bytes 52
  22.0 15.7 %all-to-all-start.1 = ((bf16[12,16,8,128]{3,2,0,1:T(8,128)(2,1)}), bf16[12,16,8,128]{3,2,0,1:T(8,128)(2,1)S(1)}, u32[]{:S(2)}, u32[]{:S(2)}) async-start(bf16[12,16,8,128]{3,2,0,1:T(8,128)(2,1)} %copy.25), calls=%async_computation.1 | async-start | bytes 786432 | tf_op jit(solution)/shard_map/all_to_all | solution.py:50
  37.7 15.7 %all-to-all-start.2 = ((bf16[12,16,8,128]{3,2,0,1:T(8,128)(2,1)}), bf16[12,16,8,128]{3,2,0,1:T(8,128)(2,1)S(1)}, u32[]{:S(2)}, u32[]{:S(2)}) async-start(bf16[12,16,8,128]{3,2,0,1:T(8,128)(2,1)} %copy.28), calls=%async_computation.2 | async-start | bytes 786432 | tf_op jit(solution)/shard_map/all_to_all | solution.py:51
where the time goes:
time: 71.1 us; the launch traced here: 70.6 us
  waiting for transfers between devices  33 us (46%)
  blocking collectives  15.5 us (22%)
  starting transfers between devices  14.6 us (21%)
  local copies, waits for them, and re-layouts  6.16 us (9%)
  matrix products  1.19 us (2%)
    all_to_all x1, blocking collectives, body(): lax.all_to_all(combined, 'seq', split_axis=0, concat_axis=1, tiled=True)  15.5 us
    all_to_all x1, waiting for transfers between devices, body(): lax.all_to_all(value_slots, 'seq', split_axis=1, concat_axis=0, tiled=True)  11.1 us
    all_to_all x1, waiting for transfers between devices, body(): lax.all_to_all(query_slots, 'seq', split_axis=1, concat_axis=0, tiled=True)  11 us
    all_to_all x1, waiting for transfers between devices, body(): lax.all_to_all(key_slots, 'seq', split_axis=1, concat_axis=0, tiled=True)  10.9 us
    all_to_all x1, starting transfers between devices, body(): lax.all_to_all(query_slots, 'seq', split_axis=1, concat_axis=0, tiled=True)  7.49 us
    all_to_all x1, starting transfers between devices, body(): lax.all_to_all(key_slots, 'seq', split_axis=1, concat_axis=0, tiled=True)  3.55 us
    all_to_all x1, starting transfers between devices, body(): lax.all_to_all(value_slots, 'seq', split_axis=1, concat_axis=0, tiled=True)  3.55 us
    reshape x2, local copies, waits for them, and re-layouts, body(): query_slots = queries.reshape(tokens, devices, per_device, HDIM)  2.27 us
  transfers between devices with their start and end apart: 3, of which 3 were waited for; matrix products, arithmetic and copies ran while one was open for 5% of the time, Pallas kernels for 0%

commit v1 on v0

v1 whole, which is shorter than its diff:
```python
import math
import jax
import jax.numpy as jnp
from jax import lax
from jax.sharding import PartitionSpec as P

HEADS = 32
HDIM = 128
FRAMES = 8
neg_large = -1e30

def attend(query_rows, key_rows, value_rows, key_bias):
    scores = jnp.einsum("qnd,knd->nqk", query_rows, key_rows, preferred_element_type=jnp.float32)
    scores = scores * (1.0 / math.sqrt(HDIM)) + key_bias[:, None, :]
    row_max = jnp.max(scores, axis=2, keepdims=True)
    exponent = jnp.exp(scores - row_max)
    weights = (exponent / jnp.sum(exponent, axis=2, keepdims=True)).astype(jnp.bfloat16)
    combined = jnp.einsum("nqk,knd->qnd", weights, value_rows, preferred_element_type=jnp.float32)
    return combined.astype(jnp.bfloat16)

def body(queries, keys, values, clip_frames):
    tokens, seq_count, feature_dim = queries.shape
    devices = lax.axis_size("seq")
    me = lax.axis_index("seq")
    slot_count = seq_count * HEADS
    per_device = slot_count // devices
    length = tokens * devices
    frame_tokens = length // FRAMES
    own = (jnp.arange(per_device, dtype=jnp.int32) + me * per_device) // HEADS
    limit = clip_frames[own] * frame_tokens
    place = jnp.arange(length, dtype=jnp.int32)
    key_bias = jnp.where(place[None, :] < limit[:, None], 0.0, neg_large).astype(jnp.float32)
    packed = jnp.stack([x.reshape(tokens, devices, per_device, HDIM) for x in (queries, keys, values)])
    packed = jnp.transpose(packed, (2, 0, 1, 3, 4))
    got = lax.all_to_all(packed, "seq", split_axis=0, concat_axis=0, tiled=True)
    got = jnp.transpose(got, (1, 0, 2, 3, 4)).reshape(3, length, per_device, HDIM)
    combined = attend(got[0], got[1], got[2], key_bias)
    combined = combined.reshape(devices, tokens, per_device, HDIM)
    returned = lax.all_to_all(combined, "seq", split_axis=0, concat_axis=0, tiled=True)
    return jnp.transpose(returned, (1, 0, 2, 3)).reshape(tokens, seq_count, feature_dim)

def solution(mesh):
    return jax.shard_map(
        body, mesh=mesh,
        in_specs=(P("seq", "grp", None), P("seq", "grp", None), P("seq", "grp", None), P("grp")),
        out_specs=P("seq", "grp", None), check_vma=False)
```

time: 71.1 us -> 59.5 us (0.84)
  waiting for transfers between devices: 33 us -> 24.4 us
  starting transfers between devices: 14.6 us -> 7.36 us
  blocking collectives: 15.5 us -> 19.5 us
    all_to_all x3 -> x1, waiting for transfers between devices: 33 us -> 24.4 us  [body(): got = lax.all_to_all(packed, 'seq', split_axis=0, concat_axis=0, tiled=True)]
    all_to_all x3 -> x1, starting transfers between devices: 14.6 us -> 7.36 us  [body(): got = lax.all_to_all(packed, 'seq', split_axis=0, concat_axis=0, tiled=True)]
    reshape x8 -> x1, local copies, waits for them, and re-layouts: 5.65 us -> 0.84 us  [body(): jnp.transpose(returned, (1, 0, 2, 3))]
    all_to_all x1, blocking collectives: 15.5 us -> 19.5 us  [body(): lax.all_to_all(combined, 'seq', split_axis=0, concat_axis=0, tiled=True)]
    another operation x1 -> x3, local copies, waits for them, and re-layouts: 0.26 us -> 3.28 us  [body(): jnp.stack([x.reshape(tokens, devices, per_device, HDIM) for x in (queries...]
    transpose x0 -> x2, local copies, waits for them, and re-layouts: none -> 1.3 us  [the longest x1 1.21 us: body(): packed = jnp.transpose(packed, (2, 0, 1, 3, 4))]
  transfers between devices with their start and end apart: 3 -> 1, of which waited for: 3 -> 1; matrix products, arithmetic and copies ran while one was open for 5% -> 1% of each run, Pallas kernels for 0% -> 0%
where the time goes in v1:
time: 59.5 us; the launch traced here: 59.2 us
  waiting for transfers between devices  24.4 us (41%)
  blocking collectives  19.5 us (33%)
  starting transfers between devices  7.36 us (12%)
  local copies, waits for them, and re-layouts  6.52 us (11%)
  matrix products  1.2 us (2%)
    all_to_all x1, waiting for transfers between devices, body(): got = lax.all_to_all(packed, 'seq', split_axis=0, concat_axis=0, tiled=True)  24.4 us
    all_to_all x1, blocking collectives, body(): lax.all_to_all(combined, 'seq', split_axis=0, concat_axis=0, tiled=True)  19.5 us
    all_to_all x1, starting transfers between devices, body(): got = lax.all_to_all(packed, 'seq', split_axis=0, concat_axis=0, tiled=True)  7.36 us
    another operation x3, local copies, waits for them, and re-layouts, body(): jnp.stack([x.reshape(tokens, devices, per_device, HDIM) for x in (queries...  3.28 us
    transpose x1, local copies, waits for them, and re-layouts, body(): packed = jnp.transpose(packed, (2, 0, 1, 3, 4))  1.21 us
  transfers between devices with their start and end apart: 1, of which 1 were waited for; matrix products, arithmetic and copies ran while one was open for 1% of the time, Pallas kernels for 0%

profile of v1, /device:TPU:0, one launch (start us, length us, event | category | flops | bytes accessed | tf_op | source)
XLA Modules:
  0.0 59.2 jit_solution(1196090832173480917)
XLA Ops:
  0.0 0.0 copy-start
  0.0 0.0 copy-start.1
  0.0 1.5 %stack_reshape.9 = bf16[1,12,16,8,128]{4,3,2,1,0:T(8,128)(2,1)S(1)} reshape(bf16[12,4,4096]{2,1,0:T(4,128)(2,1)} %param.4) | data formatting | bytes 786432 | tf_op jit(solution)/shard_map/stack;reshape | solution.py:33
  1.5 1.4 %stack_reshape.10 = bf16[1,12,16,8,128]{4,3,2,1,0:T(8,128)(2,1)S(1)} reshape(bf16[12,4,4096]{2,1,0:T(4,128)(2,1)} %param.5) | data formatting | bytes 786432 | tf_op jit(solution)/shard_map/stack;reshape | solution.py:33
  2.9 0.0 copy-done.1
  2.9 0.4 stack_reshape.11
  3.3 0.1 maximum_bitcast_fusion
  3.4 1.2 %copy.24 = bf16[16,3,12,8,128]{4,3,2,1,0:T(8,128)(2,1)} copy(bf16[16,3,12,8,128]{4,3,0,2,1:T(8,128)(2,1)S(1)} %maximum_bitcast_fusion) | data formatting | bytes 2359296 | tf_op jit(solution)/shard_map/transpose | solution.py:34
  4.7 7.4 %all-to-all-start = ((bf16[16,3,12,8,128]{4,3,2,1,0:T(8,128)(2,1)}), bf16[16,3,12,8,128]{4,3,2,1,0:T(8,128)(2,1)S(1)}, u32[]{:S(2)}, u32[]{:S(2)}) async-start(bf16[16,3,12,8,128]{4,3,2,1,0:T(8,128)(2,1)} %copy.24), calls=%async_computation | async-start | bytes 2359296 | tf_op jit(solution)/shard_map/all_to_all | solution.py:35
  12.1 0.0 copy-done
  12.1 0.6 %gather_fusion = s32[8]{0:T(128)S(1)} fusion(s32[4]{0:T(128)S(1)} %copy-done, s32[1024]{0:T(1024)S(1)} %pad_clamp_fusion), kind=kCustom, calls=%fused_computation | custom fusion | bytes 96 | tf_op jit(solution)/shard_map/gather | solution.py:30
  12.7 0.1 fusion.11
  12.8 24.4 %all-to-all-done = bf16[16,3,12,8,128]{4,3,2,1,0:T(8,128)(2,1)S(1)} async-done(((bf16[16,3,12,8,128]{4,3,2,1,0:T(8,128)(2,1)}), bf16[16,3,12,8,128]{4,3,2,1,0:T(8,128)(2,1)S(1)}, u32[]{:S(2)}, u32[]{:S(2)}) %all-to-all-start) | async-done | bytes 1179680 | tf_op jit(solution)/shard_map/all_to_all | solution.py:35
  37.2 0.1 copy.52
  37.3 0.1 fusion.19
  37.4 0.7 %fusion.20 = (f32[8,192]{1,0:T(8,128)S(1)}, f32[8,192,192]{1,2,0:T(8,128)S(1)}) fusion(f32[8,192]{1,0:T(8,128)S(1)} %fusion.11, bf16[192,8,128]{2,1,0:T(8,128)(2,1)S(1)} %bitcast.20, bf16[192,8,128]{2,1,0:T(8,128)(2,1)S(1)} %bitcast.21), kind=kOutput, calls=%fused_computation.26 | convolution fusion | flops 76677312 | bytes 1978368 | tf_op jit(solution)/shard_map/sub | solution.py:16
  38.1 0.5 fusion.3
  38.6 0.3 copy.30
  38.8 19.5 %all_to_all.10 = bf16[16,12,8,128]{3,2,1,0:T(8,128)(2,1)S(1)} all-to-all(bf16[16,12,8,128]{3,2,1,0:T(8,128)(2,1)S(1)} %bitcast.17), channel_id=1, replica_groups=mesh['grp'=2,'seq'=16] {'seq'}, dimensions={0} | all-to-all | bytes 786432 | tf_op jit(solution)/shard_map/all_to_all | solution.py:39
  58.3 0.1 copy.31
  58.4 0.8 %reshape.98 = bf16[12,4,4096]{2,1,0:T(4,128)(2,1)} reshape(bf16[12,16,8,128]{3,2,1,0:T(8,128)(2,1)S(1)} %copy.31) | data formatting | bytes 786432 | tf_op jit(solution)/shard_map/reshape | solution.py:40
  (3 shorter events, 0.0 us)
Async XLA Ops:
  0.0 12.1 %copy-start = (s32[4]{0:T(128)S(1)}, s32[4]{0:T(128)}, u32[]{:S(2)}) copy-start(s32[4]{0:T(128)} %param.7) | copy-start | bytes 52
  0.0 2.9 %copy-start.1 = (bf16[12,4,4096]{2,1,0:T(4,128)(2,1)S(1)}, bf16[12,4,4096]{2,1,0:T(4,128)(2,1)}, u32[]{:S(2)}) copy-start(bf16[12,4,4096]{2,1,0:T(4,128)(2,1)} %param.6) | copy-start | bytes 1179652
  4.7 32.5 %all-to-all-start = ((bf16[16,3,12,8,128]{4,3,2,1,0:T(8,128)(2,1)}), bf16[16,3,12,8,128]{4,3,2,1,0:T(8,128)(2,1)S(1)}, u32[]{:S(2)}, u32[]{:S(2)}) async-start(bf16[16,3,12,8,128]{4,3,2,1,0:T(8,128)(2,1)} %copy.24), calls=%async_computation | async-start | bytes 2359296 | tf_op jit(solution)/shard_map/all_to_all | solution.py:35

commit v2 on v1

v2 whole, which is shorter than its diff:
```python
import functools
import math
import jax
import jax.numpy as jnp
from jax import lax
from jax.experimental import pallas as pl
from jax.experimental.pallas import tpu as pltpu
from jax.sharding import PartitionSpec as P

HEADS = 32
HDIM = 128
FRAMES = 8
neg_large = -1e30
VM = pl.BlockSpec(memory_space=pltpu.VMEM)
HB = pl.BlockSpec(memory_space=pltpu.HBM)
SM = pl.BlockSpec(memory_space=pltpu.SMEM)
LARGE = pltpu.CompilerParams(vmem_limit_bytes=24 * 1024 * 1024)
SMALL = pltpu.CompilerParams(vmem_limit_bytes=8 * 1024 * 1024)


def cost(micros):
    return pl.CostEstimate(flops=int(micros * 1e9), bytes_accessed=int(micros * 3e6), transcendentals=0)


def position(outer):
    me = lax.axis_index("seq")
    return me // (lax.axis_size("seq") // outer), me % 2


def pack_kernel(outer, *refs):
    srcs, (own, peer, sem) = refs[:-3], refs[-3:]
    heads = own.shape[3]
    line, core = position(outer)
    copies = []
    for i, dst in ((1, peer), (0, own)):
        for a in range(outer):
            group = jnp.bitwise_xor(line, a) * 2 + jnp.bitwise_xor(core, i)
            for j, src in enumerate(srcs):
                copies.append(pltpu.make_async_copy(
                    src.at[:, pl.ds(group * heads, heads)], dst.at[a, j], sem.at[i, a, j]))
    for c in copies:
        c.start()
    for c in copies:
        c.wait()


def pack(outer, *srcs):
    tokens, _, clips, _ = srcs[0].shape
    heads = HEADS // (2 * outer)
    shape = jax.ShapeDtypeStruct((outer, len(srcs), tokens, heads, clips, HDIM), jnp.bfloat16)
    own, peer = pl.pallas_call(
        functools.partial(pack_kernel, outer),
        out_shape=[shape, shape], in_specs=[HB] * len(srcs), out_specs=[VM, VM],
        scratch_shapes=[pltpu.SemaphoreType.DMA((2, outer, len(srcs)))], compiler_params=SMALL,
    )(*srcs)
    shape = (outer, len(srcs), tokens, heads * clips, HDIM)
    return own.reshape(shape), peer.reshape(shape)


def turn(pieces, j):
    return jnp.swapaxes(jnp.concatenate([x[j, c] for x in pieces for c in range(2)], axis=0), 0, 1)


def query_kernel(*refs):
    srcs, out = refs[:-1], refs[-1]
    out[...] = turn(srcs, 0)


def near_kernel(marks, frame_tokens, frames_ref, *refs):
    kvs, (k_out, v_out, bias_out) = refs[:-3], refs[-3:]
    k_out[...] = turn(kvs, 0)
    v_out[...] = turn(kvs, 1)
    clips, length = bias_out.shape
    tokens = length // len(marks)
    me = lax.axis_index("seq")
    key = lax.broadcasted_iota(jnp.int32, (1, length), 1)
    place = jnp.zeros((1, length), jnp.int32)
    for s, mark in enumerate(marks):
        start = jnp.bitwise_xor(me, mark) * tokens - s * tokens
        place = jnp.where(key >= s * tokens, key + start, place)
    for c in range(clips):
        bias_out[c:c + 1, :] = jnp.where(place < frames_ref[c] * frame_tokens, 0.0, neg_large)


def main_kernel(nkv, q, *refs):
    kvs, (k_near, v_near, bias), outs = refs[:nkv], refs[nkv:nkv + 3], refs[nkv + 3:]
    k = jnp.concatenate([k_near[...], turn(kvs, 0)], axis=1)
    v = jnp.concatenate([v_near[...], turn(kvs, 1)], axis=1)
    slots = k.shape[0]
    clips = bias.shape[0]
    s = lax.dot_general(q[...], k, (((2,), (2,)), ((0,), (0,))), preferred_element_type=jnp.float32)
    s = s * (1.0 / math.sqrt(HDIM)) + jnp.concatenate([bias[...]] * (slots // clips), axis=0)[:, None, :]
    e = jnp.exp(s - jnp.max(s, axis=2, keepdims=True))
    w = (e / jnp.sum(e, axis=2, keepdims=True)).astype(jnp.bfloat16)
    o = lax.dot_general(w, v, (((2,), (1,)), ((0,), (0,))), preferred_element_type=jnp.float32)
    o = jnp.swapaxes(o.astype(jnp.bfloat16), 0, 1)
    tokens = outs[0].shape[1]
    for i, out in enumerate(outs):
        for c in range(2):
            out[c] = o[(2 * i + c) * tokens:(2 * i + c + 1) * tokens]


def unpack_kernel(outer, order, *refs):
    kept, came, out = refs[:outer], refs[outer:-1], refs[-1]
    heads = kept[0].shape[2]
    line, core = position(outer)
    for i, a in enumerate(order):
        group = jnp.bitwise_xor(line, a) * 2
        out[:, pl.ds((group + core) * heads, heads)] = kept[i][0]
        out[:, pl.ds((group + 1 - core) * heads, heads)] = came[i][1]


def after(x, y):
    y = y[(0,) * (y.ndim - 1)]
    return jnp.where(y == y, x, jnp.zeros_like(x))


def body(queries, keys, values, clip_frames):
    tokens, clips, features = queries.shape
    devices = lax.axis_size("seq")
    outer = 1
    while outer * outer < devices:
        outer *= 2
    inner = devices // outer
    heads = HEADS // (2 * outer)
    slots = heads * clips
    length = tokens * devices
    bf = jnp.bfloat16

    def swap(x, mask):
        return lax.ppermute(x, "seq", [(i, i ^ mask) for i in range(devices)])

    far = list(range(outer - 1, outer // 2 - 1, -1))
    near = list(range(outer // 2 - 1, -1, -1))
    srcs = [jnp.transpose(x.reshape(tokens, clips, HEADS, HDIM), (0, 2, 1, 3)) for x in (keys, values, queries)]
    kv_own, kv_peer = pack(outer, *srcs[:2])
    q_own, q_peer = pack(outer, srcs[2])
    kv_got, q_got = swap(kv_peer, 1), swap(q_peer, 1)
    kv, qs = {}, {}
    for a in far + near:
        pay = jnp.stack([kv_own[a], kv_got[a]], axis=1)
        kv[a] = swap(pay, a * inner) if a else pay
    for a in far + near:
        pay = jnp.stack([q_own[a], q_got[a]], axis=1)
        if 1 and a:
            pay = after(pay, kv[near[0]])
        qs[a] = swap(pay, a * inner) if a else pay

    def plane(part):
        pieces, marks = [], []
        for a in part:
            stack, mark = [kv[a]], [a * inner]
            step = inner // 2
            while step > 1:
                stack = stack + [swap(x[:2], step) for x in stack]
                mark = mark + [m ^ step for m in mark]
                step //= 2
            pieces += stack
            marks += [m ^ c for m in mark for c in (0, 1)]
        return pieces, marks

    near_pieces, near_marks = plane(near[::-1])
    far_pieces, far_marks = plane(far)
    marks = near_marks + far_marks
    some = jax.ShapeDtypeStruct((slots, length // 2, HDIM), bf)
    k_near, v_near, bias = pl.pallas_call(
        functools.partial(near_kernel, marks, length // FRAMES),
        out_shape=[some, some, jax.ShapeDtypeStruct((clips, length), jnp.float32)],
        in_specs=[SM] + [VM] * len(near_pieces), out_specs=[VM] * 3,
        compiler_params=LARGE, cost_estimate=cost(0.01),
    )(clip_frames, *near_pieces)
    parts = far + near
    q = pl.pallas_call(
        query_kernel, out_shape=jax.ShapeDtypeStruct((slots, outer * 2 * tokens, HDIM), bf),
        in_specs=[VM] * outer, out_specs=VM, compiler_params=SMALL, cost_estimate=cost(0.01),
    )(*[qs[a] for a in parts])
    piece = jax.ShapeDtypeStruct((2, tokens, slots, HDIM), bf)
    res = pl.pallas_call(
        functools.partial(main_kernel, len(far_pieces)),
        out_shape=[piece] * outer,
        in_specs=[VM] * (len(far_pieces) + 4), out_specs=[VM] * outer,
        compiler_params=LARGE, cost_estimate=cost(2),
    )(q, *far_pieces, k_near, v_near, bias)
    outs = [swap(o, a * inner) if a else o for a, o in zip(parts, res)]
    came = [swap(o, 1) for o in outs]
    out = pl.pallas_call(
        functools.partial(unpack_kernel, outer, parts),
        out_shape=jax.ShapeDtypeStruct((tokens, HEADS, clips, HDIM), bf),
        in_specs=[VM] * (2 * outer), out_specs=VM, compiler_params=SMALL,
    )(*[x.reshape(2, tokens, heads, clips, HDIM) for x in outs + came])
    return jnp.transpose(out, (0, 2, 1, 3)).reshape(tokens, clips, features)


def solution(mesh):
    return jax.shard_map(
        body, mesh=mesh,
        in_specs=(P("seq", "grp", None), P("seq", "grp", None), P("seq", "grp", None), P("grp")),
        out_specs=P("seq", "grp", None), check_vma=False)
```

time: 59.5 us -> 53.9 us (0.906)
  blocking collectives: 19.5 us -> 0 us
  starting transfers between devices: 7.36 us -> 26.4 us
  waiting for transfers between devices: 24.4 us -> 20.4 us
  Pallas kernels: 0 us -> 3.46 us
  local copies, waits for them, and re-layouts: 6.52 us -> 3.12 us
  matrix products: 1.2 us -> 0 us
    ppermute x0 -> x19, starting transfers between devices: none -> 26.4 us  [swap(): return lax.ppermute(x, 'seq', [(i, i ^ mask) for i in range(devices)])]
    all_to_all x1 -> x0, waiting for transfers between devices: 24.4 us -> none  [body(): got = lax.all_to_all(packed, 'seq', split_axis=0, concat_axis=0, tiled=True)]
    ppermute x0 -> x19, waiting for transfers between devices: none -> 20.4 us  [swap(): return lax.ppermute(x, 'seq', [(i, i ^ mask) for i in range(devices)])]
    all_to_all x1 -> x0, blocking collectives: 19.5 us -> none  [body(): lax.all_to_all(combined, 'seq', split_axis=0, concat_axis=0, tiled=True)]
    all_to_all x1 -> x0, starting transfers between devices: 7.36 us -> none  [body(): got = lax.all_to_all(packed, 'seq', split_axis=0, concat_axis=0, tiled=True)]
    pallas_call x0 -> x6, Pallas kernels: none -> 3.46 us  [the longest x1 1.31 us: body(): pl.pallas_call(functools.partial(main_kernel, len(far_pieces)), out_shape...]
    another operation x3 -> x2, local copies, waits for them, and re-layouts: 3.28 us -> 0.04 us  [body(): pay = jnp.stack([kv_own[a], kv_got[a]], axis=1)]
    unnamed x4 -> x8, local copies, waits for them, and re-layouts: 0.01 us -> 2.78 us
  transfers between devices with their start and end apart: 1 -> 19, of which waited for: 1 -> 9; matrix products, arithmetic and copies ran while one was open for 1% -> 1% of each run, Pallas kernels for 0% -> 2%
where the time goes in v2:
time: 53.9 us; the launch traced here: 53.7 us
  starting transfers between devices  26.4 us (49%)
  waiting for transfers between devices  20.4 us (38%)
  Pallas kernels  3.46 us (6%)
  local copies, waits for them, and re-layouts  3.12 us (6%)
    ppermute x19, starting transfers between devices, swap(): return lax.ppermute(x, 'seq', [(i, i ^ mask) for i in range(devices)])  26.4 us
    ppermute x19, waiting for transfers between devices, swap(): return lax.ppermute(x, 'seq', [(i, i ^ mask) for i in range(devices)])  20.4 us
    unnamed x8, local copies, waits for them, and re-layouts  2.78 us
    pallas_call x1, Pallas kernels, body(): pl.pallas_call(functools.partial(main_kernel, len(far_pieces)), out_shape...  1.31 us
  transfers between devices with their start and end apart: 19, of which 9 were waited for; matrix products, arithmetic and copies ran while one was open for 1% of the time, Pallas kernels for 2%

profile of v2, /device:TPU:0, one launch (start us, length us, event | category | flops | bytes accessed | tf_op | source)
XLA Modules:
  0.0 53.7 jit_solution(7231075371705279841)
XLA Ops:
  0.0 0.0 copy-start
  0.0 1.0 %copy-done = bf16[12,4,4096]{2,1,0:T(4,128)(2,1)S(1)} copy-done((bf16[12,4,4096]{2,1,0:T(4,128)(2,1)S(1)}, bf16[12,4,4096]{2,1,0:T(4,128)(2,1)}, u32[]{:S(2)}) %copy-start) | copy-done | bytes 393240
  1.0 0.0 copy-start.1
  1.0 1.0 %copy-done.1 = bf16[12,4,4096]{2,1,0:T(4,128)(2,1)S(1)} copy-done((bf16[12,4,4096]{2,1,0:T(4,128)(2,1)S(1)}, bf16[12,4,4096]{2,1,0:T(4,128)(2,1)}, u32[]{:S(2)}) %copy-start.1) | copy-done | bytes 393240
  2.0 0.0 copy-start.2
  2.0 0.3 shard_map.46
  2.3 0.5 collective-permute-start
  2.8 0.2 copy-done.2
  3.0 0.1 shard_map.47
  3.1 0.5 collective-permute-start.2
  3.7 0.1 fusion
  3.8 0.1 fusion.1
  3.9 0.9 %collective-permute-done.2 = bf16[4,1,12,16,128]{4,3,2,1,0:T(8,128)(2,1)S(1)} collective-permute-done((bf16[4,1,12,16,128]{4,3,2,1,0:T(8,128)(2,1)S(1)}, bf16[4,1,12,16,128]{4,3,2,1,0:T(8,128)(2,1)S(1)}, u32[]{:S(2)}, u32[]{:S(2)}) %collective-permute-start.2) | collective-permute-done | bytes 196640 | tf_op jit(solution)/shard_map/ppermute | solution.py:131
  4.7 0.0 collective-permute-done
  4.8 3.0 %collective-permute-start.1 = (bf16[2,2,12,16,128]{4,3,2,0,1:T(8,128)(2,1)S(1)}, bf16[2,2,12,16,128]{4,3,2,0,1:T(8,128)(2,1)S(1)}, u32[]{:S(2)}, u32[]{:S(2)}) collective-permute-start(bf16[2,2,12,16,128]{4,3,2,0,1:T(8,128)(2,1)S(1)} %pad_maximum_fusion), channel_id=1, source_target_pairs={{0,4},{1,5},{2,6},{3,7},{4,0},{5,1},{6,2},{7,3},{8,12},{9,13},{10,... | collective-permute-start | bytes 589832 | tf_op jit(solution)/shard_map/ppermute | solution.py:131
  7.9 1.6 %collective-permute-start.10 = (bf16[2,2,12,16,128]{4,3,2,0,1:T(8,128)(2,1)S(1)}, bf16[2,2,12,16,128]{4,3,2,0,1:T(8,128)(2,1)S(1)}, u32[]{:S(2)}, u32[]{:S(2)}) collective-permute-start(bf16[2,2,12,16,128]{4,3,2,0,1:T(8,128)(2,1)S(1)} %pad_maximum_fusion.3), channel_id=1, source_target_pairs={{0,2},{1,3},{2,0},{3,1},{4,6},{5,7},{6,4},{7,5},{8,10},{9,11},{10,... | collective-permute-start | bytes 589832 | tf_op jit(solution)/shard_map/ppermute | solution.py:131
  9.4 2.5 %collective-permute-start.6 = (bf16[2,2,12,16,128]{4,3,2,0,1:T(8,128)(2,1)S(1)}, bf16[2,2,12,16,128]{4,3,2,0,1:T(8,128)(2,1)S(1)}, u32[]{:S(2)}, u32[]{:S(2)}) collective-permute-start(bf16[2,2,12,16,128]{4,3,2,0,1:T(8,128)(2,1)S(1)} %pad_maximum_fusion.1), channel_id=1, source_target_pairs={{0,12},{1,13},{2,14},{3,15},{4,8},{5,9},{6,10},{7,11},{8,4},{9,5},... | collective-permute-start | bytes 589832 | tf_op jit(solution)/shard_map/ppermute | solution.py:131
  12.0 0.2 collective-permute-start.8
  12.2 0.8 %collective-permute-done.1 = bf16[2,2,12,16,128]{4,3,2,0,1:T(8,128)(2,1)S(1)} collective-permute-done((bf16[2,2,12,16,128]{4,3,2,0,1:T(8,128)(2,1)S(1)}, bf16[2,2,12,16,128]{4,3,2,0,1:T(8,128)(2,1)S(1)}, u32[]{:S(2)}, u32[]{:S(2)}) %collective-permute-start.1) | collective-permute-done | bytes 196640 | tf_op jit(solution)/shard_map/ppermute | solution.py:131
  13.1 7.4 %collective-permute-start.3 = (bf16[1,2,12,16,128]{4,3,2,1,0:T(8,128)(2,1)S(1)}, bf16[1,2,12,16,128]{4,3,2,1,0:T(8,128)(2,1)S(1)}, u32[]{:S(2)}, u32[]{:S(2)}) collective-permute-start(bf16[1,2,12,16,128]{4,3,2,1,0:T(8,128)(2,1)S(1)} %get-tuple-element.45), channel_id=1, source_target_pairs={{0,12},{1,13},{2,14},{3,15},{4,8},{5,9},{6,10},{7,11},{8,4},{9,5},... | collective-permute-start | bytes 294920 | tf_op jit(solution)/shard_map/ppermute | solution.py:131
  20.4 1.5 %collective-permute-start.11 = (bf16[2,2,12,16,128]{4,3,2,0,1:T(8,128)(2,1)S(1)}, bf16[2,2,12,16,128]{4,3,2,0,1:T(8,128)(2,1)S(1)}, u32[]{:S(2)}, u32[]{:S(2)}) collective-permute-start(bf16[2,2,12,16,128]{4,3,2,0,1:T(8,128)(2,1)S(1)} %collective-permute-done.1), channel_id=1, source_target_pairs={{0,2},{1,3},{2,0},{3,1},{4,6},{5,7},{6,4},{7,5},{8,10},{9,11},{10,... | collective-permute-start | bytes 589832 | tf_op jit(solution)/shard_map/ppermute | solution.py:131
  21.9 0.0 collective-permute-done.6
  21.9 0.5 collective-permute-start.7
  22.5 10.1 %collective-permute-done.8.refs_2_ = bf16[2,2,12,16,128]{4,3,2,1,0:T(8,128)(2,1)S(1)} collective-permute-done((bf16[2,2,12,16,128]{4,3,2,1,0:T(8,128)(2,1)S(1)}, bf16[2,2,12,16,128]{4,3,2,1,0:T(8,128)(2,1)S(1)}, u32[]{:S(2)}, u32[]{:S(2)}) %collective-permute-start.8) | collective-permute-done | bytes 196640 | tf_op jit(solution)/shard_map/ppermute | solution.py:131
  32.5 0.5 collective-permute-start.9
  33.1 0.0 collective-permute-done.10
  33.1 0.0 collective-permute-start.4
  33.1 0.0 collective-permute-done.3.refs_0_
  33.1 3.2 %collective-permute-start.5 = (bf16[1,2,12,16,128]{4,3,2,1,0:T(8,128)(2,1)S(1)}, bf16[1,2,12,16,128]{4,3,2,1,0:T(8,128)(2,1)S(1)}, u32[]{:S(2)}, u32[]{:S(2)}) collective-permute-start(bf16[1,2,12,16,128]{4,3,2,1,0:T(8,128)(2,1)S(1)} %get-tuple-element.43), channel_id=1, source_target_pairs={{0,4},{1,5},{2,6},{3,7},{4,0},{5,1},{6,2},{7,3},{8,12},{9,13},{10,... | collective-permute-start | bytes 294920 | tf_op jit(solution)/shard_map/ppermute | solution.py:131
  36.4 3.2 %collective-permute-done.4.refs_1_ = bf16[1,2,12,16,128]{4,3,2,1,0:T(8,128)(2,1)S(1)} collective-permute-done((bf16[1,2,12,16,128]{4,3,2,1,0:T(8,128)(2,1)S(1)}, bf16[1,2,12,16,128]{4,3,2,1,0:T(8,128)(2,1)S(1)}, u32[]{:S(2)}, u32[]{:S(2)}) %collective-permute-start.4) | collective-permute-done | bytes 98336 | tf_op jit(solution)/shard_map/ppermute | solution.py:131
  39.6 0.3 collective-permute-done.5.refs_2_
  39.9 0.1 shard_map.48.q
  40.0 0.0 collective-permute-done.11
  40.1 0.0 copy-start.3
  40.1 0.0 collective-permute-done.7
  40.1 0.6 %copy-done.3 = s32[4]{0:T(128)S(1)} copy-done((s32[4]{0:T(128)S(1)}, s32[4]{0:T(128)}, u32[]{:S(2)}) %copy-start.3) | copy-done | bytes 40
  40.7 0.8 %shard_map.49 = (bf16[16,96,128]{2,1,0:T(8,128)(2,1)S(1)}, bf16[16,96,128]{2,1,0:T(8,128)(2,1)S(1)}, f32[4,192]{1,0:T(4,128)S(1)}) custom-call(s32[4]{0:T(128)S(1)} %copy-done.3, bf16[2,2,12,16,128]{4,3,2,1,0:T(8,128)(2,1)S(1)} %copy.5.refs_0_, bf16[2,2,12,16,128]{4,3,2,1,0:T(8,128)(2,1)S(1)} %copy.6.refs_1_, bf16[2,2,12,16,128]{4,3,2,1,0:T(8,128)(2,1)S(1)} %copy.7.refs_2_, ...), custom_call_target="tpu_custom_call" | custom-call | flops 10000000 | bytes 30000 | tf_op jit(solution)/shard_map/pallas_call | solution.py:166
  41.5 0.0 collective-permute-done.9.refs_3_
  41.5 1.3 %shard_map.50 = (bf16[2,12,16,128]{3,2,1,0:T(8,128)(2,1)S(1)}, bf16[2,12,16,128]{3,2,1,0:T(8,128)(2,1)S(1)}, bf16[2,12,16,128]{3,2,1,0:T(8,128)(2,1)S(1)}, bf16[2,12,16,128]{3,2,1,0:T(8,128)(2,1)S(1)}) custom-call(bf16[16,96,128]{2,1,0:T(8,128)(2,1)S(1)} %shard_map.48.q, bf16[2,2,12,16,128]{4,3,2,1,0:T(8,128)(2,1)S(1)} %copy.9.refs_0_, ...), custom_call_target="tpu_custom_call" | custom-call | flops 2000000000 | bytes 6000000 | tf_op jit(solution)/shard_map/pallas_call | solution.py:178
  42.9 2.3 %collective-permute-start.12 = (bf16[2,12,16,128]{3,2,1,0:T(8,128)(2,1)S(1)}, bf16[2,12,16,128]{3,2,1,0:T(8,128)(2,1)S(1)}, u32[]{:S(2)}, u32[]{:S(2)}) collective-permute-start(bf16[2,12,16,128]{3,2,1,0:T(8,128)(2,1)S(1)} %get-tuple-element.23), channel_id=1, source_target_pairs={{0,12},{1,13},{2,14},{3,15},{4,8},{5,9},{6,10},{7,11},{8,4},{9,5},... | collective-permute-start | bytes 294920 | tf_op jit(solution)/shard_map/ppermute | solution.py:131
  45.2 0.2 collective-permute-start.13
  45.4 1.9 %collective-permute-start.14 = (bf16[2,12,16,128]{3,2,1,0:T(8,128)(2,1)S(1)}, bf16[2,12,16,128]{3,2,1,0:T(8,128)(2,1)S(1)}, u32[]{:S(2)}, u32[]{:S(2)}) collective-permute-start(bf16[2,12,16,128]{3,2,1,0:T(8,128)(2,1)S(1)} %get-tuple-element.25), channel_id=1, source_target_pairs={{0,4},{1,5},{2,6},{3,7},{4,0},{5,1},{6,2},{7,3},{8,12},{9,13},{10,... | collective-permute-start | bytes 294920 | tf_op jit(solution)/shard_map/ppermute | solution.py:131
  47.3 0.0 collective-permute-start.18
  47.3 2.1 %collective-permute-done.12 = bf16[2,12,16,128]{3,2,1,0:T(8,128)(2,1)S(1)} collective-permute-done((bf16[2,12,16,128]{3,2,1,0:T(8,128)(2,1)S(1)}, bf16[2,12,16,128]{3,2,1,0:T(8,128)(2,1)S(1)}, u32[]{:S(2)}, u32[]{:S(2)}) %collective-permute-start.12) | collective-permute-done | bytes 98336 | tf_op jit(solution)/shard_map/ppermute | solution.py:131
  49.4 0.0 collective-permute-start.15
  49.4 2.1 %collective-permute-done.13 = bf16[2,12,16,128]{3,2,1,0:T(8,128)(2,1)S(1)} collective-permute-done((bf16[2,12,16,128]{3,2,1,0:T(8,128)(2,1)S(1)}, bf16[2,12,16,128]{3,2,1,0:T(8,128)(2,1)S(1)}, u32[]{:S(2)}, u32[]{:S(2)}) %collective-permute-start.13) | collective-permute-done | bytes 98336 | tf_op jit(solution)/shard_map/ppermute | solution.py:131
  51.4 0.0 collective-permute-start.16
  51.4 0.0 collective-permute-done.14
  51.4 0.5 collective-permute-start.17
  52.0 0.0 collective-permute-done.18
  52.0 0.0 collective-permute-done.15
  52.0 0.8 %collective-permute-done.16 = bf16[2,12,16,128]{3,2,1,0:T(8,128)(2,1)S(1)} collective-permute-done((bf16[2,12,16,128]{3,2,1,0:T(8,128)(2,1)S(1)}, bf16[2,12,16,128]{3,2,1,0:T(8,128)(2,1)S(1)}, u32[]{:S(2)}, u32[]{:S(2)}) %collective-permute-start.16) | collective-permute-done | bytes 98336 | tf_op jit(solution)/shard_map/ppermute | solution.py:131
  52.7 0.2 collective-permute-done.17
  52.9 0.8 %shard_map.51 = bf16[12,32,4,128]{3,2,1,0:T(4,128)(2,1)} custom-call(bf16[2,12,4,4,128]{4,3,2,1,0:T(4,128)(2,1)S(1)} %bitcast.44, bf16[2,12,4,4,128]{4,3,2,1,0:T(4,128)(2,1)S(1)} %bitcast.45, bf16[2,12,4,4,128]{4,3,2,1,0:T(4,128)(2,1)S(1)} %bitcast.46, bf16[2,12,4,4,128]{4,3,2,1,0:T(4,128)(2,1)S(1)} %bitcast.43, bf16[2,12,4,4,128]{4,3,2,1,0:T(4,128)(2,1)S(1)} %bitcast.48, ...), custom_call_target="tpu_custom_call" | custom-call | tf_op jit(solution)/shard_map/pallas_call | solution.py:186
  (15 shorter events, 0.3 us)
Async XLA Ops:
  0.0 1.0 %copy-start = (bf16[12,4,4096]{2,1,0:T(4,128)(2,1)S(1)}, bf16[12,4,4096]{2,1,0:T(4,128)(2,1)}, u32[]{:S(2)}) copy-start(bf16[12,4,4096]{2,1,0:T(4,128)(2,1)} %param.5) | copy-start | bytes 1179652
  1.0 1.0 %copy-start.1 = (bf16[12,4,4096]{2,1,0:T(4,128)(2,1)S(1)}, bf16[12,4,4096]{2,1,0:T(4,128)(2,1)}, u32[]{:S(2)}) copy-start(bf16[12,4,4096]{2,1,0:T(4,128)(2,1)} %param.6) | copy-start | bytes 1179652
  2.0 1.0 %copy-start.2 = (bf16[12,4,4096]{2,1,0:T(4,128)(2,1)S(1)}, bf16[12,4,4096]{2,1,0:T(4,128)(2,1)}, u32[]{:S(2)}) copy-start(bf16[12,4,4096]{2,1,0:T(4,128)(2,1)} %param.4) | copy-start | bytes 1179652
  2.3 2.5 %collective-permute-start = (bf16[4,2,12,16,128]{4,3,2,1,0:T(8,128)(2,1)S(1)}, bf16[4,2,12,16,128]{4,3,2,1,0:T(8,128)(2,1)S(1)}, u32[]{:S(2)}, u32[]{:S(2)}) collective-permute-start(bf16[4,2,12,16,128]{4,3,2,1,0:T(8,128)(2,1)S(1)} %bitcast.51), channel_id=1, source_target_pairs={{0,1},{1,0},{2,3},{3,2},{4,5},{5,4},{6,7},{7,6},{8,9},{9,8},{10,11... | collective-permute-start | bytes 1179656 | tf_op jit(solution)/shard_map/ppermute | solution.py:131
  3.1 1.6 %collective-permute-start.2 = (bf16[4,1,12,16,128]{4,3,2,1,0:T(8,128)(2,1)S(1)}, bf16[4,1,12,16,128]{4,3,2,1,0:T(8,128)(2,1)S(1)}, u32[]{:S(2)}, u32[]{:S(2)}) collective-permute-start(bf16[4,1,12,16,128]{4,3,2,1,0:T(8,128)(2,1)S(1)} %bitcast.52), channel_id=1, source_target_pairs={{0,1},{1,0},{2,3},{3,2},{4,5},{5,4},{6,7},{7,6},{8,9},{9,8},{10,11... | collective-permute-start | bytes 589832 | tf_op jit(solution)/shard_map/ppermute | solution.py:131
  4.8 8.2 %collective-permute-start.1 = (bf16[2,2,12,16,128]{4,3,2,0,1:T(8,128)(2,1)S(1)}, bf16[2,2,12,16,128]{4,3,2,0,1:T(8,128)(2,1)S(1)}, u32[]{:S(2)}, u32[]{:S(2)}) collective-permute-start(bf16[2,2,12,16,128]{4,3,2,0,1:T(8,128)(2,1)S(1)} %pad_maximum_fusion), channel_id=1, source_target_pairs={{0,4},{1,5},{2,6},{3,7},{4,0},{5,1},{6,2},{7,3},{8,12},{9,13},{10,... | collective-permute-start | bytes 589832 | tf_op jit(solution)/shard_map/ppermute | solution.py:131
  7.9 25.2 %collective-permute-start.10 = (bf16[2,2,12,16,128]{4,3,2,0,1:T(8,128)(2,1)S(1)}, bf16[2,2,12,16,128]{4,3,2,0,1:T(8,128)(2,1)S(1)}, u32[]{:S(2)}, u32[]{:S(2)}) collective-permute-start(bf16[2,2,12,16,128]{4,3,2,0,1:T(8,128)(2,1)S(1)} %pad_maximum_fusion.3), channel_id=1, source_target_pairs={{0,2},{1,3},{2,0},{3,1},{4,6},{5,7},{6,4},{7,5},{8,10},{9,11},{10,... | collective-permute-start | bytes 589832 | tf_op jit(solution)/shard_map/ppermute | solution.py:131
  9.4 12.5 %collective-permute-start.6 = (bf16[2,2,12,16,128]{4,3,2,0,1:T(8,128)(2,1)S(1)}, bf16[2,2,12,16,128]{4,3,2,0,1:T(8,128)(2,1)S(1)}, u32[]{:S(2)}, u32[]{:S(2)}) collective-permute-start(bf16[2,2,12,16,128]{4,3,2,0,1:T(8,128)(2,1)S(1)} %pad_maximum_fusion.1), channel_id=1, source_target_pairs={{0,12},{1,13},{2,14},{3,15},{4,8},{5,9},{6,10},{7,11},{8,4},{9,5},... | collective-permute-start | bytes 589832 | tf_op jit(solution)/shard_map/ppermute | solution.py:131
  12.0 20.5 %collective-permute-start.8 = (bf16[2,2,12,16,128]{4,3,2,1,0:T(8,128)(2,1)S(1)}, bf16[2,2,12,16,128]{4,3,2,1,0:T(8,128)(2,1)S(1)}, u32[]{:S(2)}, u32[]{:S(2)}) collective-permute-start(bf16[2,2,12,16,128]{4,3,2,1,0:T(8,128)(2,1)S(1)} %pad_maximum_fusion.2), channel_id=1, source_target_pairs={{0,8},{1,9},{2,10},{3,11},{4,12},{5,13},{6,14},{7,15},{8,0},{9,1},... | collective-permute-start | bytes 589832 | tf_op jit(solution)/shard_map/ppermute | solution.py:131
  13.1 20.0 %collective-permute-start.3 = (bf16[1,2,12,16,128]{4,3,2,1,0:T(8,128)(2,1)S(1)}, bf16[1,2,12,16,128]{4,3,2,1,0:T(8,128)(2,1)S(1)}, u32[]{:S(2)}, u32[]{:S(2)}) collective-permute-start(bf16[1,2,12,16,128]{4,3,2,1,0:T(8,128)(2,1)S(1)} %get-tuple-element.45), channel_id=1, source_target_pairs={{0,12},{1,13},{2,14},{3,15},{4,8},{5,9},{6,10},{7,11},{8,4},{9,5},... | collective-permute-start | bytes 294920 | tf_op jit(solution)/shard_map/ppermute | solution.py:131
  20.4 19.6 %collective-permute-start.11 = (bf16[2,2,12,16,128]{4,3,2,0,1:T(8,128)(2,1)S(1)}, bf16[2,2,12,16,128]{4,3,2,0,1:T(8,128)(2,1)S(1)}, u32[]{:S(2)}, u32[]{:S(2)}) collective-permute-start(bf16[2,2,12,16,128]{4,3,2,0,1:T(8,128)(2,1)S(1)} %collective-permute-done.1), channel_id=1, source_target_pairs={{0,2},{1,3},{2,0},{3,1},{4,6},{5,7},{6,4},{7,5},{8,10},{9,11},{10,... | collective-permute-start | bytes 589832 | tf_op jit(solution)/shard_map/ppermute | solution.py:131
  21.9 18.1 %collective-permute-start.7 = (bf16[2,2,12,16,128]{4,3,2,0,1:T(8,128)(2,1)S(1)}, bf16[2,2,12,16,128]{4,3,2,0,1:T(8,128)(2,1)S(1)}, u32[]{:S(2)}, u32[]{:S(2)}) collective-permute-start(bf16[2,2,12,16,128]{4,3,2,0,1:T(8,128)(2,1)S(1)} %collective-permute-done.6), channel_id=1, source_target_pairs={{0,2},{1,3},{2,0},{3,1},{4,6},{5,7},{6,4},{7,5},{8,10},{9,11},{10,... | collective-permute-start | bytes 589832 | tf_op jit(solution)/shard_map/ppermute | solution.py:131
  32.5 9.0 %collective-permute-start.9 = (bf16[2,2,12,16,128]{4,3,2,1,0:T(8,128)(2,1)S(1)}, bf16[2,2,12,16,128]{4,3,2,1,0:T(8,128)(2,1)S(1)}, u32[]{:S(2)}, u32[]{:S(2)}) collective-permute-start(bf16[2,2,12,16,128]{4,3,2,1,0:T(8,128)(2,1)S(1)} %collective-permute-done.8.refs_2_), channel_id=1, source_target_pairs={{0,2},{1,3},{2,0},{3,1},{4,6},{5,7},{6,4},{7,5},{8,10},{9,11},{10,... | collective-permute-start | bytes 589832 | tf_op jit(solution)/shard_map/ppermute | solution.py:131
  33.1 6.5 %collective-permute-start.4 = (bf16[1,2,12,16,128]{4,3,2,1,0:T(8,128)(2,1)S(1)}, bf16[1,2,12,16,128]{4,3,2,1,0:T(8,128)(2,1)S(1)}, u32[]{:S(2)}, u32[]{:S(2)}) collective-permute-start(bf16[1,2,12,16,128]{4,3,2,1,0:T(8,128)(2,1)S(1)} %get-tuple-element.44), channel_id=1, source_target_pairs={{0,8},{1,9},{2,10},{3,11},{4,12},{5,13},{6,14},{7,15},{8,0},{9,1},... | collective-permute-start | bytes 294920 | tf_op jit(solution)/shard_map/ppermute | solution.py:131
  33.1 6.8 %collective-permute-start.5 = (bf16[1,2,12,16,128]{4,3,2,1,0:T(8,128)(2,1)S(1)}, bf16[1,2,12,16,128]{4,3,2,1,0:T(8,128)(2,1)S(1)}, u32[]{:S(2)}, u32[]{:S(2)}) collective-permute-start(bf16[1,2,12,16,128]{4,3,2,1,0:T(8,128)(2,1)S(1)} %get-tuple-element.43), channel_id=1, source_target_pairs={{0,4},{1,5},{2,6},{3,7},{4,0},{5,1},{6,2},{7,3},{8,12},{9,13},{10,... | collective-permute-start | bytes 294920 | tf_op jit(solution)/shard_map/ppermute | solution.py:131
  40.1 0.7 %copy-start.3 = (s32[4]{0:T(128)S(1)}, s32[4]{0:T(128)}, u32[]{:S(2)}) copy-start(s32[4]{0:T(128)} %frames_ref.1) | copy-start | bytes 52
  42.9 6.5 %collective-permute-start.12 = (bf16[2,12,16,128]{3,2,1,0:T(8,128)(2,1)S(1)}, bf16[2,12,16,128]{3,2,1,0:T(8,128)(2,1)S(1)}, u32[]{:S(2)}, u32[]{:S(2)}) collective-permute-start(bf16[2,12,16,128]{3,2,1,0:T(8,128)(2,1)S(1)} %get-tuple-element.23), channel_id=1, source_target_pairs={{0,12},{1,13},{2,14},{3,15},{4,8},{5,9},{6,10},{7,11},{8,4},{9,5},... | collective-permute-start | bytes 294920 | tf_op jit(solution)/shard_map/ppermute | solution.py:131
  45.2 6.3 %collective-permute-start.13 = (bf16[2,12,16,128]{3,2,1,0:T(8,128)(2,1)S(1)}, bf16[2,12,16,128]{3,2,1,0:T(8,128)(2,1)S(1)}, u32[]{:S(2)}, u32[]{:S(2)}) collective-permute-start(bf16[2,12,16,128]{3,2,1,0:T(8,128)(2,1)S(1)} %get-tuple-element.24), channel_id=1, source_target_pairs={{0,8},{1,9},{2,10},{3,11},{4,12},{5,13},{6,14},{7,15},{8,0},{9,1},... | collective-permute-start | bytes 294920 | tf_op jit(solution)/shard_map/ppermute | solution.py:131
  45.4 6.1 %collective-permute-start.14 = (bf16[2,12,16,128]{3,2,1,0:T(8,128)(2,1)S(1)}, bf16[2,12,16,128]{3,2,1,0:T(8,128)(2,1)S(1)}, u32[]{:S(2)}, u32[]{:S(2)}) collective-permute-start(bf16[2,12,16,128]{3,2,1,0:T(8,128)(2,1)S(1)} %get-tuple-element.25), channel_id=1, source_target_pairs={{0,4},{1,5},{2,6},{3,7},{4,0},{5,1},{6,2},{7,3},{8,12},{9,13},{10,... | collective-permute-start | bytes 294920 | tf_op jit(solution)/shard_map/ppermute | solution.py:131
  47.3 4.7 %collective-permute-start.18 = (bf16[2,12,16,128]{3,2,1,0:T(8,128)(2,1)S(1)}, bf16[2,12,16,128]{3,2,1,0:T(8,128)(2,1)S(1)}, u32[]{:S(2)}, u32[]{:S(2)}) collective-permute-start(bf16[2,12,16,128]{3,2,1,0:T(8,128)(2,1)S(1)} %get-tuple-element.26), channel_id=1, source_target_pairs={{0,1},{1,0},{2,3},{3,2},{4,5},{5,4},{6,7},{7,6},{8,9},{9,8},{10,11... | collective-permute-start | bytes 294920 | tf_op jit(solution)/shard_map/ppermute | solution.py:131
  49.4 2.6 %collective-permute-start.15 = (bf16[2,12,16,128]{3,2,1,0:T(8,128)(2,1)S(1)}, bf16[2,12,16,128]{3,2,1,0:T(8,128)(2,1)S(1)}, u32[]{:S(2)}, u32[]{:S(2)}) collective-permute-start(bf16[2,12,16,128]{3,2,1,0:T(8,128)(2,1)S(1)} %collective-permute-done.12), channel_id=1, source_target_pairs={{0,1},{1,0},{2,3},{3,2},{4,5},{5,4},{6,7},{7,6},{8,9},{9,8},{10,11... | collective-permute-start | bytes 294920 | tf_op jit(solution)/shard_map/ppermute | solution.py:131
  51.4 1.3 %collective-permute-start.16 = (bf16[2,12,16,128]{3,2,1,0:T(8,128)(2,1)S(1)}, bf16[2,12,16,128]{3,2,1,0:T(8,128)(2,1)S(1)}, u32[]{:S(2)}, u32[]{:S(2)}) collective-permute-start(bf16[2,12,16,128]{3,2,1,0:T(8,128)(2,1)S(1)} %collective-permute-done.13), channel_id=1, source_target_pairs={{0,1},{1,0},{2,3},{3,2},{4,5},{5,4},{6,7},{7,6},{8,9},{9,8},{10,11... | collective-permute-start | bytes 294920 | tf_op jit(solution)/shard_map/ppermute | solution.py:131
  51.4 1.5 %collective-permute-start.17 = (bf16[2,12,16,128]{3,2,1,0:T(8,128)(2,1)S(1)}, bf16[2,12,16,128]{3,2,1,0:T(8,128)(2,1)S(1)}, u32[]{:S(2)}, u32[]{:S(2)}) collective-permute-start(bf16[2,12,16,128]{3,2,1,0:T(8,128)(2,1)S(1)} %collective-permute-done.14), channel_id=1, source_target_pairs={{0,1},{1,0},{2,3},{3,2},{4,5},{5,4},{6,7},{7,6},{8,9},{9,8},{10,11... | collective-permute-start | bytes 294920 | tf_op jit(solution)/shard_map/ppermute | solution.py:131

commit v3 on v2

--- a/solution.py
+++ b/solution.py
@@ -136,43 +136,51 @@
     kv_own, kv_peer = pack(outer, *srcs[:2])
     q_own, q_peer = pack(outer, srcs[2])
     kv_got, q_got = swap(kv_peer, 1), swap(q_peer, 1)
+    late = far[len(far) // 2:]
     kv, qs = {}, {}
     for a in far + near:
         pay = jnp.stack([kv_own[a], kv_got[a]], axis=1)
         kv[a] = swap(pay, a * inner) if a else pay
-    for a in far + near:
-        pay = jnp.stack([q_own[a], q_got[a]], axis=1)
-        if 1 and a:
-            pay = after(pay, kv[near[0]])
-        qs[a] = swap(pay, a * inner) if a else pay
-
     def plane(part):
-        pieces, marks = [], []
+        pieces = []
         for a in part:
-            stack, mark = [kv[a]], [a * inner]
+            stack = [kv[a]]
             step = inner // 2
             while step > 1:
-                stack = stack + [swap(x[:2], step) for x in stack]
-                mark = mark + [m ^ step for m in mark]
+                stack = stack + [swap(x, step) for x in stack]
                 step //= 2
             pieces += stack
-            marks += [m ^ c for m in mark for c in (0, 1)]
-        return pieces, marks
-
-    near_pieces, near_marks = plane(near[::-1])
-    far_pieces, far_marks = plane(far)
-    marks = near_marks + far_marks
+        return pieces
+
+    order = [0]
+    step = inner // 2
+    while step > 1:
+        order = order + [m ^ step for m in order]
+        step //= 2
+    marks = [(a * inner) ^ m ^ c for a in near[::-1] + far for m in order for c in (0, 1)]
+    near_pieces = plane(near[::-1])
     some = jax.ShapeDtypeStruct((slots, length // 2, HDIM), bf)
     k_near, v_near, bias = pl.pallas_call(
         functools.partial(near_kernel, marks, length // FRAMES),
         out_shape=[some, some, jax.ShapeDtypeStruct((clips, length), jnp.float32)],
         in_specs=[SM] + [VM] * len(near_pieces), out_specs=[VM] * 3,
-        compiler_params=LARGE, cost_estimate=cost(0.01),
+        compiler_params=LARGE, cost_estimate=cost(.01),
     )(clip_frames, *near_pieces)
+    for a in far + near:
+        pay = jnp.stack([q_own[a], q_got[a]], axis=1)
+        if a and (a in far and 3 & 1 or a in near and 3 & 2):
+            pay = after(pay, k_near)
+        if a and (a in far and 3 & 4 or a in near and 3 & 8):
+            pay = after(pay, kv[near[0]])
+        qs[a] = swap(pay, a * inner) if a else pay
+    for a in late:
+        if 1:
+            kv[a] = after(kv[a], k_near)
+    far_pieces = plane(far)
     parts = far + near
     q = pl.pallas_call(
         query_kernel, out_shape=jax.ShapeDtypeStruct((slots, outer * 2 * tokens, HDIM), bf),
-        in_specs=[VM] * outer, out_specs=VM, compiler_params=SMALL, cost_estimate=cost(0.01),
+        in_specs=[VM] * outer, out_specs=VM, compiler_params=SMALL, cost_estimate=cost(1.0),
     )(*[qs[a] for a in parts])
     piece = jax.ShapeDtypeStruct((2, tokens, slots, HDIM), bf)
     res = pl.pallas_call(

time: 53.9 us -> 51.7 us (0.959)
  waiting for transfers between devices: 20.4 us -> 16.6 us
  starting transfers between devices: 26.4 us -> 28.5 us
  local copies, waits for them, and re-layouts: 3.12 us -> 2.5 us
    ppermute x19, waiting for transfers between devices: 20.4 us -> 16.6 us  [swap(): return lax.ppermute(x, 'seq', [(i, i ^ mask) for i in range(devices)])]
    ppermute x19, starting transfers between devices: 26.4 us -> 28.5 us  [swap(): return lax.ppermute(x, 'seq', [(i, i ^ mask) for i in range(devices)])]
    unnamed x8, local copies, waits for them, and re-layouts: 2.78 us -> 2.17 us
  transfers between devices with their start and end apart: 19 -> 19, of which waited for: 9 -> 10; matrix products, arithmetic and copies ran while one was open for 1% -> 1% of each run, Pallas kernels for 2% -> 2%
where the time goes in v3:
time: 51.7 us; the launch traced here: 51.4 us
  starting transfers between devices  28.5 us (55%)
  waiting for transfers between devices  16.6 us (32%)
  Pallas kernels  3.45 us (7%)
  local copies, waits for them, and re-layouts  2.5 us (5%)
    ppermute x19, starting transfers between devices, swap(): return lax.ppermute(x, 'seq', [(i, i ^ mask) for i in range(devices)])  28.5 us
    ppermute x19, waiting for transfers between devices, swap(): return lax.ppermute(x, 'seq', [(i, i ^ mask) for i in range(devices)])  16.6 us
    unnamed x8, local copies, waits for them, and re-layouts  2.17 us
    pallas_call x1, Pallas kernels, body(): pl.pallas_call(functools.partial(main_kernel, len(far_pieces)), out_shape...  1.3 us
  transfers between devices with their start and end apart: 19, of which 10 were waited for; matrix products, arithmetic and copies ran while one was open for 1% of the time, Pallas kernels for 2%

profile of v3, /device:TPU:0, one launch (start us, length us, event | category | flops | bytes accessed | tf_op | source)
XLA Modules:
  0.0 51.4 jit_solution(9788267031673845643)
XLA Ops:
  0.0 0.0 copy-start
  0.0 1.0 %copy-done = bf16[12,4,4096]{2,1,0:T(4,128)(2,1)S(1)} copy-done((bf16[12,4,4096]{2,1,0:T(4,128)(2,1)S(1)}, bf16[12,4,4096]{2,1,0:T(4,128)(2,1)}, u32[]{:S(2)}) %copy-start) | copy-done | bytes 393240
  1.0 0.0 copy-start.1
  1.0 1.0 %copy-done.1 = bf16[12,4,4096]{2,1,0:T(4,128)(2,1)S(1)} copy-done((bf16[12,4,4096]{2,1,0:T(4,128)(2,1)S(1)}, bf16[12,4,4096]{2,1,0:T(4,128)(2,1)}, u32[]{:S(2)}) %copy-start.1) | copy-done | bytes 393240
  2.0 0.0 copy-start.2
  2.0 0.3 shard_map.46
  2.3 0.5 %collective-permute-start = (bf16[4,2,12,16,128]{4,3,2,1,0:T(8,128)(2,1)S(1)}, bf16[4,2,12,16,128]{4,3,2,1,0:T(8,128)(2,1)S(1)}, u32[]{:S(2)}, u32[]{:S(2)}) collective-permute-start(bf16[4,2,12,16,128]{4,3,2,1,0:T(8,128)(2,1)S(1)} %bitcast.51), channel_id=1, source_target_pairs={{0,1},{1,0},{2,3},{3,2},{4,5},{5,4},{6,7},{7,6},{8,9},{9,8},{10,11... | collective-permute-start | bytes 1179656 | tf_op jit(solution)/shard_map/ppermute | solution.py:131
  2.8 0.2 copy-done.2
  3.0 0.1 shard_map.48
  3.1 0.5 %collective-permute-start.4 = (bf16[4,1,12,16,128]{4,3,2,1,0:T(8,128)(2,1)S(1)}, bf16[4,1,12,16,128]{4,3,2,1,0:T(8,128)(2,1)S(1)}, u32[]{:S(2)}, u32[]{:S(2)}) collective-permute-start(bf16[4,1,12,16,128]{4,3,2,1,0:T(8,128)(2,1)S(1)} %bitcast.52), channel_id=1, source_target_pairs={{0,1},{1,0},{2,3},{3,2},{4,5},{5,4},{6,7},{7,6},{8,9},{9,8},{10,11... | collective-permute-start | bytes 589832 | tf_op jit(solution)/shard_map/ppermute | solution.py:131
  3.7 0.1 fusion.1
  3.7 0.1 fusion
  3.9 0.3 collective-permute-done
  4.2 3.0 %collective-permute-start.2 = (bf16[2,2,12,16,128]{4,3,2,0,1:T(8,128)(2,1)S(1)}, bf16[2,2,12,16,128]{4,3,2,0,1:T(8,128)(2,1)S(1)}, u32[]{:S(2)}, u32[]{:S(2)}) collective-permute-start(bf16[2,2,12,16,128]{4,3,2,0,1:T(8,128)(2,1)S(1)} %pad_maximum_fusion.1), channel_id=1, source_target_pairs={{0,4},{1,5},{2,6},{3,7},{4,0},{5,1},{6,2},{7,3},{8,12},{9,13},{10,... | collective-permute-start | bytes 589832 | tf_op jit(solution)/shard_map/ppermute | solution.py:131
  7.3 1.6 %collective-permute-start.1 = (bf16[2,2,12,16,128]{4,3,2,0,1:T(8,128)(2,1)S(1)}, bf16[2,2,12,16,128]{4,3,2,0,1:T(8,128)(2,1)S(1)}, u32[]{:S(2)}, u32[]{:S(2)}) collective-permute-start(bf16[2,2,12,16,128]{4,3,2,0,1:T(8,128)(2,1)S(1)} %pad_maximum_fusion), channel_id=1, source_target_pairs={{0,2},{1,3},{2,0},{3,1},{4,6},{5,7},{6,4},{7,5},{8,10},{9,11},{10,... | collective-permute-start | bytes 589832 | tf_op jit(solution)/shard_map/ppermute | solution.py:131
  8.8 2.5 %collective-permute-start.8 = (bf16[2,2,12,16,128]{4,3,2,0,1:T(8,128)(2,1)S(1)}, bf16[2,2,12,16,128]{4,3,2,0,1:T(8,128)(2,1)S(1)}, u32[]{:S(2)}, u32[]{:S(2)}) collective-permute-start(bf16[2,2,12,16,128]{4,3,2,0,1:T(8,128)(2,1)S(1)} %pad_maximum_fusion.2), channel_id=1, source_target_pairs={{0,12},{1,13},{2,14},{3,15},{4,8},{5,9},{6,10},{7,11},{8,4},{9,5},... | collective-permute-start | bytes 589832 | tf_op jit(solution)/shard_map/ppermute | solution.py:131
  11.4 1.1 %collective-permute-done.2 = bf16[2,2,12,16,128]{4,3,2,0,1:T(8,128)(2,1)S(1)} collective-permute-done((bf16[2,2,12,16,128]{4,3,2,0,1:T(8,128)(2,1)S(1)}, bf16[2,2,12,16,128]{4,3,2,0,1:T(8,128)(2,1)S(1)}, u32[]{:S(2)}, u32[]{:S(2)}) %collective-permute-start.2) | collective-permute-done | bytes 196640 | tf_op jit(solution)/shard_map/ppermute | solution.py:131
  12.4 1.7 %collective-permute-start.3 = (bf16[2,2,12,16,128]{4,3,2,0,1:T(8,128)(2,1)S(1)}, bf16[2,2,12,16,128]{4,3,2,0,1:T(8,128)(2,1)S(1)}, u32[]{:S(2)}, u32[]{:S(2)}) collective-permute-start(bf16[2,2,12,16,128]{4,3,2,0,1:T(8,128)(2,1)S(1)} %collective-permute-done.2), channel_id=1, source_target_pairs={{0,2},{1,3},{2,0},{3,1},{4,6},{5,7},{6,4},{7,5},{8,10},{9,11},{10,... | collective-permute-start | bytes 589832 | tf_op jit(solution)/shard_map/ppermute | solution.py:131
  14.1 0.0 collective-permute-done.4
  14.2 3.5 %collective-permute-start.10 = (bf16[2,2,12,16,128]{4,3,2,1,0:T(8,128)(2,1)S(1)}, bf16[2,2,12,16,128]{4,3,2,1,0:T(8,128)(2,1)S(1)}, u32[]{:S(2)}, u32[]{:S(2)}) collective-permute-start(bf16[2,2,12,16,128]{4,3,2,1,0:T(8,128)(2,1)S(1)} %pad_maximum_fusion.3), channel_id=1, source_target_pairs={{0,8},{1,9},{2,10},{3,11},{4,12},{5,13},{6,14},{7,15},{8,0},{9,1},... | collective-permute-start | bytes 589832 | tf_op jit(solution)/shard_map/ppermute | solution.py:131
  17.6 0.0 collective-permute-done.1
  17.7 0.0 copy-start.3
  17.7 2.1 %collective-permute-done.8 = bf16[2,2,12,16,128]{4,3,2,0,1:T(8,128)(2,1)S(1)} collective-permute-done((bf16[2,2,12,16,128]{4,3,2,0,1:T(8,128)(2,1)S(1)}, bf16[2,2,12,16,128]{4,3,2,0,1:T(8,128)(2,1)S(1)}, u32[]{:S(2)}, u32[]{:S(2)}) %collective-permute-start.8) | collective-permute-done | bytes 196640 | tf_op jit(solution)/shard_map/ppermute | solution.py:131
  19.7 1.5 %collective-permute-start.9 = (bf16[2,2,12,16,128]{4,3,2,0,1:T(8,128)(2,1)S(1)}, bf16[2,2,12,16,128]{4,3,2,0,1:T(8,128)(2,1)S(1)}, u32[]{:S(2)}, u32[]{:S(2)}) collective-permute-start(bf16[2,2,12,16,128]{4,3,2,0,1:T(8,128)(2,1)S(1)} %collective-permute-done.8), channel_id=1, source_target_pairs={{0,2},{1,3},{2,0},{3,1},{4,6},{5,7},{6,4},{7,5},{8,10},{9,11},{10,... | collective-permute-start | bytes 589832 | tf_op jit(solution)/shard_map/ppermute | solution.py:131
  21.2 0.0 collective-permute-done.3
  21.3 0.0 copy-done.3
  21.3 0.8 %shard_map.47 = (bf16[16,96,128]{2,1,0:T(8,128)(2,1)S(1)}, bf16[16,96,128]{2,1,0:T(8,128)(2,1)S(1)}, f32[4,192]{1,0:T(4,128)S(1)}) custom-call(s32[4]{0:T(128)S(1)} %copy-done.3, bf16[2,2,12,16,128]{4,3,2,1,0:T(8,128)(2,1)S(1)} %copy.5.refs_0_, bf16[2,2,12,16,128]{4,3,2,1,0:T(8,128)(2,1)S(1)} %copy.6.refs_1_, bf16[2,2,12,16,128]{4,3,2,1,0:T(8,128)(2,1)S(1)} %copy.7.refs_2_, ...), custom_call_target="tpu_custom_call" | custom-call | flops 10000000 | bytes 30000 | tf_op jit(solution)/shard_map/pallas_call | solution.py:163
  22.1 5.2 %collective-permute-start.5 = (bf16[1,2,12,16,128]{4,3,2,1,0:T(8,128)(2,1)S(1)}, bf16[1,2,12,16,128]{4,3,2,1,0:T(8,128)(2,1)S(1)}, u32[]{:S(2)}, u32[]{:S(2)}) collective-permute-start(bf16[1,2,12,16,128]{4,3,2,1,0:T(8,128)(2,1)S(1)} %get-tuple-element.45), channel_id=1, source_target_pairs={{0,12},{1,13},{2,14},{3,15},{4,8},{5,9},{6,10},{7,11},{8,4},{9,5},... | collective-permute-start | bytes 294920 | tf_op jit(solution)/shard_map/ppermute | solution.py:131
  27.3 3.1 %collective-permute-start.6 = (bf16[1,2,12,16,128]{4,3,2,1,0:T(8,128)(2,1)S(1)}, bf16[1,2,12,16,128]{4,3,2,1,0:T(8,128)(2,1)S(1)}, u32[]{:S(2)}, u32[]{:S(2)}) collective-permute-start(bf16[1,2,12,16,128]{4,3,2,1,0:T(8,128)(2,1)S(1)} %get-tuple-element.44), channel_id=1, source_target_pairs={{0,8},{1,9},{2,10},{3,11},{4,12},{5,13},{6,14},{7,15},{8,0},{9,1},... | collective-permute-start | bytes 294920 | tf_op jit(solution)/shard_map/ppermute | solution.py:131
  30.4 0.5 collective-permute-start.7
  30.9 2.2 %collective-permute-done.10 = bf16[2,2,12,16,128]{4,3,2,1,0:T(8,128)(2,1)S(1)} collective-permute-done((bf16[2,2,12,16,128]{4,3,2,1,0:T(8,128)(2,1)S(1)}, bf16[2,2,12,16,128]{4,3,2,1,0:T(8,128)(2,1)S(1)}, u32[]{:S(2)}, u32[]{:S(2)}) %collective-permute-start.10) | collective-permute-done | bytes 196640 | tf_op jit(solution)/shard_map/ppermute | solution.py:131
  33.1 0.1 collective-permute-start.11
  33.2 0.0 collective-permute-done.9
  33.2 0.0 collective-permute-done.5.refs_0_
  33.3 4.0 %collective-permute-done.6.refs_1_ = bf16[1,2,12,16,128]{4,3,2,1,0:T(8,128)(2,1)S(1)} collective-permute-done((bf16[1,2,12,16,128]{4,3,2,1,0:T(8,128)(2,1)S(1)}, bf16[1,2,12,16,128]{4,3,2,1,0:T(8,128)(2,1)S(1)}, u32[]{:S(2)}, u32[]{:S(2)}) %collective-permute-start.6) | collective-permute-done | bytes 98336 | tf_op jit(solution)/shard_map/ppermute | solution.py:131
  37.2 0.0 collective-permute-done.7.refs_2_
  37.2 0.1 shard_map.49.q
  37.3 1.5 %collective-permute-done.11.refs_3_ = bf16[2,2,12,16,128]{4,3,2,1,0:T(8,128)(2,1)S(1)} collective-permute-done((bf16[2,2,12,16,128]{4,3,2,1,0:T(8,128)(2,1)S(1)}, bf16[2,2,12,16,128]{4,3,2,1,0:T(8,128)(2,1)S(1)}, u32[]{:S(2)}, u32[]{:S(2)}) %collective-permute-start.11) | collective-permute-done | bytes 196640 | tf_op jit(solution)/shard_map/ppermute | solution.py:131
  38.8 1.3 %shard_map.50 = (bf16[2,12,16,128]{3,2,1,0:T(8,128)(2,1)S(1)}, bf16[2,12,16,128]{3,2,1,0:T(8,128)(2,1)S(1)}, bf16[2,12,16,128]{3,2,1,0:T(8,128)(2,1)S(1)}, bf16[2,12,16,128]{3,2,1,0:T(8,128)(2,1)S(1)}) custom-call(bf16[16,96,128]{2,1,0:T(8,128)(2,1)S(1)} %shard_map.49.q, bf16[2,2,12,16,128]{4,3,2,1,0:T(8,128)(2,1)S(1)} %copy.9.refs_0_, ...), custom_call_target="tpu_custom_call" | custom-call | flops 2000000000 | bytes 6000000 | tf_op jit(solution)/shard_map/pallas_call | solution.py:186
  40.1 2.8 %collective-permute-start.12 = (bf16[2,12,16,128]{3,2,1,0:T(8,128)(2,1)S(1)}, bf16[2,12,16,128]{3,2,1,0:T(8,128)(2,1)S(1)}, u32[]{:S(2)}, u32[]{:S(2)}) collective-permute-start(bf16[2,12,16,128]{3,2,1,0:T(8,128)(2,1)S(1)} %get-tuple-element.23), channel_id=1, source_target_pairs={{0,12},{1,13},{2,14},{3,15},{4,8},{5,9},{6,10},{7,11},{8,4},{9,5},... | collective-permute-start | bytes 294920 | tf_op jit(solution)/shard_map/ppermute | solution.py:131
  42.9 0.0 collective-permute-start.13
  42.9 1.7 %collective-permute-start.14 = (bf16[2,12,16,128]{3,2,1,0:T(8,128)(2,1)S(1)}, bf16[2,12,16,128]{3,2,1,0:T(8,128)(2,1)S(1)}, u32[]{:S(2)}, u32[]{:S(2)}) collective-permute-start(bf16[2,12,16,128]{3,2,1,0:T(8,128)(2,1)S(1)} %get-tuple-element.25), channel_id=1, source_target_pairs={{0,4},{1,5},{2,6},{3,7},{4,0},{5,1},{6,2},{7,3},{8,12},{9,13},{10,... | collective-permute-start | bytes 294920 | tf_op jit(solution)/shard_map/ppermute | solution.py:131
  44.6 0.0 collective-permute-start.18
  44.6 2.2 %collective-permute-done.12 = bf16[2,12,16,128]{3,2,1,0:T(8,128)(2,1)S(1)} collective-permute-done((bf16[2,12,16,128]{3,2,1,0:T(8,128)(2,1)S(1)}, bf16[2,12,16,128]{3,2,1,0:T(8,128)(2,1)S(1)}, u32[]{:S(2)}, u32[]{:S(2)}) %collective-permute-start.12) | collective-permute-done | bytes 98336 | tf_op jit(solution)/shard_map/ppermute | solution.py:131
  46.7 0.0 collective-permute-start.15
  46.7 2.4 %collective-permute-done.13 = bf16[2,12,16,128]{3,2,1,0:T(8,128)(2,1)S(1)} collective-permute-done((bf16[2,12,16,128]{3,2,1,0:T(8,128)(2,1)S(1)}, bf16[2,12,16,128]{3,2,1,0:T(8,128)(2,1)S(1)}, u32[]{:S(2)}, u32[]{:S(2)}) %collective-permute-start.13) | collective-permute-done | bytes 98336 | tf_op jit(solution)/shard_map/ppermute | solution.py:131
  49.2 0.0 collective-permute-start.16
  49.2 0.0 collective-permute-done.14
  49.2 0.5 collective-permute-start.17
  49.7 0.0 collective-permute-done.18
  49.7 0.0 collective-permute-done.15
  49.7 0.8 %collective-permute-done.16 = bf16[2,12,16,128]{3,2,1,0:T(8,128)(2,1)S(1)} collective-permute-done((bf16[2,12,16,128]{3,2,1,0:T(8,128)(2,1)S(1)}, bf16[2,12,16,128]{3,2,1,0:T(8,128)(2,1)S(1)}, u32[]{:S(2)}, u32[]{:S(2)}) %collective-permute-start.16) | collective-permute-done | bytes 98336 | tf_op jit(solution)/shard_map/ppermute | solution.py:131
  50.5 0.2 collective-permute-done.17
  50.6 0.8 %shard_map.51 = bf16[12,32,4,128]{3,2,1,0:T(4,128)(2,1)} custom-call(bf16[2,12,4,4,128]{4,3,2,1,0:T(4,128)(2,1)S(1)} %bitcast.44, bf16[2,12,4,4,128]{4,3,2,1,0:T(4,128)(2,1)S(1)} %bitcast.45, bf16[2,12,4,4,128]{4,3,2,1,0:T(4,128)(2,1)S(1)} %bitcast.46, bf16[2,12,4,4,128]{4,3,2,1,0:T(4,128)(2,1)S(1)} %bitcast.43, bf16[2,12,4,4,128]{4,3,2,1,0:T(4,128)(2,1)S(1)} %bitcast.48, ...), custom_call_target="tpu_custom_call" | custom-call | tf_op jit(solution)/shard_map/pallas_call | solution.py:194
  (16 shorter events, 0.3 us)
Async XLA Ops:
  0.0 1.0 %copy-start = (bf16[12,4,4096]{2,1,0:T(4,128)(2,1)S(1)}, bf16[12,4,4096]{2,1,0:T(4,128)(2,1)}, u32[]{:S(2)}) copy-start(bf16[12,4,4096]{2,1,0:T(4,128)(2,1)} %param.5) | copy-start | bytes 1179652
  1.0 1.0 %copy-start.1 = (bf16[12,4,4096]{2,1,0:T(4,128)(2,1)S(1)}, bf16[12,4,4096]{2,1,0:T(4,128)(2,1)}, u32[]{:S(2)}) copy-start(bf16[12,4,4096]{2,1,0:T(4,128)(2,1)} %param.6) | copy-start | bytes 1179652
  2.0 1.0 %copy-start.2 = (bf16[12,4,4096]{2,1,0:T(4,128)(2,1)S(1)}, bf16[12,4,4096]{2,1,0:T(4,128)(2,1)}, u32[]{:S(2)}) copy-start(bf16[12,4,4096]{2,1,0:T(4,128)(2,1)} %param.4) | copy-start | bytes 1179652
  2.3 1.9 %collective-permute-start = (bf16[4,2,12,16,128]{4,3,2,1,0:T(8,128)(2,1)S(1)}, bf16[4,2,12,16,128]{4,3,2,1,0:T(8,128)(2,1)S(1)}, u32[]{:S(2)}, u32[]{:S(2)}) collective-permute-start(bf16[4,2,12,16,128]{4,3,2,1,0:T(8,128)(2,1)S(1)} %bitcast.51), channel_id=1, source_target_pairs={{0,1},{1,0},{2,3},{3,2},{4,5},{5,4},{6,7},{7,6},{8,9},{9,8},{10,11... | collective-permute-start | bytes 1179656 | tf_op jit(solution)/shard_map/ppermute | solution.py:131
  3.1 11.0 %collective-permute-start.4 = (bf16[4,1,12,16,128]{4,3,2,1,0:T(8,128)(2,1)S(1)}, bf16[4,1,12,16,128]{4,3,2,1,0:T(8,128)(2,1)S(1)}, u32[]{:S(2)}, u32[]{:S(2)}) collective-permute-start(bf16[4,1,12,16,128]{4,3,2,1,0:T(8,128)(2,1)S(1)} %bitcast.52), channel_id=1, source_target_pairs={{0,1},{1,0},{2,3},{3,2},{4,5},{5,4},{6,7},{7,6},{8,9},{9,8},{10,11... | collective-permute-start | bytes 589832 | tf_op jit(solution)/shard_map/ppermute | solution.py:131
  4.2 8.2 %collective-permute-start.2 = (bf16[2,2,12,16,128]{4,3,2,0,1:T(8,128)(2,1)S(1)}, bf16[2,2,12,16,128]{4,3,2,0,1:T(8,128)(2,1)S(1)}, u32[]{:S(2)}, u32[]{:S(2)}) collective-permute-start(bf16[2,2,12,16,128]{4,3,2,0,1:T(8,128)(2,1)S(1)} %pad_maximum_fusion.1), channel_id=1, source_target_pairs={{0,4},{1,5},{2,6},{3,7},{4,0},{5,1},{6,2},{7,3},{8,12},{9,13},{10,... | collective-permute-start | bytes 589832 | tf_op jit(solution)/shard_map/ppermute | solution.py:131
  7.3 10.4 %collective-permute-start.1 = (bf16[2,2,12,16,128]{4,3,2,0,1:T(8,128)(2,1)S(1)}, bf16[2,2,12,16,128]{4,3,2,0,1:T(8,128)(2,1)S(1)}, u32[]{:S(2)}, u32[]{:S(2)}) collective-permute-start(bf16[2,2,12,16,128]{4,3,2,0,1:T(8,128)(2,1)S(1)} %pad_maximum_fusion), channel_id=1, source_target_pairs={{0,2},{1,3},{2,0},{3,1},{4,6},{5,7},{6,4},{7,5},{8,10},{9,11},{10,... | collective-permute-start | bytes 589832 | tf_op jit(solution)/shard_map/ppermute | solution.py:131
  8.8 10.9 %collective-permute-start.8 = (bf16[2,2,12,16,128]{4,3,2,0,1:T(8,128)(2,1)S(1)}, bf16[2,2,12,16,128]{4,3,2,0,1:T(8,128)(2,1)S(1)}, u32[]{:S(2)}, u32[]{:S(2)}) collective-permute-start(bf16[2,2,12,16,128]{4,3,2,0,1:T(8,128)(2,1)S(1)} %pad_maximum_fusion.2), channel_id=1, source_target_pairs={{0,12},{1,13},{2,14},{3,15},{4,8},{5,9},{6,10},{7,11},{8,4},{9,5},... | collective-permute-start | bytes 589832 | tf_op jit(solution)/shard_map/ppermute | solution.py:131
  12.4 8.8 %collective-permute-start.3 = (bf16[2,2,12,16,128]{4,3,2,0,1:T(8,128)(2,1)S(1)}, bf16[2,2,12,16,128]{4,3,2,0,1:T(8,128)(2,1)S(1)}, u32[]{:S(2)}, u32[]{:S(2)}) collective-permute-start(bf16[2,2,12,16,128]{4,3,2,0,1:T(8,128)(2,1)S(1)} %collective-permute-done.2), channel_id=1, source_target_pairs={{0,2},{1,3},{2,0},{3,1},{4,6},{5,7},{6,4},{7,5},{8,10},{9,11},{10,... | collective-permute-start | bytes 589832 | tf_op jit(solution)/shard_map/ppermute | solution.py:131
  14.2 18.9 %collective-permute-start.10 = (bf16[2,2,12,16,128]{4,3,2,1,0:T(8,128)(2,1)S(1)}, bf16[2,2,12,16,128]{4,3,2,1,0:T(8,128)(2,1)S(1)}, u32[]{:S(2)}, u32[]{:S(2)}) collective-permute-start(bf16[2,2,12,16,128]{4,3,2,1,0:T(8,128)(2,1)S(1)} %pad_maximum_fusion.3), channel_id=1, source_target_pairs={{0,8},{1,9},{2,10},{3,11},{4,12},{5,13},{6,14},{7,15},{8,0},{9,1},... | collective-permute-start | bytes 589832 | tf_op jit(solution)/shard_map/ppermute | solution.py:131
  17.7 3.6 %copy-start.3 = (s32[4]{0:T(128)S(1)}, s32[4]{0:T(128)}, u32[]{:S(2)}) copy-start(s32[4]{0:T(128)} %frames_ref.1) | copy-start | bytes 52
  19.7 13.5 %collective-permute-start.9 = (bf16[2,2,12,16,128]{4,3,2,0,1:T(8,128)(2,1)S(1)}, bf16[2,2,12,16,128]{4,3,2,0,1:T(8,128)(2,1)S(1)}, u32[]{:S(2)}, u32[]{:S(2)}) collective-permute-start(bf16[2,2,12,16,128]{4,3,2,0,1:T(8,128)(2,1)S(1)} %collective-permute-done.8), channel_id=1, source_target_pairs={{0,2},{1,3},{2,0},{3,1},{4,6},{5,7},{6,4},{7,5},{8,10},{9,11},{10,... | collective-permute-start | bytes 589832 | tf_op jit(solution)/shard_map/ppermute | solution.py:131
  22.1 11.1 %collective-permute-start.5 = (bf16[1,2,12,16,128]{4,3,2,1,0:T(8,128)(2,1)S(1)}, bf16[1,2,12,16,128]{4,3,2,1,0:T(8,128)(2,1)S(1)}, u32[]{:S(2)}, u32[]{:S(2)}) collective-permute-start(bf16[1,2,12,16,128]{4,3,2,1,0:T(8,128)(2,1)S(1)} %get-tuple-element.45), channel_id=1, source_target_pairs={{0,12},{1,13},{2,14},{3,15},{4,8},{5,9},{6,10},{7,11},{8,4},{9,5},... | collective-permute-start | bytes 294920 | tf_op jit(solution)/shard_map/ppermute | solution.py:131
  27.3 9.9 %collective-permute-start.6 = (bf16[1,2,12,16,128]{4,3,2,1,0:T(8,128)(2,1)S(1)}, bf16[1,2,12,16,128]{4,3,2,1,0:T(8,128)(2,1)S(1)}, u32[]{:S(2)}, u32[]{:S(2)}) collective-permute-start(bf16[1,2,12,16,128]{4,3,2,1,0:T(8,128)(2,1)S(1)} %get-tuple-element.44), channel_id=1, source_target_pairs={{0,8},{1,9},{2,10},{3,11},{4,12},{5,13},{6,14},{7,15},{8,0},{9,1},... | collective-permute-start | bytes 294920 | tf_op jit(solution)/shard_map/ppermute | solution.py:131
  30.4 6.8 %collective-permute-start.7 = (bf16[1,2,12,16,128]{4,3,2,1,0:T(8,128)(2,1)S(1)}, bf16[1,2,12,16,128]{4,3,2,1,0:T(8,128)(2,1)S(1)}, u32[]{:S(2)}, u32[]{:S(2)}) collective-permute-start(bf16[1,2,12,16,128]{4,3,2,1,0:T(8,128)(2,1)S(1)} %get-tuple-element.43), channel_id=1, source_target_pairs={{0,4},{1,5},{2,6},{3,7},{4,0},{5,1},{6,2},{7,3},{8,12},{9,13},{10,... | collective-permute-start | bytes 294920 | tf_op jit(solution)/shard_map/ppermute | solution.py:131
  33.1 5.7 %collective-permute-start.11 = (bf16[2,2,12,16,128]{4,3,2,1,0:T(8,128)(2,1)S(1)}, bf16[2,2,12,16,128]{4,3,2,1,0:T(8,128)(2,1)S(1)}, u32[]{:S(2)}, u32[]{:S(2)}) collective-permute-start(bf16[2,2,12,16,128]{4,3,2,1,0:T(8,128)(2,1)S(1)} %broadcast_select_fusion.refs_2_), channel_id=1, source_target_pairs={{0,2},{1,3},{2,0},{3,1},{4,6},{5,7},{6,4},{7,5},{8,10},{9,11},{10,... | collective-permute-start | bytes 589832 | tf_op jit(solution)/shard_map/ppermute | solution.py:131
  40.1 6.6 %collective-permute-start.12 = (bf16[2,12,16,128]{3,2,1,0:T(8,128)(2,1)S(1)}, bf16[2,12,16,128]{3,2,1,0:T(8,128)(2,1)S(1)}, u32[]{:S(2)}, u32[]{:S(2)}) collective-permute-start(bf16[2,12,16,128]{3,2,1,0:T(8,128)(2,1)S(1)} %get-tuple-element.23), channel_id=1, source_target_pairs={{0,12},{1,13},{2,14},{3,15},{4,8},{5,9},{6,10},{7,11},{8,4},{9,5},... | collective-permute-start | bytes 294920 | tf_op jit(solution)/shard_map/ppermute | solution.py:131
  42.9 6.3 %collective-permute-start.13 = (bf16[2,12,16,128]{3,2,1,0:T(8,128)(2,1)S(1)}, bf16[2,12,16,128]{3,2,1,0:T(8,128)(2,1)S(1)}, u32[]{:S(2)}, u32[]{:S(2)}) collective-permute-start(bf16[2,12,16,128]{3,2,1,0:T(8,128)(2,1)S(1)} %get-tuple-element.24), channel_id=1, source_target_pairs={{0,8},{1,9},{2,10},{3,11},{4,12},{5,13},{6,14},{7,15},{8,0},{9,1},... | collective-permute-start | bytes 294920 | tf_op jit(solution)/shard_map/ppermute | solution.py:131
  42.9 6.3 %collective-permute-start.14 = (bf16[2,12,16,128]{3,2,1,0:T(8,128)(2,1)S(1)}, bf16[2,12,16,128]{3,2,1,0:T(8,128)(2,1)S(1)}, u32[]{:S(2)}, u32[]{:S(2)}) collective-permute-start(bf16[2,12,16,128]{3,2,1,0:T(8,128)(2,1)S(1)} %get-tuple-element.25), channel_id=1, source_target_pairs={{0,4},{1,5},{2,6},{3,7},{4,0},{5,1},{6,2},{7,3},{8,12},{9,13},{10,... | collective-permute-start | bytes 294920 | tf_op jit(solution)/shard_map/ppermute | solution.py:131
  44.6 5.1 %collective-permute-start.18 = (bf16[2,12,16,128]{3,2,1,0:T(8,128)(2,1)S(1)}, bf16[2,12,16,128]{3,2,1,0:T(8,128)(2,1)S(1)}, u32[]{:S(2)}, u32[]{:S(2)}) collective-permute-start(bf16[2,12,16,128]{3,2,1,0:T(8,128)(2,1)S(1)} %get-tuple-element.26), channel_id=1, source_target_pairs={{0,1},{1,0},{2,3},{3,2},{4,5},{5,4},{6,7},{7,6},{8,9},{9,8},{10,11... | collective-permute-start | bytes 294920 | tf_op jit(solution)/shard_map/ppermute | solution.py:131
  46.7 3.0 %collective-permute-start.15 = (bf16[2,12,16,128]{3,2,1,0:T(8,128)(2,1)S(1)}, bf16[2,12,16,128]{3,2,1,0:T(8,128)(2,1)S(1)}, u32[]{:S(2)}, u32[]{:S(2)}) collective-permute-start(bf16[2,12,16,128]{3,2,1,0:T(8,128)(2,1)S(1)} %collective-permute-done.12), channel_id=1, source_target_pairs={{0,1},{1,0},{2,3},{3,2},{4,5},{5,4},{6,7},{7,6},{8,9},{9,8},{10,11... | collective-permute-start | bytes 294920 | tf_op jit(solution)/shard_map/ppermute | solution.py:131
  49.2 1.3 %collective-permute-start.16 = (bf16[2,12,16,128]{3,2,1,0:T(8,128)(2,1)S(1)}, bf16[2,12,16,128]{3,2,1,0:T(8,128)(2,1)S(1)}, u32[]{:S(2)}, u32[]{:S(2)}) collective-permute-start(bf16[2,12,16,128]{3,2,1,0:T(8,128)(2,1)S(1)} %collective-permute-done.13), channel_id=1, source_target_pairs={{0,1},{1,0},{2,3},{3,2},{4,5},{5,4},{6,7},{7,6},{8,9},{9,8},{10,11... | collective-permute-start | bytes 294920 | tf_op jit(solution)/shard_map/ppermute | solution.py:131
  49.2 1.5 %collective-permute-start.17 = (bf16[2,12,16,128]{3,2,1,0:T(8,128)(2,1)S(1)}, bf16[2,12,16,128]{3,2,1,0:T(8,128)(2,1)S(1)}, u32[]{:S(2)}, u32[]{:S(2)}) collective-permute-start(bf16[2,12,16,128]{3,2,1,0:T(8,128)(2,1)S(1)} %collective-permute-done.14), channel_id=1, source_target_pairs={{0,1},{1,0},{2,3},{3,2},{4,5},{5,4},{6,7},{7,6},{8,9},{9,8},{10,11... | collective-permute-start | bytes 294920 | tf_op jit(solution)/shard_map/ppermute | solution.py:131

commit v4 on v3

--- a/solution.py
+++ b/solution.py
@@ -158,6 +158,7 @@
         order = order + [m ^ step for m in order]
         step //= 2
     marks = [(a * inner) ^ m ^ c for a in near[::-1] + far for m in order for c in (0, 1)]
+    kv[0] = after(kv[0], kv[near[0]])
     near_pieces = plane(near[::-1])
     some = jax.ShapeDtypeStruct((slots, length // 2, HDIM), bf)
     k_near, v_near, bias = pl.pallas_call(
@@ -168,14 +169,11 @@
     )(clip_frames, *near_pieces)
     for a in far + near:
         pay = jnp.stack([q_own[a], q_got[a]], axis=1)
-        if a and (a in far and 3 & 1 or a in near and 3 & 2):
+        if a:
             pay = after(pay, k_near)
-        if a and (a in far and 3 & 4 or a in near and 3 & 8):
-            pay = after(pay, kv[near[0]])
         qs[a] = swap(pay, a * inner) if a else pay
     for a in late:
-        if 1:
-            kv[a] = after(kv[a], k_near)
+        kv[a] = after(kv[a], k_near)
     far_pieces = plane(far)
     parts = far + near
     q = pl.pallas_call(

time: 51.7 us -> 49.6 us (0.959)
  starting transfers between devices: 28.5 us -> 25.2 us
  waiting for transfers between devices: 16.6 us -> 17.9 us
    ppermute x19, starting transfers between devices: 28.5 us -> 25.2 us  [swap(): return lax.ppermute(x, 'seq', [(i, i ^ mask) for i in range(devices)])]
    ppermute x19, waiting for transfers between devices: 16.6 us -> 17.9 us  [swap(): return lax.ppermute(x, 'seq', [(i, i ^ mask) for i in range(devices)])]
where the time goes in v4:
time: 49.6 us; the launch traced here: 49.4 us
  starting transfers between devices  25.2 us (51%)
  waiting for transfers between devices  17.9 us (36%)
  Pallas kernels  3.45 us (7%)
  local copies, waits for them, and re-layouts  2.47 us (5%)
    ppermute x19, starting transfers between devices, swap(): return lax.ppermute(x, 'seq', [(i, i ^ mask) for i in range(devices)])  25.2 us
    ppermute x19, waiting for transfers between devices, swap(): return lax.ppermute(x, 'seq', [(i, i ^ mask) for i in range(devices)])  17.9 us
    unnamed x8, local copies, waits for them, and re-layouts  2.17 us
    pallas_call x1, Pallas kernels, body(): pl.pallas_call(functools.partial(main_kernel, len(far_pieces)), out_shape...  1.3 us
  transfers between devices with their start and end apart: 19, of which 10 were waited for; matrix products, arithmetic and copies ran while one was open for 1% of the time, Pallas kernels for 2%

profile of v4, /device:TPU:0, one launch (start us, length us, event | category | flops | bytes accessed | tf_op | source)
XLA Modules:
  0.0 49.4 jit_solution(10677226867393197700)
XLA Ops:
  0.0 0.0 copy-start
  0.0 1.0 %copy-done = bf16[12,4,4096]{2,1,0:T(4,128)(2,1)S(1)} copy-done((bf16[12,4,4096]{2,1,0:T(4,128)(2,1)S(1)}, bf16[12,4,4096]{2,1,0:T(4,128)(2,1)}, u32[]{:S(2)}) %copy-start) | copy-done | bytes 393240
  1.0 0.0 copy-start.1
  1.0 1.0 %copy-done.1 = bf16[12,4,4096]{2,1,0:T(4,128)(2,1)S(1)} copy-done((bf16[12,4,4096]{2,1,0:T(4,128)(2,1)S(1)}, bf16[12,4,4096]{2,1,0:T(4,128)(2,1)}, u32[]{:S(2)}) %copy-start.1) | copy-done | bytes 393240
  2.0 0.0 copy-start.2
  2.0 0.3 shard_map.46
  2.3 0.5 %collective-permute-start = (bf16[4,2,12,16,128]{4,3,2,1,0:T(8,128)(2,1)S(1)}, bf16[4,2,12,16,128]{4,3,2,1,0:T(8,128)(2,1)S(1)}, u32[]{:S(2)}, u32[]{:S(2)}) collective-permute-start(bf16[4,2,12,16,128]{4,3,2,1,0:T(8,128)(2,1)S(1)} %bitcast.53), channel_id=1, source_target_pairs={{0,1},{1,0},{2,3},{3,2},{4,5},{5,4},{6,7},{7,6},{8,9},{9,8},{10,11... | collective-permute-start | bytes 1179656 | tf_op jit(solution)/shard_map/ppermute | solution.py:131
  2.8 0.2 copy-done.2
  3.0 0.1 shard_map.48
  3.1 0.5 %collective-permute-start.4 = (bf16[4,1,12,16,128]{4,3,2,1,0:T(8,128)(2,1)S(1)}, bf16[4,1,12,16,128]{4,3,2,1,0:T(8,128)(2,1)S(1)}, u32[]{:S(2)}, u32[]{:S(2)}) collective-permute-start(bf16[4,1,12,16,128]{4,3,2,1,0:T(8,128)(2,1)S(1)} %bitcast.54), channel_id=1, source_target_pairs={{0,1},{1,0},{2,3},{3,2},{4,5},{5,4},{6,7},{7,6},{8,9},{9,8},{10,11... | collective-permute-start | bytes 589832 | tf_op jit(solution)/shard_map/ppermute | solution.py:131
  3.7 0.1 fusion
  3.8 0.4 collective-permute-done
  4.2 3.0 %collective-permute-start.1 = (bf16[2,2,12,16,128]{4,3,2,0,1:T(8,128)(2,1)S(1)}, bf16[2,2,12,16,128]{4,3,2,0,1:T(8,128)(2,1)S(1)}, u32[]{:S(2)}, u32[]{:S(2)}) collective-permute-start(bf16[2,2,12,16,128]{4,3,2,0,1:T(8,128)(2,1)S(1)} %pad_maximum_fusion), channel_id=1, source_target_pairs={{0,4},{1,5},{2,6},{3,7},{4,0},{5,1},{6,2},{7,3},{8,12},{9,13},{10,... | collective-permute-start | bytes 589832 | tf_op jit(solution)/shard_map/ppermute | solution.py:131
  7.2 0.1 fusion.1
  7.3 2.5 %collective-permute-start.8 = (bf16[2,2,12,16,128]{4,3,2,0,1:T(8,128)(2,1)S(1)}, bf16[2,2,12,16,128]{4,3,2,0,1:T(8,128)(2,1)S(1)}, u32[]{:S(2)}, u32[]{:S(2)}) collective-permute-start(bf16[2,2,12,16,128]{4,3,2,0,1:T(8,128)(2,1)S(1)} %pad_maximum_fusion.1), channel_id=1, source_target_pairs={{0,12},{1,13},{2,14},{3,15},{4,8},{5,9},{6,10},{7,11},{8,4},{9,5},... | collective-permute-start | bytes 589832 | tf_op jit(solution)/shard_map/ppermute | solution.py:131
  9.9 2.6 %collective-permute-done.1 = bf16[2,2,12,16,128]{4,3,2,0,1:T(8,128)(2,1)S(1)} collective-permute-done((bf16[2,2,12,16,128]{4,3,2,0,1:T(8,128)(2,1)S(1)}, bf16[2,2,12,16,128]{4,3,2,0,1:T(8,128)(2,1)S(1)}, u32[]{:S(2)}, u32[]{:S(2)}) %collective-permute-start.1) | collective-permute-done | bytes 196640 | tf_op jit(solution)/shard_map/ppermute | solution.py:131
  12.5 1.7 %collective-permute-start.2 = (bf16[2,2,12,16,128]{4,3,2,1,0:T(8,128)(2,1)S(1)}, bf16[2,2,12,16,128]{4,3,2,1,0:T(8,128)(2,1)S(1)}, u32[]{:S(2)}, u32[]{:S(2)}) collective-permute-start(bf16[2,2,12,16,128]{4,3,2,1,0:T(8,128)(2,1)S(1)} %maximum_select_fusion.refs_0_), channel_id=1, source_target_pairs={{0,2},{1,3},{2,0},{3,1},{4,6},{5,7},{6,4},{7,5},{8,10},{9,11},{10,... | collective-permute-start | bytes 589832 | tf_op jit(solution)/shard_map/ppermute | solution.py:131
  14.2 0.4 collective-permute-start.3
  14.6 0.0 collective-permute-done.4
  14.7 3.6 %collective-permute-start.10 = (bf16[2,2,12,16,128]{4,3,2,0,1:T(8,128)(2,1)S(1)}, bf16[2,2,12,16,128]{4,3,2,0,1:T(8,128)(2,1)S(1)}, u32[]{:S(2)}, u32[]{:S(2)}) collective-permute-start(bf16[2,2,12,16,128]{4,3,2,0,1:T(8,128)(2,1)S(1)} %pad_maximum_fusion.2), channel_id=1, source_target_pairs={{0,8},{1,9},{2,10},{3,11},{4,12},{5,13},{6,14},{7,15},{8,0},{9,1},... | collective-permute-start | bytes 589832 | tf_op jit(solution)/shard_map/ppermute | solution.py:131
  18.3 0.0 copy-start.3
  18.3 1.2 %collective-permute-done.8 = bf16[2,2,12,16,128]{4,3,2,0,1:T(8,128)(2,1)S(1)} collective-permute-done((bf16[2,2,12,16,128]{4,3,2,0,1:T(8,128)(2,1)S(1)}, bf16[2,2,12,16,128]{4,3,2,0,1:T(8,128)(2,1)S(1)}, u32[]{:S(2)}, u32[]{:S(2)}) %collective-permute-start.8) | collective-permute-done | bytes 196640 | tf_op jit(solution)/shard_map/ppermute | solution.py:131
  19.5 1.5 %collective-permute-start.9 = (bf16[2,2,12,16,128]{4,3,2,0,1:T(8,128)(2,1)S(1)}, bf16[2,2,12,16,128]{4,3,2,0,1:T(8,128)(2,1)S(1)}, u32[]{:S(2)}, u32[]{:S(2)}) collective-permute-start(bf16[2,2,12,16,128]{4,3,2,0,1:T(8,128)(2,1)S(1)} %collective-permute-done.8), channel_id=1, source_target_pairs={{0,2},{1,3},{2,0},{3,1},{4,6},{5,7},{6,4},{7,5},{8,10},{9,11},{10,... | collective-permute-start | bytes 589832 | tf_op jit(solution)/shard_map/ppermute | solution.py:131
  21.0 3.7 %collective-permute-done.3 = bf16[2,2,12,16,128]{4,3,2,0,1:T(8,128)(2,1)S(1)} collective-permute-done((bf16[2,2,12,16,128]{4,3,2,0,1:T(8,128)(2,1)S(1)}, bf16[2,2,12,16,128]{4,3,2,0,1:T(8,128)(2,1)S(1)}, u32[]{:S(2)}, u32[]{:S(2)}) %collective-permute-start.3) | collective-permute-done | bytes 196640 | tf_op jit(solution)/shard_map/ppermute | solution.py:131
  24.7 0.0 collective-permute-done.2.refs_1_
  24.7 0.0 copy-done.3
  24.7 0.8 %shard_map.47 = (bf16[16,96,128]{2,1,0:T(8,128)(2,1)S(1)}, bf16[16,96,128]{2,1,0:T(8,128)(2,1)S(1)}, f32[4,192]{1,0:T(4,128)S(1)}) custom-call(s32[4]{0:T(128)S(1)} %copy-done.3, bf16[2,2,12,16,128]{4,3,2,1,0:T(8,128)(2,1)S(1)} %maximum_select_fusion.refs_0_, bf16[2,2,12,16,128]{4,3,2,1,0:T(8,128)(2,1)S(1)} %collective-permute-done.2.refs_1_, ...), custom_call_target="tpu_custom_call" | custom-call | flops 10000000 | bytes 30000 | tf_op jit(solution)/shard_map/pallas_call | solution.py:164
  25.5 2.1 %collective-permute-start.7 = (bf16[1,2,12,16,128]{4,3,2,1,0:T(8,128)(2,1)S(1)}, bf16[1,2,12,16,128]{4,3,2,1,0:T(8,128)(2,1)S(1)}, u32[]{:S(2)}, u32[]{:S(2)}) collective-permute-start(bf16[1,2,12,16,128]{4,3,2,1,0:T(8,128)(2,1)S(1)} %get-tuple-element.43), channel_id=1, source_target_pairs={{0,4},{1,5},{2,6},{3,7},{4,0},{5,1},{6,2},{7,3},{8,12},{9,13},{10,... | collective-permute-start | bytes 294920 | tf_op jit(solution)/shard_map/ppermute | solution.py:131
  27.7 2.8 %collective-permute-start.6 = (bf16[1,2,12,16,128]{4,3,2,1,0:T(8,128)(2,1)S(1)}, bf16[1,2,12,16,128]{4,3,2,1,0:T(8,128)(2,1)S(1)}, u32[]{:S(2)}, u32[]{:S(2)}) collective-permute-start(bf16[1,2,12,16,128]{4,3,2,1,0:T(8,128)(2,1)S(1)} %get-tuple-element.44), channel_id=1, source_target_pairs={{0,8},{1,9},{2,10},{3,11},{4,12},{5,13},{6,14},{7,15},{8,0},{9,1},... | collective-permute-start | bytes 294920 | tf_op jit(solution)/shard_map/ppermute | solution.py:131
  30.5 0.0 collective-permute-start.5
  30.5 0.0 collective-permute-done.10
  30.5 1.6 %collective-permute-start.11 = (bf16[2,2,12,16,128]{4,3,2,1,0:T(8,128)(2,1)S(1)}, bf16[2,2,12,16,128]{4,3,2,1,0:T(8,128)(2,1)S(1)}, u32[]{:S(2)}, u32[]{:S(2)}) collective-permute-start(bf16[2,2,12,16,128]{4,3,2,1,0:T(8,128)(2,1)S(1)} %copy_select_fusion.refs_2_), channel_id=1, source_target_pairs={{0,2},{1,3},{2,0},{3,1},{4,6},{5,7},{6,4},{7,5},{8,10},{9,11},{10,... | collective-permute-start | bytes 589832 | tf_op jit(solution)/shard_map/ppermute | solution.py:131
  32.1 0.0 collective-permute-done.9
  32.1 0.0 collective-permute-done.7.refs_2_
  32.2 2.1 %collective-permute-done.6.refs_1_ = bf16[1,2,12,16,128]{4,3,2,1,0:T(8,128)(2,1)S(1)} collective-permute-done((bf16[1,2,12,16,128]{4,3,2,1,0:T(8,128)(2,1)S(1)}, bf16[1,2,12,16,128]{4,3,2,1,0:T(8,128)(2,1)S(1)}, u32[]{:S(2)}, u32[]{:S(2)}) %collective-permute-start.6) | collective-permute-done | bytes 98336 | tf_op jit(solution)/shard_map/ppermute | solution.py:131
  34.3 2.7 %collective-permute-done.5.refs_0_ = bf16[1,2,12,16,128]{4,3,2,1,0:T(8,128)(2,1)S(1)} collective-permute-done((bf16[1,2,12,16,128]{4,3,2,1,0:T(8,128)(2,1)S(1)}, bf16[1,2,12,16,128]{4,3,2,1,0:T(8,128)(2,1)S(1)}, u32[]{:S(2)}, u32[]{:S(2)}) %collective-permute-start.5) | collective-permute-done | bytes 98336 | tf_op jit(solution)/shard_map/ppermute | solution.py:131
  37.0 0.1 shard_map.49.q
  37.1 0.0 collective-permute-done.11.refs_3_
  37.1 1.3 %shard_map.50 = (bf16[2,12,16,128]{3,2,1,0:T(8,128)(2,1)S(1)}, bf16[2,12,16,128]{3,2,1,0:T(8,128)(2,1)S(1)}, bf16[2,12,16,128]{3,2,1,0:T(8,128)(2,1)S(1)}, bf16[2,12,16,128]{3,2,1,0:T(8,128)(2,1)S(1)}) custom-call(bf16[16,96,128]{2,1,0:T(8,128)(2,1)S(1)} %shard_map.49.q, bf16[2,2,12,16,128]{4,3,2,1,0:T(8,128)(2,1)S(1)} %copy.8.refs_0_, ...), custom_call_target="tpu_custom_call" | custom-call | flops 2000000000 | bytes 6000000 | tf_op jit(solution)/shard_map/pallas_call | solution.py:184
  38.4 3.0 %collective-permute-start.12 = (bf16[2,12,16,128]{3,2,1,0:T(8,128)(2,1)S(1)}, bf16[2,12,16,128]{3,2,1,0:T(8,128)(2,1)S(1)}, u32[]{:S(2)}, u32[]{:S(2)}) collective-permute-start(bf16[2,12,16,128]{3,2,1,0:T(8,128)(2,1)S(1)} %get-tuple-element.23), channel_id=1, source_target_pairs={{0,12},{1,13},{2,14},{3,15},{4,8},{5,9},{6,10},{7,11},{8,4},{9,5},... | collective-permute-start | bytes 294920 | tf_op jit(solution)/shard_map/ppermute | solution.py:131
  41.5 0.0 collective-permute-start.13
  41.5 1.4 %collective-permute-start.14 = (bf16[2,12,16,128]{3,2,1,0:T(8,128)(2,1)S(1)}, bf16[2,12,16,128]{3,2,1,0:T(8,128)(2,1)S(1)}, u32[]{:S(2)}, u32[]{:S(2)}) collective-permute-start(bf16[2,12,16,128]{3,2,1,0:T(8,128)(2,1)S(1)} %get-tuple-element.25), channel_id=1, source_target_pairs={{0,4},{1,5},{2,6},{3,7},{4,0},{5,1},{6,2},{7,3},{8,12},{9,13},{10,... | collective-permute-start | bytes 294920 | tf_op jit(solution)/shard_map/ppermute | solution.py:131
  42.9 0.0 collective-permute-start.18
  42.9 2.0 %collective-permute-done.12 = bf16[2,12,16,128]{3,2,1,0:T(8,128)(2,1)S(1)} collective-permute-done((bf16[2,12,16,128]{3,2,1,0:T(8,128)(2,1)S(1)}, bf16[2,12,16,128]{3,2,1,0:T(8,128)(2,1)S(1)}, u32[]{:S(2)}, u32[]{:S(2)}) %collective-permute-start.12) | collective-permute-done | bytes 98336 | tf_op jit(solution)/shard_map/ppermute | solution.py:131
  44.9 0.0 collective-permute-start.15
  44.9 2.2 %collective-permute-done.13 = bf16[2,12,16,128]{3,2,1,0:T(8,128)(2,1)S(1)} collective-permute-done((bf16[2,12,16,128]{3,2,1,0:T(8,128)(2,1)S(1)}, bf16[2,12,16,128]{3,2,1,0:T(8,128)(2,1)S(1)}, u32[]{:S(2)}, u32[]{:S(2)}) %collective-permute-start.13) | collective-permute-done | bytes 98336 | tf_op jit(solution)/shard_map/ppermute | solution.py:131
  47.1 0.0 collective-permute-start.16
  47.1 0.0 collective-permute-done.14
  47.1 0.5 collective-permute-start.17
  47.6 0.0 collective-permute-done.18
  47.6 0.0 collective-permute-done.15
  47.6 0.8 %collective-permute-done.16 = bf16[2,12,16,128]{3,2,1,0:T(8,128)(2,1)S(1)} collective-permute-done((bf16[2,12,16,128]{3,2,1,0:T(8,128)(2,1)S(1)}, bf16[2,12,16,128]{3,2,1,0:T(8,128)(2,1)S(1)}, u32[]{:S(2)}, u32[]{:S(2)}) %collective-permute-start.16) | collective-permute-done | bytes 98336 | tf_op jit(solution)/shard_map/ppermute | solution.py:131
  48.4 0.2 collective-permute-done.17
  48.6 0.8 %shard_map.51 = bf16[12,32,4,128]{3,2,1,0:T(4,128)(2,1)} custom-call(bf16[2,12,4,4,128]{4,3,2,1,0:T(4,128)(2,1)S(1)} %bitcast.46, bf16[2,12,4,4,128]{4,3,2,1,0:T(4,128)(2,1)S(1)} %bitcast.47, bf16[2,12,4,4,128]{4,3,2,1,0:T(4,128)(2,1)S(1)} %bitcast.48, bf16[2,12,4,4,128]{4,3,2,1,0:T(4,128)(2,1)S(1)} %bitcast.45, bf16[2,12,4,4,128]{4,3,2,1,0:T(4,128)(2,1)S(1)} %bitcast.50, ...), custom_call_target="tpu_custom_call" | custom-call | tf_op jit(solution)/shard_map/pallas_call | solution.py:192
  (15 shorter events, 0.3 us)
Async XLA Ops:
  0.0 1.0 %copy-start = (bf16[12,4,4096]{2,1,0:T(4,128)(2,1)S(1)}, bf16[12,4,4096]{2,1,0:T(4,128)(2,1)}, u32[]{:S(2)}) copy-start(bf16[12,4,4096]{2,1,0:T(4,128)(2,1)} %param.5) | copy-start | bytes 1179652
  1.0 1.0 %copy-start.1 = (bf16[12,4,4096]{2,1,0:T(4,128)(2,1)S(1)}, bf16[12,4,4096]{2,1,0:T(4,128)(2,1)}, u32[]{:S(2)}) copy-start(bf16[12,4,4096]{2,1,0:T(4,128)(2,1)} %param.6) | copy-start | bytes 1179652
  2.0 1.0 %copy-start.2 = (bf16[12,4,4096]{2,1,0:T(4,128)(2,1)S(1)}, bf16[12,4,4096]{2,1,0:T(4,128)(2,1)}, u32[]{:S(2)}) copy-start(bf16[12,4,4096]{2,1,0:T(4,128)(2,1)} %param.4) | copy-start | bytes 1179652
  2.3 1.9 %collective-permute-start = (bf16[4,2,12,16,128]{4,3,2,1,0:T(8,128)(2,1)S(1)}, bf16[4,2,12,16,128]{4,3,2,1,0:T(8,128)(2,1)S(1)}, u32[]{:S(2)}, u32[]{:S(2)}) collective-permute-start(bf16[4,2,12,16,128]{4,3,2,1,0:T(8,128)(2,1)S(1)} %bitcast.53), channel_id=1, source_target_pairs={{0,1},{1,0},{2,3},{3,2},{4,5},{5,4},{6,7},{7,6},{8,9},{9,8},{10,11... | collective-permute-start | bytes 1179656 | tf_op jit(solution)/shard_map/ppermute | solution.py:131
  3.1 11.5 %collective-permute-start.4 = (bf16[4,1,12,16,128]{4,3,2,1,0:T(8,128)(2,1)S(1)}, bf16[4,1,12,16,128]{4,3,2,1,0:T(8,128)(2,1)S(1)}, u32[]{:S(2)}, u32[]{:S(2)}) collective-permute-start(bf16[4,1,12,16,128]{4,3,2,1,0:T(8,128)(2,1)S(1)} %bitcast.54), channel_id=1, source_target_pairs={{0,1},{1,0},{2,3},{3,2},{4,5},{5,4},{6,7},{7,6},{8,9},{9,8},{10,11... | collective-permute-start | bytes 589832 | tf_op jit(solution)/shard_map/ppermute | solution.py:131
  4.2 8.3 %collective-permute-start.1 = (bf16[2,2,12,16,128]{4,3,2,0,1:T(8,128)(2,1)S(1)}, bf16[2,2,12,16,128]{4,3,2,0,1:T(8,128)(2,1)S(1)}, u32[]{:S(2)}, u32[]{:S(2)}) collective-permute-start(bf16[2,2,12,16,128]{4,3,2,0,1:T(8,128)(2,1)S(1)} %pad_maximum_fusion), channel_id=1, source_target_pairs={{0,4},{1,5},{2,6},{3,7},{4,0},{5,1},{6,2},{7,3},{8,12},{9,13},{10,... | collective-permute-start | bytes 589832 | tf_op jit(solution)/shard_map/ppermute | solution.py:131
  7.3 12.2 %collective-permute-start.8 = (bf16[2,2,12,16,128]{4,3,2,0,1:T(8,128)(2,1)S(1)}, bf16[2,2,12,16,128]{4,3,2,0,1:T(8,128)(2,1)S(1)}, u32[]{:S(2)}, u32[]{:S(2)}) collective-permute-start(bf16[2,2,12,16,128]{4,3,2,0,1:T(8,128)(2,1)S(1)} %pad_maximum_fusion.1), channel_id=1, source_target_pairs={{0,12},{1,13},{2,14},{3,15},{4,8},{5,9},{6,10},{7,11},{8,4},{9,5},... | collective-permute-start | bytes 589832 | tf_op jit(solution)/shard_map/ppermute | solution.py:131
  12.5 12.1 %collective-permute-start.2 = (bf16[2,2,12,16,128]{4,3,2,1,0:T(8,128)(2,1)S(1)}, bf16[2,2,12,16,128]{4,3,2,1,0:T(8,128)(2,1)S(1)}, u32[]{:S(2)}, u32[]{:S(2)}) collective-permute-start(bf16[2,2,12,16,128]{4,3,2,1,0:T(8,128)(2,1)S(1)} %maximum_select_fusion.refs_0_), channel_id=1, source_target_pairs={{0,2},{1,3},{2,0},{3,1},{4,6},{5,7},{6,4},{7,5},{8,10},{9,11},{10,... | collective-permute-start | bytes 589832 | tf_op jit(solution)/shard_map/ppermute | solution.py:131
  14.2 10.4 %collective-permute-start.3 = (bf16[2,2,12,16,128]{4,3,2,0,1:T(8,128)(2,1)S(1)}, bf16[2,2,12,16,128]{4,3,2,0,1:T(8,128)(2,1)S(1)}, u32[]{:S(2)}, u32[]{:S(2)}) collective-permute-start(bf16[2,2,12,16,128]{4,3,2,0,1:T(8,128)(2,1)S(1)} %collective-permute-done.1), channel_id=1, source_target_pairs={{0,2},{1,3},{2,0},{3,1},{4,6},{5,7},{6,4},{7,5},{8,10},{9,11},{10,... | collective-permute-start | bytes 589832 | tf_op jit(solution)/shard_map/ppermute | solution.py:131
  14.7 15.8 %collective-permute-start.10 = (bf16[2,2,12,16,128]{4,3,2,0,1:T(8,128)(2,1)S(1)}, bf16[2,2,12,16,128]{4,3,2,0,1:T(8,128)(2,1)S(1)}, u32[]{:S(2)}, u32[]{:S(2)}) collective-permute-start(bf16[2,2,12,16,128]{4,3,2,0,1:T(8,128)(2,1)S(1)} %pad_maximum_fusion.2), channel_id=1, source_target_pairs={{0,8},{1,9},{2,10},{3,11},{4,12},{5,13},{6,14},{7,15},{8,0},{9,1},... | collective-permute-start | bytes 589832 | tf_op jit(solution)/shard_map/ppermute | solution.py:131
  18.3 6.4 %copy-start.3 = (s32[4]{0:T(128)S(1)}, s32[4]{0:T(128)}, u32[]{:S(2)}) copy-start(s32[4]{0:T(128)} %frames_ref.1) | copy-start | bytes 52
  19.5 12.6 %collective-permute-start.9 = (bf16[2,2,12,16,128]{4,3,2,0,1:T(8,128)(2,1)S(1)}, bf16[2,2,12,16,128]{4,3,2,0,1:T(8,128)(2,1)S(1)}, u32[]{:S(2)}, u32[]{:S(2)}) collective-permute-start(bf16[2,2,12,16,128]{4,3,2,0,1:T(8,128)(2,1)S(1)} %collective-permute-done.8), channel_id=1, source_target_pairs={{0,2},{1,3},{2,0},{3,1},{4,6},{5,7},{6,4},{7,5},{8,10},{9,11},{10,... | collective-permute-start | bytes 589832 | tf_op jit(solution)/shard_map/ppermute | solution.py:131
  25.5 6.6 %collective-permute-start.7 = (bf16[1,2,12,16,128]{4,3,2,1,0:T(8,128)(2,1)S(1)}, bf16[1,2,12,16,128]{4,3,2,1,0:T(8,128)(2,1)S(1)}, u32[]{:S(2)}, u32[]{:S(2)}) collective-permute-start(bf16[1,2,12,16,128]{4,3,2,1,0:T(8,128)(2,1)S(1)} %get-tuple-element.43), channel_id=1, source_target_pairs={{0,4},{1,5},{2,6},{3,7},{4,0},{5,1},{6,2},{7,3},{8,12},{9,13},{10,... | collective-permute-start | bytes 294920 | tf_op jit(solution)/shard_map/ppermute | solution.py:131
  27.7 6.6 %collective-permute-start.6 = (bf16[1,2,12,16,128]{4,3,2,1,0:T(8,128)(2,1)S(1)}, bf16[1,2,12,16,128]{4,3,2,1,0:T(8,128)(2,1)S(1)}, u32[]{:S(2)}, u32[]{:S(2)}) collective-permute-start(bf16[1,2,12,16,128]{4,3,2,1,0:T(8,128)(2,1)S(1)} %get-tuple-element.44), channel_id=1, source_target_pairs={{0,8},{1,9},{2,10},{3,11},{4,12},{5,13},{6,14},{7,15},{8,0},{9,1},... | collective-permute-start | bytes 294920 | tf_op jit(solution)/shard_map/ppermute | solution.py:131
  30.5 6.5 %collective-permute-start.5 = (bf16[1,2,12,16,128]{4,3,2,1,0:T(8,128)(2,1)S(1)}, bf16[1,2,12,16,128]{4,3,2,1,0:T(8,128)(2,1)S(1)}, u32[]{:S(2)}, u32[]{:S(2)}) collective-permute-start(bf16[1,2,12,16,128]{4,3,2,1,0:T(8,128)(2,1)S(1)} %get-tuple-element.45), channel_id=1, source_target_pairs={{0,12},{1,13},{2,14},{3,15},{4,8},{5,9},{6,10},{7,11},{8,4},{9,5},... | collective-permute-start | bytes 294920 | tf_op jit(solution)/shard_map/ppermute | solution.py:131
  30.5 6.6 %collective-permute-start.11 = (bf16[2,2,12,16,128]{4,3,2,1,0:T(8,128)(2,1)S(1)}, bf16[2,2,12,16,128]{4,3,2,1,0:T(8,128)(2,1)S(1)}, u32[]{:S(2)}, u32[]{:S(2)}) collective-permute-start(bf16[2,2,12,16,128]{4,3,2,1,0:T(8,128)(2,1)S(1)} %copy_select_fusion.refs_2_), channel_id=1, source_target_pairs={{0,2},{1,3},{2,0},{3,1},{4,6},{5,7},{6,4},{7,5},{8,10},{9,11},{10,... | collective-permute-start | bytes 589832 | tf_op jit(solution)/shard_map/ppermute | solution.py:131
  38.4 6.5 %collective-permute-start.12 = (bf16[2,12,16,128]{3,2,1,0:T(8,128)(2,1)S(1)}, bf16[2,12,16,128]{3,2,1,0:T(8,128)(2,1)S(1)}, u32[]{:S(2)}, u32[]{:S(2)}) collective-permute-start(bf16[2,12,16,128]{3,2,1,0:T(8,128)(2,1)S(1)} %get-tuple-element.23), channel_id=1, source_target_pairs={{0,12},{1,13},{2,14},{3,15},{4,8},{5,9},{6,10},{7,11},{8,4},{9,5},... | collective-permute-start | bytes 294920 | tf_op jit(solution)/shard_map/ppermute | solution.py:131
  41.5 5.7 %collective-permute-start.13 = (bf16[2,12,16,128]{3,2,1,0:T(8,128)(2,1)S(1)}, bf16[2,12,16,128]{3,2,1,0:T(8,128)(2,1)S(1)}, u32[]{:S(2)}, u32[]{:S(2)}) collective-permute-start(bf16[2,12,16,128]{3,2,1,0:T(8,128)(2,1)S(1)} %get-tuple-element.24), channel_id=1, source_target_pairs={{0,8},{1,9},{2,10},{3,11},{4,12},{5,13},{6,14},{7,15},{8,0},{9,1},... | collective-permute-start | bytes 294920 | tf_op jit(solution)/shard_map/ppermute | solution.py:131
  41.5 5.7 %collective-permute-start.14 = (bf16[2,12,16,128]{3,2,1,0:T(8,128)(2,1)S(1)}, bf16[2,12,16,128]{3,2,1,0:T(8,128)(2,1)S(1)}, u32[]{:S(2)}, u32[]{:S(2)}) collective-permute-start(bf16[2,12,16,128]{3,2,1,0:T(8,128)(2,1)S(1)} %get-tuple-element.25), channel_id=1, source_target_pairs={{0,4},{1,5},{2,6},{3,7},{4,0},{5,1},{6,2},{7,3},{8,12},{9,13},{10,... | collective-permute-start | bytes 294920 | tf_op jit(solution)/shard_map/ppermute | solution.py:131
  42.9 4.8 %collective-permute-start.18 = (bf16[2,12,16,128]{3,2,1,0:T(8,128)(2,1)S(1)}, bf16[2,12,16,128]{3,2,1,0:T(8,128)(2,1)S(1)}, u32[]{:S(2)}, u32[]{:S(2)}) collective-permute-start(bf16[2,12,16,128]{3,2,1,0:T(8,128)(2,1)S(1)} %get-tuple-element.26), channel_id=1, source_target_pairs={{0,1},{1,0},{2,3},{3,2},{4,5},{5,4},{6,7},{7,6},{8,9},{9,8},{10,11... | collective-permute-start | bytes 294920 | tf_op jit(solution)/shard_map/ppermute | solution.py:131
  44.9 2.7 %collective-permute-start.15 = (bf16[2,12,16,128]{3,2,1,0:T(8,128)(2,1)S(1)}, bf16[2,12,16,128]{3,2,1,0:T(8,128)(2,1)S(1)}, u32[]{:S(2)}, u32[]{:S(2)}) collective-permute-start(bf16[2,12,16,128]{3,2,1,0:T(8,128)(2,1)S(1)} %collective-permute-done.12), channel_id=1, source_target_pairs={{0,1},{1,0},{2,3},{3,2},{4,5},{5,4},{6,7},{7,6},{8,9},{9,8},{10,11... | collective-permute-start | bytes 294920 | tf_op jit(solution)/shard_map/ppermute | solution.py:131
  47.1 1.3 %collective-permute-start.16 = (bf16[2,12,16,128]{3,2,1,0:T(8,128)(2,1)S(1)}, bf16[2,12,16,128]{3,2,1,0:T(8,128)(2,1)S(1)}, u32[]{:S(2)}, u32[]{:S(2)}) collective-permute-start(bf16[2,12,16,128]{3,2,1,0:T(8,128)(2,1)S(1)} %collective-permute-done.13), channel_id=1, source_target_pairs={{0,1},{1,0},{2,3},{3,2},{4,5},{5,4},{6,7},{7,6},{8,9},{9,8},{10,11... | collective-permute-start | bytes 294920 | tf_op jit(solution)/shard_map/ppermute | solution.py:131
  47.1 1.4 %collective-permute-start.17 = (bf16[2,12,16,128]{3,2,1,0:T(8,128)(2,1)S(1)}, bf16[2,12,16,128]{3,2,1,0:T(8,128)(2,1)S(1)}, u32[]{:S(2)}, u32[]{:S(2)}) collective-permute-start(bf16[2,12,16,128]{3,2,1,0:T(8,128)(2,1)S(1)} %collective-permute-done.14), channel_id=1, source_target_pairs={{0,1},{1,0},{2,3},{3,2},{4,5},{5,4},{6,7},{7,6},{8,9},{9,8},{10,11... | collective-permute-start | bytes 294920 | tf_op jit(solution)/shard_map/ppermute | solution.py:131

commit v5 on v2

v5 whole, which is shorter than its diff:
```python
import functools
import math

import jax
import jax.numpy as jnp
from jax import lax
from jax.experimental import pallas as pl
from jax.experimental.pallas import tpu as pltpu
from jax.sharding import PartitionSpec as P

HEADS = 32
HDIM = 128
FRAMES = 8
neg_large = -1e30
VM = pl.BlockSpec(memory_space=pltpu.VMEM)
ANY = pl.BlockSpec(memory_space=pl.ANY)
SM = pl.BlockSpec(memory_space=pltpu.SMEM)
LARGE = pltpu.CompilerParams(vmem_limit_bytes=24 * 1024 * 1024)
SMALL = pltpu.CompilerParams(vmem_limit_bytes=8 * 1024 * 1024)


def cost(micros):
    return pl.CostEstimate(flops=int(micros * 1e9), bytes_accessed=int(micros * 3e6), transcendentals=0)


def position(outer):
    me = lax.axis_index("seq")
    return me // (lax.axis_size("seq") // outer), me % 2


def pack_kernel(outer, count, *refs):
    srcs, dsts, sem = refs[:count], refs[count:-1], refs[-1]
    heads = dsts[0].shape[3]
    line, core = position(outer)
    copies = []
    for dst, flip in zip(dsts, (1, 0)):
        for a in range(outer):
            group = jnp.bitwise_xor(line, a) * 2 + jnp.bitwise_xor(core, flip)
            for j, src in enumerate(srcs):
                copies.append(pltpu.make_async_copy(
                    src.at[:, pl.ds(group * heads, heads)], dst.at[j, a], sem.at[len(copies)]))
    for c in copies:
        c.start()
    for c in copies:
        c.wait()


def pack(outer, *srcs):
    tokens, _, clips, _ = srcs[0].shape
    heads = HEADS // (2 * outer)
    shape = jax.ShapeDtypeStruct((len(srcs), outer, tokens, heads, clips, HDIM), jnp.bfloat16)
    out = pl.pallas_call(
        functools.partial(pack_kernel, outer, len(srcs)),
        out_shape=[shape, shape], in_specs=[ANY] * len(srcs), out_specs=[VM, VM],
        scratch_shapes=[pltpu.SemaphoreType.DMA((2 * outer * len(srcs),))], compiler_params=SMALL,
    )(*srcs)
    return [x.reshape(x.shape[:3] + (heads * clips, HDIM)) for x in out]


def turn(pieces, j):
    return jnp.swapaxes(jnp.concatenate([x[j, c] for x in pieces for c in range(2)], axis=0), 0, 1)


def near_kernel(marks, frame_tokens, frames_ref, *refs):
    kvs, (k_out, v_out, bias_out) = refs[:-3], refs[-3:]
    k_out[...] = turn(kvs, 0)
    v_out[...] = turn(kvs, 1)
    clips, length = bias_out.shape
    tokens = length // len(marks)
    me = lax.axis_index("seq")
    key = lax.broadcasted_iota(jnp.int32, (1, length), 1)
    place = jnp.zeros((1, length), jnp.int32)
    for s, mark in enumerate(marks):
        start = jnp.bitwise_xor(me, mark) * tokens - s * tokens
        place = jnp.where(key >= s * tokens, key + start, place)
    for c in range(clips):
        bias_out[c:c + 1, :] = jnp.where(place < frames_ref[c] * frame_tokens, 0.0, neg_large)


def query_kernel(*refs):
    srcs, out = refs[:-1], refs[-1]
    out[...] = turn(srcs, 0)


def attend_kernel(count, q, *refs):
    kvs, (k_near, v_near, bias), outs = refs[:count], refs[count:count + 3], refs[count + 3:]
    k = jnp.concatenate([k_near[...], turn(kvs, 0)], axis=1)
    v = jnp.concatenate([v_near[...], turn(kvs, 1)], axis=1)
    slots = k.shape[0]
    clips = bias.shape[0]
    s = lax.dot_general(q[...], k, (((2,), (2,)), ((0,), (0,))), preferred_element_type=jnp.float32)
    s = s * (1.0 / math.sqrt(HDIM)) + jnp.concatenate([bias[...]] * (slots // clips), axis=0)[:, None, :]
    e = jnp.exp(s - jnp.max(s, axis=2, keepdims=True))
    w = (e / jnp.sum(e, axis=2, keepdims=True)).astype(jnp.bfloat16)
    o = lax.dot_general(w, v, (((2,), (1,)), ((0,), (0,))), preferred_element_type=jnp.float32)
    o = jnp.swapaxes(o.astype(jnp.bfloat16), 0, 1)
    tokens = outs[0].shape[1]
    for i, out in enumerate(outs):
        for c in range(2):
            out[c] = o[(2 * i + c) * tokens:(2 * i + c + 1) * tokens]


def place_kernel(outer, order, *refs):
    kept, came, out = refs[:outer], refs[outer:-1], refs[-1]
    heads = kept[0].shape[2]
    line, core = position(outer)
    for i, a in enumerate(order):
        group = jnp.bitwise_xor(line, a) * 2
        out[:, pl.ds((group + core) * heads, heads)] = kept[i][0]
        out[:, pl.ds((group + 1 - core) * heads, heads)] = came[i][1]


def after(x, y):
    y = y[(0,) * (y.ndim - 1)]
    return jnp.where(y == y, x, jnp.zeros_like(x))


def body(queries, keys, values, clip_frames):
    tokens, clips, features = queries.shape
    devices = lax.axis_size("seq")
    outer = 1
    while outer * outer < devices:
        outer *= 2
    inner = devices // outer
    heads = HEADS // (2 * outer)
    slots = heads * clips
    length = tokens * devices
    bf = jnp.bfloat16

    def swap(x, mask):
        return lax.ppermute(x, "seq", [(i, i ^ mask) for i in range(devices)])

    far = list(range(outer - 1, outer // 2 - 1, -1))
    near = list(range(outer // 2 - 1, -1, -1))
    late = far[len(far) // 2:]
    by_head = [jnp.transpose(x.reshape(tokens, clips, HEADS, HDIM), (0, 2, 1, 3)) for x in (keys, values, queries)]
    kv_peer, kv_own = pack(outer, *by_head[:2])
    q_peer, q_own = pack(outer, by_head[2])
    kv_got, q_got = swap(kv_peer, 1), swap(q_peer, 1)

    kv = {}
    for a in near + far:
        pay = jnp.stack([kv_own[:, a], kv_got[:, a]], axis=1)
        kv[a] = swap(pay, a * inner) if a else pay

    flips = [0]
    step = inner // 2
    while step > 1:
        flips = flips + [m ^ step for m in flips]
        step //= 2

    def across(x):
        pieces = [x]
        step = inner // 2
        while step > 1:
            pieces = pieces + [swap(y, step) for y in pieces]
            step //= 2
        return pieces

    kv[0] = after(kv[0], kv[near[0]])
    crossed = {a: across(kv[a]) for a in near[::-1]}
    every = [(a, n) for a in near[::-1] + far for n in range(len(flips))]
    first = [(a, n) for a, n in every if a == 0 or a in near and n == 0]
    rest = [p for p in every if p not in first]
    marks = [(a * inner) ^ flips[n] ^ c for a, n in first + rest for c in (0, 1)]
    some = jax.ShapeDtypeStruct((slots, 2 * tokens * len(first), HDIM), bf)
    k_near, v_near, bias = pl.pallas_call(
        functools.partial(near_kernel, marks, length // FRAMES),
        out_shape=[some, some, jax.ShapeDtypeStruct((clips, length), jnp.float32)],
        in_specs=[SM] + [VM] * len(first), out_specs=[VM] * 3,
        compiler_params=LARGE, cost_estimate=cost(0.01),
    )(clip_frames, *[crossed[a][n] for a, n in first])

    for a in far:
        if a not in late:
            crossed[a] = across(kv[a])
    parts = far + near
    qs = {}
    for a in parts:
        pay = jnp.stack([q_own[:, a], q_got[:, a]], axis=1)
        qs[a] = swap(after(pay, k_near), a * inner) if a else pay
    for a in late:
        crossed[a] = across(after(kv[a], crossed[near[0]][1]))
    q = pl.pallas_call(
        query_kernel, out_shape=jax.ShapeDtypeStruct((slots, outer * 2 * tokens, HDIM), bf),
        in_specs=[VM] * outer, out_specs=VM, compiler_params=SMALL, cost_estimate=cost(1.3),
    )(*[qs[a] for a in parts])
    piece = jax.ShapeDtypeStruct((2, tokens, slots, HDIM), bf)
    res = pl.pallas_call(
        functools.partial(attend_kernel, len(rest)),
        out_shape=[piece] * outer,
        in_specs=[VM] * (len(rest) + 4), out_specs=[VM] * outer,
        compiler_params=LARGE, cost_estimate=cost(2),
    )(q, *[crossed[a][n] for a, n in rest], k_near, v_near, bias)

    outs = [swap(o, a * inner) if a else o for a, o in zip(parts, res)]
    came = [swap(o, 1) for o in outs]
    out = pl.pallas_call(
        functools.partial(place_kernel, outer, parts),
        out_shape=jax.ShapeDtypeStruct((tokens, HEADS, clips, HDIM), bf),
        in_specs=[VM] * (2 * outer), out_specs=VM, compiler_params=SMALL,
    )(*[x.reshape(2, tokens, heads, clips, HDIM) for x in outs + came])
    return jnp.transpose(out, (0, 2, 1, 3)).reshape(tokens, clips, features)


def solution(mesh):
    return jax.shard_map(
        body,
        mesh=mesh,
        in_specs=(P("seq", "grp", None), P("seq", "grp", None), P("seq", "grp", None), P("grp")),
        out_specs=P("seq", "grp", None),
        check_vma=False,
    )
```

time: 53.9 us -> 49.2 us (0.913)
  waiting for transfers between devices: 20.4 us -> 15.8 us
  starting transfers between devices: 26.4 us -> 27.3 us
  local copies, waits for them, and re-layouts: 3.12 us -> 2.25 us
    ppermute x19, waiting for transfers between devices: 20.4 us -> 15.8 us  [swap(): return lax.ppermute(x, 'seq', [(i, i ^ mask) for i in range(devices)])]
    ppermute x19, starting transfers between devices: 26.4 us -> 27.3 us  [swap(): return lax.ppermute(x, 'seq', [(i, i ^ mask) for i in range(devices)])]
    unnamed x8, local copies, waits for them, and re-layouts: 2.78 us -> 2.17 us
where the time goes in v5:
time: 49.2 us; the launch traced here: 49 us
  starting transfers between devices  27.3 us (55%)
  waiting for transfers between devices  15.8 us (32%)
  Pallas kernels  3.3 us (7%)
  local copies, waits for them, and re-layouts  2.25 us (5%)
    ppermute x19, starting transfers between devices, swap(): return lax.ppermute(x, 'seq', [(i, i ^ mask) for i in range(devices)])  27.3 us
    ppermute x19, waiting for transfers between devices, swap(): return lax.ppermute(x, 'seq', [(i, i ^ mask) for i in range(devices)])  15.8 us
    unnamed x8, local copies, waits for them, and re-layouts  2.17 us
    pallas_call x1, Pallas kernels, body(): pl.pallas_call(functools.partial(attend_kernel, len(rest)), out_shape=[pi...  1.33 us
  transfers between devices with their start and end apart: 19, of which 9 were waited for; matrix products, arithmetic and copies ran while one was open for 1% of the time, Pallas kernels for 2%

profile of v5, /device:TPU:0, one launch (start us, length us, event | category | flops | bytes accessed | tf_op | source)
XLA Modules:
  0.0 49.0 jit_solution(11645317222769878290)
XLA Ops:
  0.0 0.0 copy-start
  0.0 1.0 %copy-done = bf16[12,4,4096]{2,1,0:T(4,128)(2,1)S(1)} copy-done((bf16[12,4,4096]{2,1,0:T(4,128)(2,1)S(1)}, bf16[12,4,4096]{2,1,0:T(4,128)(2,1)}, u32[]{:S(2)}) %copy-start) | copy-done | bytes 393240
  1.0 0.0 copy-start.1
  1.0 1.0 %copy-done.1 = bf16[12,4,4096]{2,1,0:T(4,128)(2,1)S(1)} copy-done((bf16[12,4,4096]{2,1,0:T(4,128)(2,1)S(1)}, bf16[12,4,4096]{2,1,0:T(4,128)(2,1)}, u32[]{:S(2)}) %copy-start.1) | copy-done | bytes 393240
  2.0 0.0 copy-start.2
  2.0 0.3 shard_map.46
  2.3 0.5 %collective-permute-start = (bf16[2,4,12,16,128]{4,3,2,1,0:T(8,128)(2,1)S(1)}, bf16[2,4,12,16,128]{4,3,2,1,0:T(8,128)(2,1)S(1)}, u32[]{:S(2)}, u32[]{:S(2)}) collective-permute-start(bf16[2,4,12,16,128]{4,3,2,1,0:T(8,128)(2,1)S(1)} %bitcast.43), channel_id=1, source_target_pairs={{0,1},{1,0},{2,3},{3,2},{4,5},{5,4},{6,7},{7,6},{8,9},{9,8},{10,11... | collective-permute-start | bytes 1179656 | tf_op jit(solution)/shard_map/ppermute | solution.py:131
  2.8 0.2 copy-done.2
  3.0 0.1 shard_map.48
  3.1 0.5 %collective-permute-start.3 = (bf16[1,4,12,16,128]{4,3,2,1,0:T(8,128)(2,1)S(1)}, bf16[1,4,12,16,128]{4,3,2,1,0:T(8,128)(2,1)S(1)}, u32[]{:S(2)}, u32[]{:S(2)}) collective-permute-start(bf16[1,4,12,16,128]{4,3,2,1,0:T(8,128)(2,1)S(1)} %bitcast.44), channel_id=1, source_target_pairs={{0,1},{1,0},{2,3},{3,2},{4,5},{5,4},{6,7},{7,6},{8,9},{9,8},{10,11... | collective-permute-start | bytes 589832 | tf_op jit(solution)/shard_map/ppermute | solution.py:131
  3.7 0.5 collective-permute-done
  4.2 3.0 %collective-permute-start.1 = (bf16[2,2,12,16,128]{4,3,2,1,0:T(8,128)(2,1)S(1)}, bf16[2,2,12,16,128]{4,3,2,1,0:T(8,128)(2,1)S(1)}, u32[]{:S(2)}, u32[]{:S(2)}) collective-permute-start(bf16[2,2,12,16,128]{4,3,2,1,0:T(8,128)(2,1)S(1)} %pad_maximum_fusion), channel_id=1, source_target_pairs={{0,4},{1,5},{2,6},{3,7},{4,0},{5,1},{6,2},{7,3},{8,12},{9,13},{10,... | collective-permute-start | bytes 589832 | tf_op jit(solution)/shard_map/ppermute | solution.py:131
  7.3 2.5 %collective-permute-start.8 = (bf16[2,2,12,16,128]{4,3,2,1,0:T(8,128)(2,1)S(1)}, bf16[2,2,12,16,128]{4,3,2,1,0:T(8,128)(2,1)S(1)}, u32[]{:S(2)}, u32[]{:S(2)}) collective-permute-start(bf16[2,2,12,16,128]{4,3,2,1,0:T(8,128)(2,1)S(1)} %pad_maximum_fusion.1), channel_id=1, source_target_pairs={{0,12},{1,13},{2,14},{3,15},{4,8},{5,9},{6,10},{7,11},{8,4},{9,5},... | collective-permute-start | bytes 589832 | tf_op jit(solution)/shard_map/ppermute | solution.py:131
  9.8 2.7 %collective-permute-done.1.refs_2_ = bf16[2,2,12,16,128]{4,3,2,1,0:T(8,128)(2,1)S(1)} collective-permute-done((bf16[2,2,12,16,128]{4,3,2,1,0:T(8,128)(2,1)S(1)}, bf16[2,2,12,16,128]{4,3,2,1,0:T(8,128)(2,1)S(1)}, u32[]{:S(2)}, u32[]{:S(2)}) %collective-permute-start.1) | collective-permute-done | bytes 196640 | tf_op jit(solution)/shard_map/ppermute | solution.py:131
  12.5 1.7 %collective-permute-start.2 = (bf16[2,2,12,16,128]{4,3,2,1,0:T(8,128)(2,1)S(1)}, bf16[2,2,12,16,128]{4,3,2,1,0:T(8,128)(2,1)S(1)}, u32[]{:S(2)}, u32[]{:S(2)}) collective-permute-start(bf16[2,2,12,16,128]{4,3,2,1,0:T(8,128)(2,1)S(1)} %maximum_select_fusion.refs_0_), channel_id=1, source_target_pairs={{0,2},{1,3},{2,0},{3,1},{4,6},{5,7},{6,4},{7,5},{8,10},{9,11},{10,... | collective-permute-start | bytes 589832 | tf_op jit(solution)/shard_map/ppermute | solution.py:131
  14.2 0.0 collective-permute-done.3
  14.2 0.0 copy-start.3
  14.3 3.5 %collective-permute-start.10 = (bf16[2,2,12,16,128]{4,3,2,1,0:T(8,128)(2,1)S(1)}, bf16[2,2,12,16,128]{4,3,2,1,0:T(8,128)(2,1)S(1)}, u32[]{:S(2)}, u32[]{:S(2)}) collective-permute-start(bf16[2,2,12,16,128]{4,3,2,1,0:T(8,128)(2,1)S(1)} %pad_maximum_fusion.2), channel_id=1, source_target_pairs={{0,8},{1,9},{2,10},{3,11},{4,12},{5,13},{6,14},{7,15},{8,0},{9,1},... | collective-permute-start | bytes 589832 | tf_op jit(solution)/shard_map/ppermute | solution.py:131
  17.7 0.5 %collective-permute-start.7 = (bf16[2,2,12,16,128]{4,3,2,1,0:T(8,128)(2,1)S(1)}, bf16[2,2,12,16,128]{4,3,2,1,0:T(8,128)(2,1)S(1)}, u32[]{:S(2)}, u32[]{:S(2)}) collective-permute-start(bf16[2,2,12,16,128]{4,3,2,1,0:T(8,128)(2,1)S(1)} %collective-permute-done.1.refs_2_), channel_id=1, source_target_pairs={{0,2},{1,3},{2,0},{3,1},{4,6},{5,7},{6,4},{7,5},{8,10},{9,11},{10,... | collective-permute-start | bytes 589832 | tf_op jit(solution)/shard_map/ppermute | solution.py:131
  18.3 1.5 %collective-permute-done.8.refs_1_ = bf16[2,2,12,16,128]{4,3,2,1,0:T(8,128)(2,1)S(1)} collective-permute-done((bf16[2,2,12,16,128]{4,3,2,1,0:T(8,128)(2,1)S(1)}, bf16[2,2,12,16,128]{4,3,2,1,0:T(8,128)(2,1)S(1)}, u32[]{:S(2)}, u32[]{:S(2)}) %collective-permute-start.8) | collective-permute-done | bytes 196640 | tf_op jit(solution)/shard_map/ppermute | solution.py:131
  19.7 1.5 %collective-permute-start.9 = (bf16[2,2,12,16,128]{4,3,2,1,0:T(8,128)(2,1)S(1)}, bf16[2,2,12,16,128]{4,3,2,1,0:T(8,128)(2,1)S(1)}, u32[]{:S(2)}, u32[]{:S(2)}) collective-permute-start(bf16[2,2,12,16,128]{4,3,2,1,0:T(8,128)(2,1)S(1)} %collective-permute-done.8.refs_1_), channel_id=1, source_target_pairs={{0,2},{1,3},{2,0},{3,1},{4,6},{5,7},{6,4},{7,5},{8,10},{9,11},{10,... | collective-permute-start | bytes 589832 | tf_op jit(solution)/shard_map/ppermute | solution.py:131
  21.2 0.0 collective-permute-done.2.refs_1_
  21.2 0.0 copy-done.3
  21.2 0.6 %shard_map.47 = (bf16[16,72,128]{2,1,0:T(8,128)(2,1)S(1)}, bf16[16,72,128]{2,1,0:T(8,128)(2,1)S(1)}, f32[4,192]{1,0:T(4,128)S(1)}) custom-call(s32[4]{0:T(128)S(1)} %copy-done.3, bf16[2,2,12,16,128]{4,3,2,1,0:T(8,128)(2,1)S(1)} %maximum_select_fusion.refs_0_, bf16[2,2,12,16,128]{4,3,2,1,0:T(8,128)(2,1)S(1)} %collective-permute-done.2.refs_1_, ...), custom_call_target="tpu_custom_call" | custom-call | flops 10000000 | bytes 30000 | tf_op jit(solution)/shard_map/pallas_call | solution.py:167
  21.9 4.6 %collective-permute-start.6 = (bf16[1,2,12,16,128]{4,3,2,1,0:T(8,128)(2,1)S(1)}, bf16[1,2,12,16,128]{4,3,2,1,0:T(8,128)(2,1)S(1)}, u32[]{:S(2)}, u32[]{:S(2)}) collective-permute-start(bf16[1,2,12,16,128]{4,3,2,1,0:T(8,128)(2,1)S(1)} %get-tuple-element.43), channel_id=1, source_target_pairs={{0,4},{1,5},{2,6},{3,7},{4,0},{5,1},{6,2},{7,3},{8,12},{9,13},{10,... | collective-permute-start | bytes 294920 | tf_op jit(solution)/shard_map/ppermute | solution.py:131
  26.5 2.0 %collective-permute-start.5 = (bf16[1,2,12,16,128]{4,3,2,1,0:T(8,128)(2,1)S(1)}, bf16[1,2,12,16,128]{4,3,2,1,0:T(8,128)(2,1)S(1)}, u32[]{:S(2)}, u32[]{:S(2)}) collective-permute-start(bf16[1,2,12,16,128]{4,3,2,1,0:T(8,128)(2,1)S(1)} %get-tuple-element.44), channel_id=1, source_target_pairs={{0,8},{1,9},{2,10},{3,11},{4,12},{5,13},{6,14},{7,15},{8,0},{9,1},... | collective-permute-start | bytes 294920 | tf_op jit(solution)/shard_map/ppermute | solution.py:131
  28.5 0.0 collective-permute-done.7.refs_0_
  28.5 1.4 %collective-permute-start.4 = (bf16[1,2,12,16,128]{4,3,2,1,0:T(8,128)(2,1)S(1)}, bf16[1,2,12,16,128]{4,3,2,1,0:T(8,128)(2,1)S(1)}, u32[]{:S(2)}, u32[]{:S(2)}) collective-permute-start(bf16[1,2,12,16,128]{4,3,2,1,0:T(8,128)(2,1)S(1)} %get-tuple-element.45), channel_id=1, source_target_pairs={{0,12},{1,13},{2,14},{3,15},{4,8},{5,9},{6,10},{7,11},{8,4},{9,5},... | collective-permute-start | bytes 294920 | tf_op jit(solution)/shard_map/ppermute | solution.py:131
  29.9 0.0 collective-permute-done.10
  29.9 0.7 %collective-permute-start.11 = (bf16[2,2,12,16,128]{4,3,2,1,0:T(8,128)(2,1)S(1)}, bf16[2,2,12,16,128]{4,3,2,1,0:T(8,128)(2,1)S(1)}, u32[]{:S(2)}, u32[]{:S(2)}) collective-permute-start(bf16[2,2,12,16,128]{4,3,2,1,0:T(8,128)(2,1)S(1)} %broadcast_select_fusion.refs_3_), channel_id=1, source_target_pairs={{0,2},{1,3},{2,0},{3,1},{4,6},{5,7},{6,4},{7,5},{8,10},{9,11},{10,... | collective-permute-start | bytes 589832 | tf_op jit(solution)/shard_map/ppermute | solution.py:131
  30.6 0.0 collective-permute-done.6.refs_2_
  30.6 4.6 %collective-permute-done.5.refs_1_ = bf16[1,2,12,16,128]{4,3,2,1,0:T(8,128)(2,1)S(1)} collective-permute-done((bf16[1,2,12,16,128]{4,3,2,1,0:T(8,128)(2,1)S(1)}, bf16[1,2,12,16,128]{4,3,2,1,0:T(8,128)(2,1)S(1)}, u32[]{:S(2)}, u32[]{:S(2)}) %collective-permute-start.5) | collective-permute-done | bytes 98336 | tf_op jit(solution)/shard_map/ppermute | solution.py:131
  35.2 0.0 collective-permute-done.4.refs_0_
  35.2 0.1 shard_map.49.q
  35.3 0.0 collective-permute-done.9.refs_2_
  35.4 0.3 collective-permute-done.11.refs_4_
  35.6 1.3 %shard_map.50 = (bf16[2,12,16,128]{3,2,1,0:T(8,128)(2,1)S(1)}, bf16[2,12,16,128]{3,2,1,0:T(8,128)(2,1)S(1)}, bf16[2,12,16,128]{3,2,1,0:T(8,128)(2,1)S(1)}, bf16[2,12,16,128]{3,2,1,0:T(8,128)(2,1)S(1)}) custom-call(bf16[16,96,128]{2,1,0:T(8,128)(2,1)S(1)} %shard_map.49.q, bf16[2,2,12,16,128]{4,3,2,1,0:T(8,128)(2,1)S(1)} %collective-permute-done.7.refs_0_, ...), custom_call_target="tpu_custom_call" | custom-call | flops 2000000000 | bytes 6000000 | tf_op jit(solution)/shard_map/pallas_call | solution.py:189
  37.0 3.0 %collective-permute-start.12 = (bf16[2,12,16,128]{3,2,1,0:T(8,128)(2,1)S(1)}, bf16[2,12,16,128]{3,2,1,0:T(8,128)(2,1)S(1)}, u32[]{:S(2)}, u32[]{:S(2)}) collective-permute-start(bf16[2,12,16,128]{3,2,1,0:T(8,128)(2,1)S(1)} %get-tuple-element.23), channel_id=1, source_target_pairs={{0,12},{1,13},{2,14},{3,15},{4,8},{5,9},{6,10},{7,11},{8,4},{9,5},... | collective-permute-start | bytes 294920 | tf_op jit(solution)/shard_map/ppermute | solution.py:131
  40.0 0.0 collective-permute-start.13
  40.0 1.5 %collective-permute-start.14 = (bf16[2,12,16,128]{3,2,1,0:T(8,128)(2,1)S(1)}, bf16[2,12,16,128]{3,2,1,0:T(8,128)(2,1)S(1)}, u32[]{:S(2)}, u32[]{:S(2)}) collective-permute-start(bf16[2,12,16,128]{3,2,1,0:T(8,128)(2,1)S(1)} %get-tuple-element.25), channel_id=1, source_target_pairs={{0,4},{1,5},{2,6},{3,7},{4,0},{5,1},{6,2},{7,3},{8,12},{9,13},{10,... | collective-permute-start | bytes 294920 | tf_op jit(solution)/shard_map/ppermute | solution.py:131
  41.4 0.0 collective-permute-start.18
  41.4 3.0 %collective-permute-done.12 = bf16[2,12,16,128]{3,2,1,0:T(8,128)(2,1)S(1)} collective-permute-done((bf16[2,12,16,128]{3,2,1,0:T(8,128)(2,1)S(1)}, bf16[2,12,16,128]{3,2,1,0:T(8,128)(2,1)S(1)}, u32[]{:S(2)}, u32[]{:S(2)}) %collective-permute-start.12) | collective-permute-done | bytes 98336 | tf_op jit(solution)/shard_map/ppermute | solution.py:131
  44.4 0.0 collective-permute-start.15
  44.4 2.4 %collective-permute-done.13 = bf16[2,12,16,128]{3,2,1,0:T(8,128)(2,1)S(1)} collective-permute-done((bf16[2,12,16,128]{3,2,1,0:T(8,128)(2,1)S(1)}, bf16[2,12,16,128]{3,2,1,0:T(8,128)(2,1)S(1)}, u32[]{:S(2)}, u32[]{:S(2)}) %collective-permute-start.13) | collective-permute-done | bytes 98336 | tf_op jit(solution)/shard_map/ppermute | solution.py:131
  46.7 0.0 collective-permute-start.16
  46.8 0.0 collective-permute-done.14
  46.8 0.5 %collective-permute-start.17 = (bf16[2,12,16,128]{3,2,1,0:T(8,128)(2,1)S(1)}, bf16[2,12,16,128]{3,2,1,0:T(8,128)(2,1)S(1)}, u32[]{:S(2)}, u32[]{:S(2)}) collective-permute-start(bf16[2,12,16,128]{3,2,1,0:T(8,128)(2,1)S(1)} %collective-permute-done.14), channel_id=1, source_target_pairs={{0,1},{1,0},{2,3},{3,2},{4,5},{5,4},{6,7},{7,6},{8,9},{9,8},{10,11... | collective-permute-start | bytes 294920 | tf_op jit(solution)/shard_map/ppermute | solution.py:131
  47.3 0.0 collective-permute-done.18
  47.3 0.0 collective-permute-done.15
  47.3 0.8 %collective-permute-done.16 = bf16[2,12,16,128]{3,2,1,0:T(8,128)(2,1)S(1)} collective-permute-done((bf16[2,12,16,128]{3,2,1,0:T(8,128)(2,1)S(1)}, bf16[2,12,16,128]{3,2,1,0:T(8,128)(2,1)S(1)}, u32[]{:S(2)}, u32[]{:S(2)}) %collective-permute-start.16) | collective-permute-done | bytes 98336 | tf_op jit(solution)/shard_map/ppermute | solution.py:131
  48.0 0.2 collective-permute-done.17
  48.2 0.8 %shard_map.51 = bf16[12,32,4,128]{3,2,1,0:T(4,128)(2,1)} custom-call(bf16[2,12,4,4,128]{4,3,2,1,0:T(4,128)(2,1)S(1)} %bitcast.36, bf16[2,12,4,4,128]{4,3,2,1,0:T(4,128)(2,1)S(1)} %bitcast.37, bf16[2,12,4,4,128]{4,3,2,1,0:T(4,128)(2,1)S(1)} %bitcast.38, bf16[2,12,4,4,128]{4,3,2,1,0:T(4,128)(2,1)S(1)} %bitcast.35, bf16[2,12,4,4,128]{4,3,2,1,0:T(4,128)(2,1)S(1)} %bitcast.40, ...), custom_call_target="tpu_custom_call" | custom-call | tf_op jit(solution)/shard_map/pallas_call | solution.py:198
  (14 shorter events, 0.3 us)
Async XLA Ops:
  0.0 1.0 %copy-start = (bf16[12,4,4096]{2,1,0:T(4,128)(2,1)S(1)}, bf16[12,4,4096]{2,1,0:T(4,128)(2,1)}, u32[]{:S(2)}) copy-start(bf16[12,4,4096]{2,1,0:T(4,128)(2,1)} %param.5) | copy-start | bytes 1179652
  1.0 1.0 %copy-start.1 = (bf16[12,4,4096]{2,1,0:T(4,128)(2,1)S(1)}, bf16[12,4,4096]{2,1,0:T(4,128)(2,1)}, u32[]{:S(2)}) copy-start(bf16[12,4,4096]{2,1,0:T(4,128)(2,1)} %param.6) | copy-start | bytes 1179652
  2.0 1.0 %copy-start.2 = (bf16[12,4,4096]{2,1,0:T(4,128)(2,1)S(1)}, bf16[12,4,4096]{2,1,0:T(4,128)(2,1)}, u32[]{:S(2)}) copy-start(bf16[12,4,4096]{2,1,0:T(4,128)(2,1)} %param.4) | copy-start | bytes 1179652
  2.3 1.9 %collective-permute-start = (bf16[2,4,12,16,128]{4,3,2,1,0:T(8,128)(2,1)S(1)}, bf16[2,4,12,16,128]{4,3,2,1,0:T(8,128)(2,1)S(1)}, u32[]{:S(2)}, u32[]{:S(2)}) collective-permute-start(bf16[2,4,12,16,128]{4,3,2,1,0:T(8,128)(2,1)S(1)} %bitcast.43), channel_id=1, source_target_pairs={{0,1},{1,0},{2,3},{3,2},{4,5},{5,4},{6,7},{7,6},{8,9},{9,8},{10,11... | collective-permute-start | bytes 1179656 | tf_op jit(solution)/shard_map/ppermute | solution.py:131
  3.1 11.1 %collective-permute-start.3 = (bf16[1,4,12,16,128]{4,3,2,1,0:T(8,128)(2,1)S(1)}, bf16[1,4,12,16,128]{4,3,2,1,0:T(8,128)(2,1)S(1)}, u32[]{:S(2)}, u32[]{:S(2)}) collective-permute-start(bf16[1,4,12,16,128]{4,3,2,1,0:T(8,128)(2,1)S(1)} %bitcast.44), channel_id=1, source_target_pairs={{0,1},{1,0},{2,3},{3,2},{4,5},{5,4},{6,7},{7,6},{8,9},{9,8},{10,11... | collective-permute-start | bytes 589832 | tf_op jit(solution)/shard_map/ppermute | solution.py:131
  4.2 8.3 %collective-permute-start.1 = (bf16[2,2,12,16,128]{4,3,2,1,0:T(8,128)(2,1)S(1)}, bf16[2,2,12,16,128]{4,3,2,1,0:T(8,128)(2,1)S(1)}, u32[]{:S(2)}, u32[]{:S(2)}) collective-permute-start(bf16[2,2,12,16,128]{4,3,2,1,0:T(8,128)(2,1)S(1)} %pad_maximum_fusion), channel_id=1, source_target_pairs={{0,4},{1,5},{2,6},{3,7},{4,0},{5,1},{6,2},{7,3},{8,12},{9,13},{10,... | collective-permute-start | bytes 589832 | tf_op jit(solution)/shard_map/ppermute | solution.py:131
  7.3 12.5 %collective-permute-start.8 = (bf16[2,2,12,16,128]{4,3,2,1,0:T(8,128)(2,1)S(1)}, bf16[2,2,12,16,128]{4,3,2,1,0:T(8,128)(2,1)S(1)}, u32[]{:S(2)}, u32[]{:S(2)}) collective-permute-start(bf16[2,2,12,16,128]{4,3,2,1,0:T(8,128)(2,1)S(1)} %pad_maximum_fusion.1), channel_id=1, source_target_pairs={{0,12},{1,13},{2,14},{3,15},{4,8},{5,9},{6,10},{7,11},{8,4},{9,5},... | collective-permute-start | bytes 589832 | tf_op jit(solution)/shard_map/ppermute | solution.py:131
  12.5 8.7 %collective-permute-start.2 = (bf16[2,2,12,16,128]{4,3,2,1,0:T(8,128)(2,1)S(1)}, bf16[2,2,12,16,128]{4,3,2,1,0:T(8,128)(2,1)S(1)}, u32[]{:S(2)}, u32[]{:S(2)}) collective-permute-start(bf16[2,2,12,16,128]{4,3,2,1,0:T(8,128)(2,1)S(1)} %maximum_select_fusion.refs_0_), channel_id=1, source_target_pairs={{0,2},{1,3},{2,0},{3,1},{4,6},{5,7},{6,4},{7,5},{8,10},{9,11},{10,... | collective-permute-start | bytes 589832 | tf_op jit(solution)/shard_map/ppermute | solution.py:131
  14.2 7.0 %copy-start.3 = (s32[4]{0:T(128)S(1)}, s32[4]{0:T(128)}, u32[]{:S(2)}) copy-start(s32[4]{0:T(128)} %frames_ref.1) | copy-start | bytes 52
  14.3 15.6 %collective-permute-start.10 = (bf16[2,2,12,16,128]{4,3,2,1,0:T(8,128)(2,1)S(1)}, bf16[2,2,12,16,128]{4,3,2,1,0:T(8,128)(2,1)S(1)}, u32[]{:S(2)}, u32[]{:S(2)}) collective-permute-start(bf16[2,2,12,16,128]{4,3,2,1,0:T(8,128)(2,1)S(1)} %pad_maximum_fusion.2), channel_id=1, source_target_pairs={{0,8},{1,9},{2,10},{3,11},{4,12},{5,13},{6,14},{7,15},{8,0},{9,1},... | collective-permute-start | bytes 589832 | tf_op jit(solution)/shard_map/ppermute | solution.py:131
  17.7 10.8 %collective-permute-start.7 = (bf16[2,2,12,16,128]{4,3,2,1,0:T(8,128)(2,1)S(1)}, bf16[2,2,12,16,128]{4,3,2,1,0:T(8,128)(2,1)S(1)}, u32[]{:S(2)}, u32[]{:S(2)}) collective-permute-start(bf16[2,2,12,16,128]{4,3,2,1,0:T(8,128)(2,1)S(1)} %collective-permute-done.1.refs_2_), channel_id=1, source_target_pairs={{0,2},{1,3},{2,0},{3,1},{4,6},{5,7},{6,4},{7,5},{8,10},{9,11},{10,... | collective-permute-start | bytes 589832 | tf_op jit(solution)/shard_map/ppermute | solution.py:131
  19.7 15.6 %collective-permute-start.9 = (bf16[2,2,12,16,128]{4,3,2,1,0:T(8,128)(2,1)S(1)}, bf16[2,2,12,16,128]{4,3,2,1,0:T(8,128)(2,1)S(1)}, u32[]{:S(2)}, u32[]{:S(2)}) collective-permute-start(bf16[2,2,12,16,128]{4,3,2,1,0:T(8,128)(2,1)S(1)} %collective-permute-done.8.refs_1_), channel_id=1, source_target_pairs={{0,2},{1,3},{2,0},{3,1},{4,6},{5,7},{6,4},{7,5},{8,10},{9,11},{10,... | collective-permute-start | bytes 589832 | tf_op jit(solution)/shard_map/ppermute | solution.py:131
  21.9 8.7 %collective-permute-start.6 = (bf16[1,2,12,16,128]{4,3,2,1,0:T(8,128)(2,1)S(1)}, bf16[1,2,12,16,128]{4,3,2,1,0:T(8,128)(2,1)S(1)}, u32[]{:S(2)}, u32[]{:S(2)}) collective-permute-start(bf16[1,2,12,16,128]{4,3,2,1,0:T(8,128)(2,1)S(1)} %get-tuple-element.43), channel_id=1, source_target_pairs={{0,4},{1,5},{2,6},{3,7},{4,0},{5,1},{6,2},{7,3},{8,12},{9,13},{10,... | collective-permute-start | bytes 294920 | tf_op jit(solution)/shard_map/ppermute | solution.py:131
  26.5 8.7 %collective-permute-start.5 = (bf16[1,2,12,16,128]{4,3,2,1,0:T(8,128)(2,1)S(1)}, bf16[1,2,12,16,128]{4,3,2,1,0:T(8,128)(2,1)S(1)}, u32[]{:S(2)}, u32[]{:S(2)}) collective-permute-start(bf16[1,2,12,16,128]{4,3,2,1,0:T(8,128)(2,1)S(1)} %get-tuple-element.44), channel_id=1, source_target_pairs={{0,8},{1,9},{2,10},{3,11},{4,12},{5,13},{6,14},{7,15},{8,0},{9,1},... | collective-permute-start | bytes 294920 | tf_op jit(solution)/shard_map/ppermute | solution.py:131
  28.5 6.7 %collective-permute-start.4 = (bf16[1,2,12,16,128]{4,3,2,1,0:T(8,128)(2,1)S(1)}, bf16[1,2,12,16,128]{4,3,2,1,0:T(8,128)(2,1)S(1)}, u32[]{:S(2)}, u32[]{:S(2)}) collective-permute-start(bf16[1,2,12,16,128]{4,3,2,1,0:T(8,128)(2,1)S(1)} %get-tuple-element.45), channel_id=1, source_target_pairs={{0,12},{1,13},{2,14},{3,15},{4,8},{5,9},{6,10},{7,11},{8,4},{9,5},... | collective-permute-start | bytes 294920 | tf_op jit(solution)/shard_map/ppermute | solution.py:131
  29.9 5.7 %collective-permute-start.11 = (bf16[2,2,12,16,128]{4,3,2,1,0:T(8,128)(2,1)S(1)}, bf16[2,2,12,16,128]{4,3,2,1,0:T(8,128)(2,1)S(1)}, u32[]{:S(2)}, u32[]{:S(2)}) collective-permute-start(bf16[2,2,12,16,128]{4,3,2,1,0:T(8,128)(2,1)S(1)} %broadcast_select_fusion.refs_3_), channel_id=1, source_target_pairs={{0,2},{1,3},{2,0},{3,1},{4,6},{5,7},{6,4},{7,5},{8,10},{9,11},{10,... | collective-permute-start | bytes 589832 | tf_op jit(solution)/shard_map/ppermute | solution.py:131
  37.0 7.4 %collective-permute-start.12 = (bf16[2,12,16,128]{3,2,1,0:T(8,128)(2,1)S(1)}, bf16[2,12,16,128]{3,2,1,0:T(8,128)(2,1)S(1)}, u32[]{:S(2)}, u32[]{:S(2)}) collective-permute-start(bf16[2,12,16,128]{3,2,1,0:T(8,128)(2,1)S(1)} %get-tuple-element.23), channel_id=1, source_target_pairs={{0,12},{1,13},{2,14},{3,15},{4,8},{5,9},{6,10},{7,11},{8,4},{9,5},... | collective-permute-start | bytes 294920 | tf_op jit(solution)/shard_map/ppermute | solution.py:131
  40.0 6.8 %collective-permute-start.13 = (bf16[2,12,16,128]{3,2,1,0:T(8,128)(2,1)S(1)}, bf16[2,12,16,128]{3,2,1,0:T(8,128)(2,1)S(1)}, u32[]{:S(2)}, u32[]{:S(2)}) collective-permute-start(bf16[2,12,16,128]{3,2,1,0:T(8,128)(2,1)S(1)} %get-tuple-element.24), channel_id=1, source_target_pairs={{0,8},{1,9},{2,10},{3,11},{4,12},{5,13},{6,14},{7,15},{8,0},{9,1},... | collective-permute-start | bytes 294920 | tf_op jit(solution)/shard_map/ppermute | solution.py:131
  40.0 6.8 %collective-permute-start.14 = (bf16[2,12,16,128]{3,2,1,0:T(8,128)(2,1)S(1)}, bf16[2,12,16,128]{3,2,1,0:T(8,128)(2,1)S(1)}, u32[]{:S(2)}, u32[]{:S(2)}) collective-permute-start(bf16[2,12,16,128]{3,2,1,0:T(8,128)(2,1)S(1)} %get-tuple-element.25), channel_id=1, source_target_pairs={{0,4},{1,5},{2,6},{3,7},{4,0},{5,1},{6,2},{7,3},{8,12},{9,13},{10,... | collective-permute-start | bytes 294920 | tf_op jit(solution)/shard_map/ppermute | solution.py:131
  41.4 5.8 %collective-permute-start.18 = (bf16[2,12,16,128]{3,2,1,0:T(8,128)(2,1)S(1)}, bf16[2,12,16,128]{3,2,1,0:T(8,128)(2,1)S(1)}, u32[]{:S(2)}, u32[]{:S(2)}) collective-permute-start(bf16[2,12,16,128]{3,2,1,0:T(8,128)(2,1)S(1)} %get-tuple-element.26), channel_id=1, source_target_pairs={{0,1},{1,0},{2,3},{3,2},{4,5},{5,4},{6,7},{7,6},{8,9},{9,8},{10,11... | collective-permute-start | bytes 294920 | tf_op jit(solution)/shard_map/ppermute | solution.py:131
  44.4 2.9 %collective-permute-start.15 = (bf16[2,12,16,128]{3,2,1,0:T(8,128)(2,1)S(1)}, bf16[2,12,16,128]{3,2,1,0:T(8,128)(2,1)S(1)}, u32[]{:S(2)}, u32[]{:S(2)}) collective-permute-start(bf16[2,12,16,128]{3,2,1,0:T(8,128)(2,1)S(1)} %collective-permute-done.12), channel_id=1, source_target_pairs={{0,1},{1,0},{2,3},{3,2},{4,5},{5,4},{6,7},{7,6},{8,9},{9,8},{10,11... | collective-permute-start | bytes 294920 | tf_op jit(solution)/shard_map/ppermute | solution.py:131
  46.7 1.3 %collective-permute-start.16 = (bf16[2,12,16,128]{3,2,1,0:T(8,128)(2,1)S(1)}, bf16[2,12,16,128]{3,2,1,0:T(8,128)(2,1)S(1)}, u32[]{:S(2)}, u32[]{:S(2)}) collective-permute-start(bf16[2,12,16,128]{3,2,1,0:T(8,128)(2,1)S(1)} %collective-permute-done.13), channel_id=1, source_target_pairs={{0,1},{1,0},{2,3},{3,2},{4,5},{5,4},{6,7},{7,6},{8,9},{9,8},{10,11... | collective-permute-start | bytes 294920 | tf_op jit(solution)/shard_map/ppermute | solution.py:131
  46.8 1.5 %collective-permute-start.17 = (bf16[2,12,16,128]{3,2,1,0:T(8,128)(2,1)S(1)}, bf16[2,12,16,128]{3,2,1,0:T(8,128)(2,1)S(1)}, u32[]{:S(2)}, u32[]{:S(2)}) collective-permute-start(bf16[2,12,16,128]{3,2,1,0:T(8,128)(2,1)S(1)} %collective-permute-done.14), channel_id=1, source_target_pairs={{0,1},{1,0},{2,3},{3,2},{4,5},{5,4},{6,7},{7,6},{8,9},{9,8},{10,11... | collective-permute-start | bytes 294920 | tf_op jit(solution)/shard_map/ppermute | solution.py:131

commit v6 on v5

--- a/solution.py
+++ b/solution.py
@@ -28,33 +28,32 @@
     return me // (lax.axis_size("seq") // outer), me % 2
 
 
-def pack_kernel(outer, count, *refs):
-    srcs, dsts, sem = refs[:count], refs[count:-1], refs[-1]
-    heads = dsts[0].shape[3]
+def pack_kernel(outer, count, partners, flip, *refs):
+    srcs, dst, sem = refs[:count], refs[count], refs[count + 1]
+    heads = dst.shape[3]
     line, core = position(outer)
     copies = []
-    for dst, flip in zip(dsts, (1, 0)):
-        for a in range(outer):
-            group = jnp.bitwise_xor(line, a) * 2 + jnp.bitwise_xor(core, flip)
-            for j, src in enumerate(srcs):
-                copies.append(pltpu.make_async_copy(
-                    src.at[:, pl.ds(group * heads, heads)], dst.at[j, a], sem.at[len(copies)]))
+    for i, a in enumerate(partners):
+        group = jnp.bitwise_xor(line, a) * 2 + jnp.bitwise_xor(core, flip)
+        for j, src in enumerate(srcs):
+            copies.append(pltpu.make_async_copy(
+                src.at[:, pl.ds(group * heads, heads)], dst.at[j, i], sem.at[len(copies)]))
     for c in copies:
         c.start()
     for c in copies:
         c.wait()
 
 
-def pack(outer, *srcs):
+def pack(outer, partners, flip, params, *srcs):
     tokens, _, clips, _ = srcs[0].shape
     heads = HEADS // (2 * outer)
-    shape = jax.ShapeDtypeStruct((len(srcs), outer, tokens, heads, clips, HDIM), jnp.bfloat16)
     out = pl.pallas_call(
-        functools.partial(pack_kernel, outer, len(srcs)),
-        out_shape=[shape, shape], in_specs=[ANY] * len(srcs), out_specs=[VM, VM],
-        scratch_shapes=[pltpu.SemaphoreType.DMA((2 * outer * len(srcs),))], compiler_params=SMALL,
+        functools.partial(pack_kernel, outer, len(srcs), partners, flip),
+        out_shape=jax.ShapeDtypeStruct((len(srcs), len(partners), tokens, heads, clips, HDIM), jnp.bfloat16),
+        in_specs=[ANY] * len(srcs), out_specs=VM,
+        scratch_shapes=[pltpu.SemaphoreType.DMA((len(partners) * len(srcs),))], compiler_params=params,
     )(*srcs)
-    return [x.reshape(x.shape[:3] + (heads * clips, HDIM)) for x in out]
+    return out.reshape(out.shape[:3] + (heads * clips, HDIM))
 
 
 def turn(pieces, j):
@@ -134,13 +133,19 @@
     near = list(range(outer // 2 - 1, -1, -1))
     late = far[len(far) // 2:]
     by_head = [jnp.transpose(x.reshape(tokens, clips, HEADS, HDIM), (0, 2, 1, 3)) for x in (keys, values, queries)]
-    kv_peer, kv_own = pack(outer, *by_head[:2])
-    q_peer, q_own = pack(outer, by_head[2])
-    kv_got, q_got = swap(kv_peer, 1), swap(q_peer, 1)
+    line = list(range(outer))
+    soon = near[:-1] + far
+    kv_got = {}
+    for part, params in ((soon, None), ([a for a in line if a not in soon], SMALL)):
+        both = swap(pack(outer, part, 1, params, *by_head[:2]), 1)
+        kv_got.update({a: both[:, i] for i, a in enumerate(part)})
+    kv_own = pack(outer, line, 0, SMALL, *by_head[:2])
+    q_got = swap(pack(outer, line, 1, SMALL, by_head[2]), 1)
+    q_own = pack(outer, line, 0, SMALL, by_head[2])
 
     kv = {}
-    for a in near + far:
-        pay = jnp.stack([kv_own[:, a], kv_got[:, a]], axis=1)
+    for a in far + near:
+        pay = jnp.stack([kv_own[:, a], kv_got[a]], axis=1)
         kv[a] = swap(pay, a * inner) if a else pay
 
     flips = [0]

time: 49.2 us -> 48.7 us (0.990)
  local copies, waits for them, and re-layouts: 2.25 us -> 0.39 us
  Pallas kernels: 3.3 us -> 4.97 us
    unnamed x8, local copies, waits for them, and re-layouts: 2.17 us -> 0.31 us
    pallas_call x2 -> x5, Pallas kernels: 0.44 us -> 2.11 us  [pack(): pl.pallas_call(functools.partial(pack_kernel, outer, len(srcs), partners,...]
    ppermute x19 -> x20, waiting for transfers between devices: 15.8 us -> 15.4 us  [swap(): return lax.ppermute(x, 'seq', [(i, i ^ mask) for i in range(devices)])]
    ppermute x19 -> x20, starting transfers between devices: 27.3 us -> 27.4 us  [swap(): return lax.ppermute(x, 'seq', [(i, i ^ mask) for i in range(devices)])]
  transfers between devices with their start and end apart: 19 -> 20, of which waited for: 9 -> 9; matrix products, arithmetic and copies ran while one was open for 1% -> 1% of each run, Pallas kernels for 2% -> 2%
where the time goes in v6:
time: 48.7 us; the launch traced here: 48.5 us
  starting transfers between devices  27.4 us (56%)
  waiting for transfers between devices  15.4 us (32%)
  Pallas kernels  4.97 us (10%)
    ppermute x20, starting transfers between devices, swap(): return lax.ppermute(x, 'seq', [(i, i ^ mask) for i in range(devices)])  27.4 us
    ppermute x20, waiting for transfers between devices, swap(): return lax.ppermute(x, 'seq', [(i, i ^ mask) for i in range(devices)])  15.4 us
    pallas_call x5, Pallas kernels, pack(): pl.pallas_call(functools.partial(pack_kernel, outer, len(srcs), partners,...  2.11 us
    pallas_call x1, Pallas kernels, body(): pl.pallas_call(functools.partial(attend_kernel, len(rest)), out_shape=[pi...  1.33 us
  transfers between devices with their start and end apart: 20, of which 9 were waited for; matrix products, arithmetic and copies ran while one was open for 1% of the time, Pallas kernels for 2%

profile of v6, /device:TPU:0, one launch (start us, length us, event | category | flops | bytes accessed | tf_op | source)
XLA Modules:
  0.0 48.5 jit_solution(7492583058639483435)
XLA Ops:
  0.0 0.0 copy-start
  0.0 0.0 copy-start.1
  0.0 1.8 %shard_map.47 = bf16[2,3,12,4,4,128]{5,4,3,2,1,0:T(4,128)(2,1)} custom-call(bf16[12,32,4,128]{3,2,1,0:T(4,128)(2,1)} %bitcast.31, bf16[12,32,4,128]{3,2,1,0:T(4,128)(2,1)} %bitcast.34), custom_call_target="tpu_custom_call" | custom-call | tf_op jit(solution)/shard_map/pallas_call | solution.py:50
  1.8 0.0 copy-start.2
  1.8 0.5 %collective-permute-start = (bf16[2,3,12,16,128]{4,3,2,1,0:T(8,128)(2,1)}, bf16[2,3,12,16,128]{4,3,2,1,0:T(8,128)(2,1)S(1)}, u32[]{:S(2)}, u32[]{:S(2)}) collective-permute-start(bf16[2,3,12,16,128]{4,3,2,1,0:T(8,128)(2,1)} %bitcast.51), channel_id=1, source_target_pairs={{0,1},{1,0},{2,3},{3,2},{4,5},{5,4},{6,7},{7,6},{8,9},{9,8},{10,11... | collective-permute-start | bytes 884744 | tf_op jit(solution)/shard_map/ppermute | solution.py:130
  2.3 0.0 copy-done
  2.3 0.0 copy-done.1
  2.4 0.1 collective-permute-start.2
  2.5 0.3 copy-done.2
  2.8 0.1 shard_map.51
  2.8 0.5 %collective-permute-start.4 = (bf16[1,4,12,16,128]{4,3,2,1,0:T(8,128)(2,1)S(1)}, bf16[1,4,12,16,128]{4,3,2,1,0:T(8,128)(2,1)S(1)}, u32[]{:S(2)}, u32[]{:S(2)}) collective-permute-start(bf16[1,4,12,16,128]{4,3,2,1,0:T(8,128)(2,1)S(1)} %bitcast.41), channel_id=1, source_target_pairs={{0,1},{1,0},{2,3},{3,2},{4,5},{5,4},{6,7},{7,6},{8,9},{9,8},{10,11... | collective-permute-start | bytes 589832 | tf_op jit(solution)/shard_map/ppermute | solution.py:130
  3.4 0.1 shard_map.50
  3.4 0.2 shard_map.46
  3.7 0.1 collective-permute-done
  3.8 3.0 %collective-permute-start.1 = (bf16[2,2,12,16,128]{4,3,2,1,0:T(8,128)(2,1)S(1)}, bf16[2,2,12,16,128]{4,3,2,1,0:T(8,128)(2,1)S(1)}, u32[]{:S(2)}, u32[]{:S(2)}) collective-permute-start(bf16[2,2,12,16,128]{4,3,2,1,0:T(8,128)(2,1)S(1)} %pad_maximum_fusion), channel_id=1, source_target_pairs={{0,4},{1,5},{2,6},{3,7},{4,0},{5,1},{6,2},{7,3},{8,12},{9,13},{10,... | collective-permute-start | bytes 589832 | tf_op jit(solution)/shard_map/ppermute | solution.py:130
  6.8 2.5 %collective-permute-start.9 = (bf16[2,2,12,16,128]{4,3,2,1,0:T(8,128)(2,1)S(1)}, bf16[2,2,12,16,128]{4,3,2,1,0:T(8,128)(2,1)S(1)}, u32[]{:S(2)}, u32[]{:S(2)}) collective-permute-start(bf16[2,2,12,16,128]{4,3,2,1,0:T(8,128)(2,1)S(1)} %pad_maximum_fusion.1), channel_id=1, source_target_pairs={{0,12},{1,13},{2,14},{3,15},{4,8},{5,9},{6,10},{7,11},{8,4},{9,5},... | collective-permute-start | bytes 589832 | tf_op jit(solution)/shard_map/ppermute | solution.py:130
  9.4 2.7 %collective-permute-done.1.refs_2_ = bf16[2,2,12,16,128]{4,3,2,1,0:T(8,128)(2,1)S(1)} collective-permute-done((bf16[2,2,12,16,128]{4,3,2,1,0:T(8,128)(2,1)S(1)}, bf16[2,2,12,16,128]{4,3,2,1,0:T(8,128)(2,1)S(1)}, u32[]{:S(2)}, u32[]{:S(2)}) %collective-permute-start.1) | collective-permute-done | bytes 196640 | tf_op jit(solution)/shard_map/ppermute | solution.py:130
  12.1 0.0 collective-permute-done.2
  12.1 1.7 %collective-permute-start.3 = (bf16[2,2,12,16,128]{4,3,2,1,0:T(8,128)(2,1)S(1)}, bf16[2,2,12,16,128]{4,3,2,1,0:T(8,128)(2,1)S(1)}, u32[]{:S(2)}, u32[]{:S(2)}) collective-permute-start(bf16[2,2,12,16,128]{4,3,2,1,0:T(8,128)(2,1)S(1)} %maximum_select_fusion.refs_0_), channel_id=1, source_target_pairs={{0,2},{1,3},{2,0},{3,1},{4,6},{5,7},{6,4},{7,5},{8,10},{9,11},{10,... | collective-permute-start | bytes 589832 | tf_op jit(solution)/shard_map/ppermute | solution.py:130
  13.8 0.0 collective-permute-done.4
  13.8 0.0 copy-start.3
  13.8 3.5 %collective-permute-start.11 = (bf16[2,2,12,16,128]{4,3,2,1,0:T(8,128)(2,1)S(1)}, bf16[2,2,12,16,128]{4,3,2,1,0:T(8,128)(2,1)S(1)}, u32[]{:S(2)}, u32[]{:S(2)}) collective-permute-start(bf16[2,2,12,16,128]{4,3,2,1,0:T(8,128)(2,1)S(1)} %pad_maximum_fusion.2), channel_id=1, source_target_pairs={{0,8},{1,9},{2,10},{3,11},{4,12},{5,13},{6,14},{7,15},{8,0},{9,1},... | collective-permute-start | bytes 589832 | tf_op jit(solution)/shard_map/ppermute | solution.py:130
  17.3 0.5 %collective-permute-start.8 = (bf16[2,2,12,16,128]{4,3,2,1,0:T(8,128)(2,1)S(1)}, bf16[2,2,12,16,128]{4,3,2,1,0:T(8,128)(2,1)S(1)}, u32[]{:S(2)}, u32[]{:S(2)}) collective-permute-start(bf16[2,2,12,16,128]{4,3,2,1,0:T(8,128)(2,1)S(1)} %collective-permute-done.1.refs_2_), channel_id=1, source_target_pairs={{0,2},{1,3},{2,0},{3,1},{4,6},{5,7},{6,4},{7,5},{8,10},{9,11},{10,... | collective-permute-start | bytes 589832 | tf_op jit(solution)/shard_map/ppermute | solution.py:130
  17.8 1.5 %collective-permute-done.9.refs_1_ = bf16[2,2,12,16,128]{4,3,2,1,0:T(8,128)(2,1)S(1)} collective-permute-done((bf16[2,2,12,16,128]{4,3,2,1,0:T(8,128)(2,1)S(1)}, bf16[2,2,12,16,128]{4,3,2,1,0:T(8,128)(2,1)S(1)}, u32[]{:S(2)}, u32[]{:S(2)}) %collective-permute-start.9) | collective-permute-done | bytes 196640 | tf_op jit(solution)/shard_map/ppermute | solution.py:130
  19.3 1.5 %collective-permute-start.10 = (bf16[2,2,12,16,128]{4,3,2,1,0:T(8,128)(2,1)S(1)}, bf16[2,2,12,16,128]{4,3,2,1,0:T(8,128)(2,1)S(1)}, u32[]{:S(2)}, u32[]{:S(2)}) collective-permute-start(bf16[2,2,12,16,128]{4,3,2,1,0:T(8,128)(2,1)S(1)} %collective-permute-done.9.refs_1_), channel_id=1, source_target_pairs={{0,2},{1,3},{2,0},{3,1},{4,6},{5,7},{6,4},{7,5},{8,10},{9,11},{10,... | collective-permute-start | bytes 589832 | tf_op jit(solution)/shard_map/ppermute | solution.py:130
  20.8 0.0 collective-permute-done.3.refs_1_
  20.8 0.0 copy-done.3
  20.8 0.6 %shard_map.49 = (bf16[16,72,128]{2,1,0:T(8,128)(2,1)S(1)}, bf16[16,72,128]{2,1,0:T(8,128)(2,1)S(1)}, f32[4,192]{1,0:T(4,128)S(1)}) custom-call(s32[4]{0:T(128)S(1)} %copy-done.3, bf16[2,2,12,16,128]{4,3,2,1,0:T(8,128)(2,1)S(1)} %maximum_select_fusion.refs_0_, bf16[2,2,12,16,128]{4,3,2,1,0:T(8,128)(2,1)S(1)} %collective-permute-done.3.refs_1_, ...), custom_call_target="tpu_custom_call" | custom-call | flops 10000000 | bytes 30000 | tf_op jit(solution)/shard_map/pallas_call | solution.py:172
  21.5 4.6 %collective-permute-start.7 = (bf16[1,2,12,16,128]{4,3,2,1,0:T(8,128)(2,1)S(1)}, bf16[1,2,12,16,128]{4,3,2,1,0:T(8,128)(2,1)S(1)}, u32[]{:S(2)}, u32[]{:S(2)}) collective-permute-start(bf16[1,2,12,16,128]{4,3,2,1,0:T(8,128)(2,1)S(1)} %get-tuple-element.34), channel_id=1, source_target_pairs={{0,4},{1,5},{2,6},{3,7},{4,0},{5,1},{6,2},{7,3},{8,12},{9,13},{10,... | collective-permute-start | bytes 294920 | tf_op jit(solution)/shard_map/ppermute | solution.py:130
  26.0 2.0 %collective-permute-start.6 = (bf16[1,2,12,16,128]{4,3,2,1,0:T(8,128)(2,1)S(1)}, bf16[1,2,12,16,128]{4,3,2,1,0:T(8,128)(2,1)S(1)}, u32[]{:S(2)}, u32[]{:S(2)}) collective-permute-start(bf16[1,2,12,16,128]{4,3,2,1,0:T(8,128)(2,1)S(1)} %get-tuple-element.35), channel_id=1, source_target_pairs={{0,8},{1,9},{2,10},{3,11},{4,12},{5,13},{6,14},{7,15},{8,0},{9,1},... | collective-permute-start | bytes 294920 | tf_op jit(solution)/shard_map/ppermute | solution.py:130
  28.0 0.0 collective-permute-done.8.refs_0_
  28.0 1.4 %collective-permute-start.5 = (bf16[1,2,12,16,128]{4,3,2,1,0:T(8,128)(2,1)S(1)}, bf16[1,2,12,16,128]{4,3,2,1,0:T(8,128)(2,1)S(1)}, u32[]{:S(2)}, u32[]{:S(2)}) collective-permute-start(bf16[1,2,12,16,128]{4,3,2,1,0:T(8,128)(2,1)S(1)} %get-tuple-element.36), channel_id=1, source_target_pairs={{0,12},{1,13},{2,14},{3,15},{4,8},{5,9},{6,10},{7,11},{8,4},{9,5},... | collective-permute-start | bytes 294920 | tf_op jit(solution)/shard_map/ppermute | solution.py:130
  29.4 0.0 collective-permute-done.11
  29.4 0.7 %collective-permute-start.12 = (bf16[2,2,12,16,128]{4,3,2,1,0:T(8,128)(2,1)S(1)}, bf16[2,2,12,16,128]{4,3,2,1,0:T(8,128)(2,1)S(1)}, u32[]{:S(2)}, u32[]{:S(2)}) collective-permute-start(bf16[2,2,12,16,128]{4,3,2,1,0:T(8,128)(2,1)S(1)} %broadcast_select_fusion.refs_3_), channel_id=1, source_target_pairs={{0,2},{1,3},{2,0},{3,1},{4,6},{5,7},{6,4},{7,5},{8,10},{9,11},{10,... | collective-permute-start | bytes 589832 | tf_op jit(solution)/shard_map/ppermute | solution.py:130
  30.1 0.0 collective-permute-done.7.refs_2_
  30.1 4.6 %collective-permute-done.6.refs_1_ = bf16[1,2,12,16,128]{4,3,2,1,0:T(8,128)(2,1)S(1)} collective-permute-done((bf16[1,2,12,16,128]{4,3,2,1,0:T(8,128)(2,1)S(1)}, bf16[1,2,12,16,128]{4,3,2,1,0:T(8,128)(2,1)S(1)}, u32[]{:S(2)}, u32[]{:S(2)}) %collective-permute-start.6) | collective-permute-done | bytes 98336 | tf_op jit(solution)/shard_map/ppermute | solution.py:130
  34.8 0.0 collective-permute-done.5.refs_0_
  34.8 0.1 shard_map.52.q
  34.9 0.0 collective-permute-done.10.refs_2_
  34.9 0.3 collective-permute-done.12.refs_4_
  35.2 1.3 %shard_map.53 = (bf16[2,12,16,128]{3,2,1,0:T(8,128)(2,1)S(1)}, bf16[2,12,16,128]{3,2,1,0:T(8,128)(2,1)S(1)}, bf16[2,12,16,128]{3,2,1,0:T(8,128)(2,1)S(1)}, bf16[2,12,16,128]{3,2,1,0:T(8,128)(2,1)S(1)}) custom-call(bf16[16,96,128]{2,1,0:T(8,128)(2,1)S(1)} %shard_map.52.q, bf16[2,2,12,16,128]{4,3,2,1,0:T(8,128)(2,1)S(1)} %collective-permute-done.8.refs_0_, ...), custom_call_target="tpu_custom_call" | custom-call | flops 2000000000 | bytes 6000000 | tf_op jit(solution)/shard_map/pallas_call | solution.py:194
  36.5 3.0 %collective-permute-start.13 = (bf16[2,12,16,128]{3,2,1,0:T(8,128)(2,1)S(1)}, bf16[2,12,16,128]{3,2,1,0:T(8,128)(2,1)S(1)}, u32[]{:S(2)}, u32[]{:S(2)}) collective-permute-start(bf16[2,12,16,128]{3,2,1,0:T(8,128)(2,1)S(1)} %get-tuple-element.15), channel_id=1, source_target_pairs={{0,12},{1,13},{2,14},{3,15},{4,8},{5,9},{6,10},{7,11},{8,4},{9,5},... | collective-permute-start | bytes 294920 | tf_op jit(solution)/shard_map/ppermute | solution.py:130
  39.5 0.0 collective-permute-start.14
  39.5 1.5 %collective-permute-start.15 = (bf16[2,12,16,128]{3,2,1,0:T(8,128)(2,1)S(1)}, bf16[2,12,16,128]{3,2,1,0:T(8,128)(2,1)S(1)}, u32[]{:S(2)}, u32[]{:S(2)}) collective-permute-start(bf16[2,12,16,128]{3,2,1,0:T(8,128)(2,1)S(1)} %get-tuple-element.17), channel_id=1, source_target_pairs={{0,4},{1,5},{2,6},{3,7},{4,0},{5,1},{6,2},{7,3},{8,12},{9,13},{10,... | collective-permute-start | bytes 294920 | tf_op jit(solution)/shard_map/ppermute | solution.py:130
  41.0 0.0 collective-permute-start.19
  41.0 3.0 %collective-permute-done.13 = bf16[2,12,16,128]{3,2,1,0:T(8,128)(2,1)S(1)} collective-permute-done((bf16[2,12,16,128]{3,2,1,0:T(8,128)(2,1)S(1)}, bf16[2,12,16,128]{3,2,1,0:T(8,128)(2,1)S(1)}, u32[]{:S(2)}, u32[]{:S(2)}) %collective-permute-start.13) | collective-permute-done | bytes 98336 | tf_op jit(solution)/shard_map/ppermute | solution.py:130
  43.9 0.0 collective-permute-start.16
  43.9 2.3 %collective-permute-done.14 = bf16[2,12,16,128]{3,2,1,0:T(8,128)(2,1)S(1)} collective-permute-done((bf16[2,12,16,128]{3,2,1,0:T(8,128)(2,1)S(1)}, bf16[2,12,16,128]{3,2,1,0:T(8,128)(2,1)S(1)}, u32[]{:S(2)}, u32[]{:S(2)}) %collective-permute-start.14) | collective-permute-done | bytes 98336 | tf_op jit(solution)/shard_map/ppermute | solution.py:130
  46.3 0.0 collective-permute-start.17
  46.3 0.0 collective-permute-done.15
  46.3 0.5 %collective-permute-start.18 = (bf16[2,12,16,128]{3,2,1,0:T(8,128)(2,1)S(1)}, bf16[2,12,16,128]{3,2,1,0:T(8,128)(2,1)S(1)}, u32[]{:S(2)}, u32[]{:S(2)}) collective-permute-start(bf16[2,12,16,128]{3,2,1,0:T(8,128)(2,1)S(1)} %collective-permute-done.15), channel_id=1, source_target_pairs={{0,1},{1,0},{2,3},{3,2},{4,5},{5,4},{6,7},{7,6},{8,9},{9,8},{10,11... | collective-permute-start | bytes 294920 | tf_op jit(solution)/shard_map/ppermute | solution.py:130
  46.8 0.0 collective-permute-done.19
  46.8 0.0 collective-permute-done.16
  46.8 0.8 %collective-permute-done.17 = bf16[2,12,16,128]{3,2,1,0:T(8,128)(2,1)S(1)} collective-permute-done((bf16[2,12,16,128]{3,2,1,0:T(8,128)(2,1)S(1)}, bf16[2,12,16,128]{3,2,1,0:T(8,128)(2,1)S(1)}, u32[]{:S(2)}, u32[]{:S(2)}) %collective-permute-start.17) | collective-permute-done | bytes 98336 | tf_op jit(solution)/shard_map/ppermute | solution.py:130
  47.6 0.2 collective-permute-done.18
  47.8 0.8 %shard_map.54 = bf16[12,32,4,128]{3,2,1,0:T(4,128)(2,1)} custom-call(bf16[2,12,4,4,128]{4,3,2,1,0:T(4,128)(2,1)S(1)} %bitcast.44, bf16[2,12,4,4,128]{4,3,2,1,0:T(4,128)(2,1)S(1)} %bitcast.45, bf16[2,12,4,4,128]{4,3,2,1,0:T(4,128)(2,1)S(1)} %bitcast.46, bf16[2,12,4,4,128]{4,3,2,1,0:T(4,128)(2,1)S(1)} %bitcast.42, bf16[2,12,4,4,128]{4,3,2,1,0:T(4,128)(2,1)S(1)} %bitcast.48, ...), custom_call_target="tpu_custom_call" | custom-call | tf_op jit(solution)/shard_map/pallas_call | solution.py:203
  (15 shorter events, 0.3 us)
Async XLA Ops:
  0.0 2.3 %copy-start = (bf16[12,4,4096]{2,1,0:T(4,128)(2,1)S(1)}, bf16[12,4,4096]{2,1,0:T(4,128)(2,1)}, u32[]{:S(2)}) copy-start(bf16[12,4,4096]{2,1,0:T(4,128)(2,1)} %param.5) | copy-start | bytes 1179652
  0.0 2.3 %copy-start.1 = (bf16[12,4,4096]{2,1,0:T(4,128)(2,1)S(1)}, bf16[12,4,4096]{2,1,0:T(4,128)(2,1)}, u32[]{:S(2)}) copy-start(bf16[12,4,4096]{2,1,0:T(4,128)(2,1)} %param.6) | copy-start | bytes 1179652
  1.8 1.0 %copy-start.2 = (bf16[12,4,4096]{2,1,0:T(4,128)(2,1)S(1)}, bf16[12,4,4096]{2,1,0:T(4,128)(2,1)}, u32[]{:S(2)}) copy-start(bf16[12,4,4096]{2,1,0:T(4,128)(2,1)} %param.4) | copy-start | bytes 1179652
  1.8 1.9 %collective-permute-start = (bf16[2,3,12,16,128]{4,3,2,1,0:T(8,128)(2,1)}, bf16[2,3,12,16,128]{4,3,2,1,0:T(8,128)(2,1)S(1)}, u32[]{:S(2)}, u32[]{:S(2)}) collective-permute-start(bf16[2,3,12,16,128]{4,3,2,1,0:T(8,128)(2,1)} %bitcast.51), channel_id=1, source_target_pairs={{0,1},{1,0},{2,3},{3,2},{4,5},{5,4},{6,7},{7,6},{8,9},{9,8},{10,11... | collective-permute-start | bytes 884744 | tf_op jit(solution)/shard_map/ppermute | solution.py:130
  2.4 9.7 %collective-permute-start.2 = (bf16[2,1,12,16,128]{4,3,2,1,0:T(8,128)(2,1)S(1)}, bf16[2,1,12,16,128]{4,3,2,1,0:T(8,128)(2,1)S(1)}, u32[]{:S(2)}, u32[]{:S(2)}) collective-permute-start(bf16[2,1,12,16,128]{4,3,2,1,0:T(8,128)(2,1)S(1)} %bitcast.43), channel_id=1, source_target_pairs={{0,1},{1,0},{2,3},{3,2},{4,5},{5,4},{6,7},{7,6},{8,9},{9,8},{10,11... | collective-permute-start | bytes 294920 | tf_op jit(solution)/shard_map/ppermute | solution.py:130
  2.8 10.9 %collective-permute-start.4 = (bf16[1,4,12,16,128]{4,3,2,1,0:T(8,128)(2,1)S(1)}, bf16[1,4,12,16,128]{4,3,2,1,0:T(8,128)(2,1)S(1)}, u32[]{:S(2)}, u32[]{:S(2)}) collective-permute-start(bf16[1,4,12,16,128]{4,3,2,1,0:T(8,128)(2,1)S(1)} %bitcast.41), channel_id=1, source_target_pairs={{0,1},{1,0},{2,3},{3,2},{4,5},{5,4},{6,7},{7,6},{8,9},{9,8},{10,11... | collective-permute-start | bytes 589832 | tf_op jit(solution)/shard_map/ppermute | solution.py:130
  3.8 8.3 %collective-permute-start.1 = (bf16[2,2,12,16,128]{4,3,2,1,0:T(8,128)(2,1)S(1)}, bf16[2,2,12,16,128]{4,3,2,1,0:T(8,128)(2,1)S(1)}, u32[]{:S(2)}, u32[]{:S(2)}) collective-permute-start(bf16[2,2,12,16,128]{4,3,2,1,0:T(8,128)(2,1)S(1)} %pad_maximum_fusion), channel_id=1, source_target_pairs={{0,4},{1,5},{2,6},{3,7},{4,0},{5,1},{6,2},{7,3},{8,12},{9,13},{10,... | collective-permute-start | bytes 589832 | tf_op jit(solution)/shard_map/ppermute | solution.py:130
  6.8 12.5 %collective-permute-start.9 = (bf16[2,2,12,16,128]{4,3,2,1,0:T(8,128)(2,1)S(1)}, bf16[2,2,12,16,128]{4,3,2,1,0:T(8,128)(2,1)S(1)}, u32[]{:S(2)}, u32[]{:S(2)}) collective-permute-start(bf16[2,2,12,16,128]{4,3,2,1,0:T(8,128)(2,1)S(1)} %pad_maximum_fusion.1), channel_id=1, source_target_pairs={{0,12},{1,13},{2,14},{3,15},{4,8},{5,9},{6,10},{7,11},{8,4},{9,5},... | collective-permute-start | bytes 589832 | tf_op jit(solution)/shard_map/ppermute | solution.py:130
  12.1 8.7 %collective-permute-start.3 = (bf16[2,2,12,16,128]{4,3,2,1,0:T(8,128)(2,1)S(1)}, bf16[2,2,12,16,128]{4,3,2,1,0:T(8,128)(2,1)S(1)}, u32[]{:S(2)}, u32[]{:S(2)}) collective-permute-start(bf16[2,2,12,16,128]{4,3,2,1,0:T(8,128)(2,1)S(1)} %maximum_select_fusion.refs_0_), channel_id=1, source_target_pairs={{0,2},{1,3},{2,0},{3,1},{4,6},{5,7},{6,4},{7,5},{8,10},{9,11},{10,... | collective-permute-start | bytes 589832 | tf_op jit(solution)/shard_map/ppermute | solution.py:130
  13.8 7.0 %copy-start.3 = (s32[4]{0:T(128)S(1)}, s32[4]{0:T(128)}, u32[]{:S(2)}) copy-start(s32[4]{0:T(128)} %frames_ref.1) | copy-start | bytes 52
  13.8 15.6 %collective-permute-start.11 = (bf16[2,2,12,16,128]{4,3,2,1,0:T(8,128)(2,1)S(1)}, bf16[2,2,12,16,128]{4,3,2,1,0:T(8,128)(2,1)S(1)}, u32[]{:S(2)}, u32[]{:S(2)}) collective-permute-start(bf16[2,2,12,16,128]{4,3,2,1,0:T(8,128)(2,1)S(1)} %pad_maximum_fusion.2), channel_id=1, source_target_pairs={{0,8},{1,9},{2,10},{3,11},{4,12},{5,13},{6,14},{7,15},{8,0},{9,1},... | collective-permute-start | bytes 589832 | tf_op jit(solution)/shard_map/ppermute | solution.py:130
  17.3 10.8 %collective-permute-start.8 = (bf16[2,2,12,16,128]{4,3,2,1,0:T(8,128)(2,1)S(1)}, bf16[2,2,12,16,128]{4,3,2,1,0:T(8,128)(2,1)S(1)}, u32[]{:S(2)}, u32[]{:S(2)}) collective-permute-start(bf16[2,2,12,16,128]{4,3,2,1,0:T(8,128)(2,1)S(1)} %collective-permute-done.1.refs_2_), channel_id=1, source_target_pairs={{0,2},{1,3},{2,0},{3,1},{4,6},{5,7},{6,4},{7,5},{8,10},{9,11},{10,... | collective-permute-start | bytes 589832 | tf_op jit(solution)/shard_map/ppermute | solution.py:130
  19.3 15.6 %collective-permute-start.10 = (bf16[2,2,12,16,128]{4,3,2,1,0:T(8,128)(2,1)S(1)}, bf16[2,2,12,16,128]{4,3,2,1,0:T(8,128)(2,1)S(1)}, u32[]{:S(2)}, u32[]{:S(2)}) collective-permute-start(bf16[2,2,12,16,128]{4,3,2,1,0:T(8,128)(2,1)S(1)} %collective-permute-done.9.refs_1_), channel_id=1, source_target_pairs={{0,2},{1,3},{2,0},{3,1},{4,6},{5,7},{6,4},{7,5},{8,10},{9,11},{10,... | collective-permute-start | bytes 589832 | tf_op jit(solution)/shard_map/ppermute | solution.py:130
  21.5 8.7 %collective-permute-start.7 = (bf16[1,2,12,16,128]{4,3,2,1,0:T(8,128)(2,1)S(1)}, bf16[1,2,12,16,128]{4,3,2,1,0:T(8,128)(2,1)S(1)}, u32[]{:S(2)}, u32[]{:S(2)}) collective-permute-start(bf16[1,2,12,16,128]{4,3,2,1,0:T(8,128)(2,1)S(1)} %get-tuple-element.34), channel_id=1, source_target_pairs={{0,4},{1,5},{2,6},{3,7},{4,0},{5,1},{6,2},{7,3},{8,12},{9,13},{10,... | collective-permute-start | bytes 294920 | tf_op jit(solution)/shard_map/ppermute | solution.py:130
  26.0 8.7 %collective-permute-start.6 = (bf16[1,2,12,16,128]{4,3,2,1,0:T(8,128)(2,1)S(1)}, bf16[1,2,12,16,128]{4,3,2,1,0:T(8,128)(2,1)S(1)}, u32[]{:S(2)}, u32[]{:S(2)}) collective-permute-start(bf16[1,2,12,16,128]{4,3,2,1,0:T(8,128)(2,1)S(1)} %get-tuple-element.35), channel_id=1, source_target_pairs={{0,8},{1,9},{2,10},{3,11},{4,12},{5,13},{6,14},{7,15},{8,0},{9,1},... | collective-permute-start | bytes 294920 | tf_op jit(solution)/shard_map/ppermute | solution.py:130
  28.0 6.7 %collective-permute-start.5 = (bf16[1,2,12,16,128]{4,3,2,1,0:T(8,128)(2,1)S(1)}, bf16[1,2,12,16,128]{4,3,2,1,0:T(8,128)(2,1)S(1)}, u32[]{:S(2)}, u32[]{:S(2)}) collective-permute-start(bf16[1,2,12,16,128]{4,3,2,1,0:T(8,128)(2,1)S(1)} %get-tuple-element.36), channel_id=1, source_target_pairs={{0,12},{1,13},{2,14},{3,15},{4,8},{5,9},{6,10},{7,11},{8,4},{9,5},... | collective-permute-start | bytes 294920 | tf_op jit(solution)/shard_map/ppermute | solution.py:130
  29.4 5.7 %collective-permute-start.12 = (bf16[2,2,12,16,128]{4,3,2,1,0:T(8,128)(2,1)S(1)}, bf16[2,2,12,16,128]{4,3,2,1,0:T(8,128)(2,1)S(1)}, u32[]{:S(2)}, u32[]{:S(2)}) collective-permute-start(bf16[2,2,12,16,128]{4,3,2,1,0:T(8,128)(2,1)S(1)} %broadcast_select_fusion.refs_3_), channel_id=1, source_target_pairs={{0,2},{1,3},{2,0},{3,1},{4,6},{5,7},{6,4},{7,5},{8,10},{9,11},{10,... | collective-permute-start | bytes 589832 | tf_op jit(solution)/shard_map/ppermute | solution.py:130
  36.5 7.4 %collective-permute-start.13 = (bf16[2,12,16,128]{3,2,1,0:T(8,128)(2,1)S(1)}, bf16[2,12,16,128]{3,2,1,0:T(8,128)(2,1)S(1)}, u32[]{:S(2)}, u32[]{:S(2)}) collective-permute-start(bf16[2,12,16,128]{3,2,1,0:T(8,128)(2,1)S(1)} %get-tuple-element.15), channel_id=1, source_target_pairs={{0,12},{1,13},{2,14},{3,15},{4,8},{5,9},{6,10},{7,11},{8,4},{9,5},... | collective-permute-start | bytes 294920 | tf_op jit(solution)/shard_map/ppermute | solution.py:130
  39.5 6.8 %collective-permute-start.14 = (bf16[2,12,16,128]{3,2,1,0:T(8,128)(2,1)S(1)}, bf16[2,12,16,128]{3,2,1,0:T(8,128)(2,1)S(1)}, u32[]{:S(2)}, u32[]{:S(2)}) collective-permute-start(bf16[2,12,16,128]{3,2,1,0:T(8,128)(2,1)S(1)} %get-tuple-element.16), channel_id=1, source_target_pairs={{0,8},{1,9},{2,10},{3,11},{4,12},{5,13},{6,14},{7,15},{8,0},{9,1},... | collective-permute-start | bytes 294920 | tf_op jit(solution)/shard_map/ppermute | solution.py:130
  39.5 6.8 %collective-permute-start.15 = (bf16[2,12,16,128]{3,2,1,0:T(8,128)(2,1)S(1)}, bf16[2,12,16,128]{3,2,1,0:T(8,128)(2,1)S(1)}, u32[]{:S(2)}, u32[]{:S(2)}) collective-permute-start(bf16[2,12,16,128]{3,2,1,0:T(8,128)(2,1)S(1)} %get-tuple-element.17), channel_id=1, source_target_pairs={{0,4},{1,5},{2,6},{3,7},{4,0},{5,1},{6,2},{7,3},{8,12},{9,13},{10,... | collective-permute-start | bytes 294920 | tf_op jit(solution)/shard_map/ppermute | solution.py:130
  41.0 5.8 %collective-permute-start.19 = (bf16[2,12,16,128]{3,2,1,0:T(8,128)(2,1)S(1)}, bf16[2,12,16,128]{3,2,1,0:T(8,128)(2,1)S(1)}, u32[]{:S(2)}, u32[]{:S(2)}) collective-permute-start(bf16[2,12,16,128]{3,2,1,0:T(8,128)(2,1)S(1)} %get-tuple-element.18), channel_id=1, source_target_pairs={{0,1},{1,0},{2,3},{3,2},{4,5},{5,4},{6,7},{7,6},{8,9},{9,8},{10,11... | collective-permute-start | bytes 294920 | tf_op jit(solution)/shard_map/ppermute | solution.py:130
  43.9 2.9 %collective-permute-start.16 = (bf16[2,12,16,128]{3,2,1,0:T(8,128)(2,1)S(1)}, bf16[2,12,16,128]{3,2,1,0:T(8,128)(2,1)S(1)}, u32[]{:S(2)}, u32[]{:S(2)}) collective-permute-start(bf16[2,12,16,128]{3,2,1,0:T(8,128)(2,1)S(1)} %collective-permute-done.13), channel_id=1, source_target_pairs={{0,1},{1,0},{2,3},{3,2},{4,5},{5,4},{6,7},{7,6},{8,9},{9,8},{10,11... | collective-permute-start | bytes 294920 | tf_op jit(solution)/shard_map/ppermute | solution.py:130
  46.3 1.3 %collective-permute-start.17 = (bf16[2,12,16,128]{3,2,1,0:T(8,128)(2,1)S(1)}, bf16[2,12,16,128]{3,2,1,0:T(8,128)(2,1)S(1)}, u32[]{:S(2)}, u32[]{:S(2)}) collective-permute-start(bf16[2,12,16,128]{3,2,1,0:T(8,128)(2,1)S(1)} %collective-permute-done.14), channel_id=1, source_target_pairs={{0,1},{1,0},{2,3},{3,2},{4,5},{5,4},{6,7},{7,6},{8,9},{9,8},{10,11... | collective-permute-start | bytes 294920 | tf_op jit(solution)/shard_map/ppermute | solution.py:130
  46.3 1.5 %collective-permute-start.18 = (bf16[2,12,16,128]{3,2,1,0:T(8,128)(2,1)S(1)}, bf16[2,12,16,128]{3,2,1,0:T(8,128)(2,1)S(1)}, u32[]{:S(2)}, u32[]{:S(2)}) collective-permute-start(bf16[2,12,16,128]{3,2,1,0:T(8,128)(2,1)S(1)} %collective-permute-done.15), channel_id=1, source_target_pairs={{0,1},{1,0},{2,3},{3,2},{4,5},{5,4},{6,7},{7,6},{8,9},{9,8},{10,11... | collective-permute-start | bytes 294920 | tf_op jit(solution)/shard_map/ppermute | solution.py:130

commit v7 on v6

--- a/solution.py
+++ b/solution.py
@@ -76,21 +76,23 @@
         bias_out[c:c + 1, :] = jnp.where(place < frames_ref[c] * frame_tokens, 0.0, neg_large)
 
 
-def query_kernel(*refs):
-    srcs, out = refs[:-1], refs[-1]
+def query_kernel(count, *refs):
+    srcs, kvs, (out, k_out, v_out) = refs[:count], refs[count:-3], refs[-3:]
     out[...] = turn(srcs, 0)
+    k_out[...] = turn(kvs, 0)
+    v_out[...] = turn(kvs, 1)
 
 
 def attend_kernel(count, q, *refs):
-    kvs, (k_near, v_near, bias), outs = refs[:count], refs[count:count + 3], refs[count + 3:]
-    k = jnp.concatenate([k_near[...], turn(kvs, 0)], axis=1)
-    v = jnp.concatenate([v_near[...], turn(kvs, 1)], axis=1)
+    kvs, (k_near, v_near, k_mid, v_mid, bias), outs = refs[:count], refs[count:count + 5], refs[count + 5:]
+    k = jnp.concatenate([k_near[...], k_mid[...], turn(kvs, 0)], axis=1)
+    v = jnp.concatenate([v_near[...], v_mid[...], turn(kvs, 1)], axis=1)
     slots = k.shape[0]
     clips = bias.shape[0]
     s = lax.dot_general(q[...], k, (((2,), (2,)), ((0,), (0,))), preferred_element_type=jnp.float32)
     s = s * (1.0 / math.sqrt(HDIM)) + jnp.concatenate([bias[...]] * (slots // clips), axis=0)[:, None, :]
     e = jnp.exp(s - jnp.max(s, axis=2, keepdims=True))
-    w = (e / jnp.sum(e, axis=2, keepdims=True)).astype(jnp.bfloat16)
+    w = (e * (1.0 / jnp.sum(e, axis=2, keepdims=True))).astype(jnp.bfloat16)
     o = lax.dot_general(w, v, (((2,), (1,)), ((0,), (0,))), preferred_element_type=jnp.float32)
     o = jnp.swapaxes(o.astype(jnp.bfloat16), 0, 1)
     tokens = outs[0].shape[1]
@@ -166,7 +168,9 @@
     crossed = {a: across(kv[a]) for a in near[::-1]}
     every = [(a, n) for a in near[::-1] + far for n in range(len(flips))]
     first = [(a, n) for a, n in every if a == 0 or a in near and n == 0]
-    rest = [p for p in every if p not in first]
+    last = [(a, n) for a, n in every if a in late and n]
+    middle = [p for p in every if p not in first and p not in last]
+    rest = middle + last
     marks = [(a * inner) ^ flips[n] ^ c for a, n in first + rest for c in (0, 1)]
     some = jax.ShapeDtypeStruct((slots, 2 * tokens * len(first), HDIM), bf)
     k_near, v_near, bias = pl.pallas_call(
@@ -186,17 +190,19 @@
         qs[a] = swap(after(pay, k_near), a * inner) if a else pay
     for a in late:
         crossed[a] = across(after(kv[a], crossed[near[0]][1]))
-    q = pl.pallas_call(
-        query_kernel, out_shape=jax.ShapeDtypeStruct((slots, outer * 2 * tokens, HDIM), bf),
-        in_specs=[VM] * outer, out_specs=VM, compiler_params=SMALL, cost_estimate=cost(1.3),
-    )(*[qs[a] for a in parts])
+    most = jax.ShapeDtypeStruct((slots, 2 * tokens * len(middle), HDIM), bf)
+    q, k_mid, v_mid = pl.pallas_call(
+        functools.partial(query_kernel, outer),
+        out_shape=[jax.ShapeDtypeStruct((slots, outer * 2 * tokens, HDIM), bf), most, most],
+        in_specs=[VM] * (outer + len(middle)), out_specs=[VM] * 3, compiler_params=LARGE, cost_estimate=cost(1.3),
+    )(*[qs[a] for a in parts], *[crossed[a][n] for a, n in middle])
     piece = jax.ShapeDtypeStruct((2, tokens, slots, HDIM), bf)
     res = pl.pallas_call(
-        functools.partial(attend_kernel, len(rest)),
+        functools.partial(attend_kernel, len(last)),
         out_shape=[piece] * outer,
-        in_specs=[VM] * (len(rest) + 4), out_specs=[VM] * outer,
+        in_specs=[VM] * (len(last) + 6), out_specs=[VM] * outer,
         compiler_params=LARGE, cost_estimate=cost(2),
-    )(q, *[crossed[a][n] for a, n in rest], k_near, v_near, bias)
+    )(q, *[crossed[a][n] for a, n in last], k_near, v_near, k_mid, v_mid, bias)
 
     outs = [swap(o, a * inner) if a else o for a, o in zip(parts, res)]
     came = [swap(o, 1) for o in outs]

time: 48.7 us -> 48.8 us (level)
  transfers between devices with their start and end apart: 20 -> 20, of which waited for: 9 -> 9; matrix products, arithmetic and copies ran while one was open for 1% -> 1% of each run, Pallas kernels for 2% -> 3%
where the time goes in v7:
time: 48.8 us; the launch traced here: 48.6 us
  starting transfers between devices  27.4 us (56%)
  waiting for transfers between devices  15.4 us (32%)
  Pallas kernels  5.04 us (10%)
    ppermute x20, starting transfers between devices, swap(): return lax.ppermute(x, 'seq', [(i, i ^ mask) for i in range(devices)])  27.4 us
    ppermute x20, waiting for transfers between devices, swap(): return lax.ppermute(x, 'seq', [(i, i ^ mask) for i in range(devices)])  15.4 us
    pallas_call x5, Pallas kernels, pack(): pl.pallas_call(functools.partial(pack_kernel, outer, len(srcs), partners,...  2.11 us
    pallas_call x1, Pallas kernels, body(): pl.pallas_call(functools.partial(attend_kernel, len(last)), out_shape=[pi...  1.17 us
  transfers between devices with their start and end apart: 20, of which 9 were waited for; matrix products, arithmetic and copies ran while one was open for 1% of the time, Pallas kernels for 3%

profile of v7, /device:TPU:0, one launch (start us, length us, event | category | flops | bytes accessed | tf_op | source)
XLA Modules:
  0.0 48.6 jit_solution(112084144856371163)
XLA Ops:
  0.0 0.0 copy-start
  0.0 0.0 copy-start.1
  0.0 1.8 %shard_map.47 = bf16[2,3,12,4,4,128]{5,4,3,2,1,0:T(4,128)(2,1)} custom-call(bf16[12,32,4,128]{3,2,1,0:T(4,128)(2,1)} %bitcast.31, bf16[12,32,4,128]{3,2,1,0:T(4,128)(2,1)} %bitcast.34), custom_call_target="tpu_custom_call" | custom-call | tf_op jit(solution)/shard_map/pallas_call | solution.py:50
  1.8 0.0 copy-start.2
  1.8 0.5 %collective-permute-start = (bf16[2,3,12,16,128]{4,3,2,1,0:T(8,128)(2,1)}, bf16[2,3,12,16,128]{4,3,2,1,0:T(8,128)(2,1)S(1)}, u32[]{:S(2)}, u32[]{:S(2)}) collective-permute-start(bf16[2,3,12,16,128]{4,3,2,1,0:T(8,128)(2,1)} %bitcast.51), channel_id=1, source_target_pairs={{0,1},{1,0},{2,3},{3,2},{4,5},{5,4},{6,7},{7,6},{8,9},{9,8},{10,11... | collective-permute-start | bytes 884744 | tf_op jit(solution)/shard_map/ppermute | solution.py:132
  2.3 0.0 copy-done
  2.3 0.0 copy-done.1
  2.4 0.1 collective-permute-start.2
  2.5 0.3 copy-done.2
  2.8 0.1 shard_map.51
  2.8 0.5 %collective-permute-start.4 = (bf16[1,4,12,16,128]{4,3,2,1,0:T(8,128)(2,1)S(1)}, bf16[1,4,12,16,128]{4,3,2,1,0:T(8,128)(2,1)S(1)}, u32[]{:S(2)}, u32[]{:S(2)}) collective-permute-start(bf16[1,4,12,16,128]{4,3,2,1,0:T(8,128)(2,1)S(1)} %bitcast.41), channel_id=1, source_target_pairs={{0,1},{1,0},{2,3},{3,2},{4,5},{5,4},{6,7},{7,6},{8,9},{9,8},{10,11... | collective-permute-start | bytes 589832 | tf_op jit(solution)/shard_map/ppermute | solution.py:132
  3.4 0.1 shard_map.50
  3.4 0.2 shard_map.46
  3.7 0.1 collective-permute-done
  3.8 3.0 %collective-permute-start.1 = (bf16[2,2,12,16,128]{4,3,2,1,0:T(8,128)(2,1)S(1)}, bf16[2,2,12,16,128]{4,3,2,1,0:T(8,128)(2,1)S(1)}, u32[]{:S(2)}, u32[]{:S(2)}) collective-permute-start(bf16[2,2,12,16,128]{4,3,2,1,0:T(8,128)(2,1)S(1)} %pad_maximum_fusion), channel_id=1, source_target_pairs={{0,4},{1,5},{2,6},{3,7},{4,0},{5,1},{6,2},{7,3},{8,12},{9,13},{10,... | collective-permute-start | bytes 589832 | tf_op jit(solution)/shard_map/ppermute | solution.py:132
  6.8 2.5 %collective-permute-start.9 = (bf16[2,2,12,16,128]{4,3,2,1,0:T(8,128)(2,1)S(1)}, bf16[2,2,12,16,128]{4,3,2,1,0:T(8,128)(2,1)S(1)}, u32[]{:S(2)}, u32[]{:S(2)}) collective-permute-start(bf16[2,2,12,16,128]{4,3,2,1,0:T(8,128)(2,1)S(1)} %pad_maximum_fusion.1), channel_id=1, source_target_pairs={{0,12},{1,13},{2,14},{3,15},{4,8},{5,9},{6,10},{7,11},{8,4},{9,5},... | collective-permute-start | bytes 589832 | tf_op jit(solution)/shard_map/ppermute | solution.py:132
  9.4 2.7 %collective-permute-done.1.refs_2_ = bf16[2,2,12,16,128]{4,3,2,1,0:T(8,128)(2,1)S(1)} collective-permute-done((bf16[2,2,12,16,128]{4,3,2,1,0:T(8,128)(2,1)S(1)}, bf16[2,2,12,16,128]{4,3,2,1,0:T(8,128)(2,1)S(1)}, u32[]{:S(2)}, u32[]{:S(2)}) %collective-permute-start.1) | collective-permute-done | bytes 196640 | tf_op jit(solution)/shard_map/ppermute | solution.py:132
  12.1 0.0 collective-permute-done.2
  12.1 1.7 %collective-permute-start.3 = (bf16[2,2,12,16,128]{4,3,2,1,0:T(8,128)(2,1)S(1)}, bf16[2,2,12,16,128]{4,3,2,1,0:T(8,128)(2,1)S(1)}, u32[]{:S(2)}, u32[]{:S(2)}) collective-permute-start(bf16[2,2,12,16,128]{4,3,2,1,0:T(8,128)(2,1)S(1)} %maximum_select_fusion.refs_0_), channel_id=1, source_target_pairs={{0,2},{1,3},{2,0},{3,1},{4,6},{5,7},{6,4},{7,5},{8,10},{9,11},{10,... | collective-permute-start | bytes 589832 | tf_op jit(solution)/shard_map/ppermute | solution.py:132
  13.8 0.0 collective-permute-done.4
  13.8 0.0 copy-start.3
  13.8 3.5 %collective-permute-start.11 = (bf16[2,2,12,16,128]{4,3,2,1,0:T(8,128)(2,1)S(1)}, bf16[2,2,12,16,128]{4,3,2,1,0:T(8,128)(2,1)S(1)}, u32[]{:S(2)}, u32[]{:S(2)}) collective-permute-start(bf16[2,2,12,16,128]{4,3,2,1,0:T(8,128)(2,1)S(1)} %pad_maximum_fusion.2), channel_id=1, source_target_pairs={{0,8},{1,9},{2,10},{3,11},{4,12},{5,13},{6,14},{7,15},{8,0},{9,1},... | collective-permute-start | bytes 589832 | tf_op jit(solution)/shard_map/ppermute | solution.py:132
  17.3 0.5 %collective-permute-start.8 = (bf16[2,2,12,16,128]{4,3,2,1,0:T(8,128)(2,1)S(1)}, bf16[2,2,12,16,128]{4,3,2,1,0:T(8,128)(2,1)S(1)}, u32[]{:S(2)}, u32[]{:S(2)}) collective-permute-start(bf16[2,2,12,16,128]{4,3,2,1,0:T(8,128)(2,1)S(1)} %collective-permute-done.1.refs_2_), channel_id=1, source_target_pairs={{0,2},{1,3},{2,0},{3,1},{4,6},{5,7},{6,4},{7,5},{8,10},{9,11},{10,... | collective-permute-start | bytes 589832 | tf_op jit(solution)/shard_map/ppermute | solution.py:132
  17.8 1.5 %collective-permute-done.9.refs_5_ = bf16[2,2,12,16,128]{4,3,2,1,0:T(8,128)(2,1)S(1)} collective-permute-done((bf16[2,2,12,16,128]{4,3,2,1,0:T(8,128)(2,1)S(1)}, bf16[2,2,12,16,128]{4,3,2,1,0:T(8,128)(2,1)S(1)}, u32[]{:S(2)}, u32[]{:S(2)}) %collective-permute-start.9) | collective-permute-done | bytes 196640 | tf_op jit(solution)/shard_map/ppermute | solution.py:132
  19.3 1.5 %collective-permute-start.10 = (bf16[2,2,12,16,128]{4,3,2,1,0:T(8,128)(2,1)S(1)}, bf16[2,2,12,16,128]{4,3,2,1,0:T(8,128)(2,1)S(1)}, u32[]{:S(2)}, u32[]{:S(2)}) collective-permute-start(bf16[2,2,12,16,128]{4,3,2,1,0:T(8,128)(2,1)S(1)} %collective-permute-done.9.refs_5_), channel_id=1, source_target_pairs={{0,2},{1,3},{2,0},{3,1},{4,6},{5,7},{6,4},{7,5},{8,10},{9,11},{10,... | collective-permute-start | bytes 589832 | tf_op jit(solution)/shard_map/ppermute | solution.py:132
  20.8 0.0 collective-permute-done.3.refs_1_
  20.8 0.0 copy-done.3
  20.8 0.6 %shard_map.49 = (bf16[16,72,128]{2,1,0:T(8,128)(2,1)S(1)}, bf16[16,72,128]{2,1,0:T(8,128)(2,1)S(1)}, f32[4,192]{1,0:T(4,128)S(1)}) custom-call(s32[4]{0:T(128)S(1)} %copy-done.3, bf16[2,2,12,16,128]{4,3,2,1,0:T(8,128)(2,1)S(1)} %maximum_select_fusion.refs_0_, bf16[2,2,12,16,128]{4,3,2,1,0:T(8,128)(2,1)S(1)} %collective-permute-done.3.refs_1_, ...), custom_call_target="tpu_custom_call" | custom-call | flops 10000000 | bytes 30000 | tf_op jit(solution)/shard_map/pallas_call | solution.py:176
  21.5 4.6 %collective-permute-start.7 = (bf16[1,2,12,16,128]{4,3,2,1,0:T(8,128)(2,1)S(1)}, bf16[1,2,12,16,128]{4,3,2,1,0:T(8,128)(2,1)S(1)}, u32[]{:S(2)}, u32[]{:S(2)}) collective-permute-start(bf16[1,2,12,16,128]{4,3,2,1,0:T(8,128)(2,1)S(1)} %get-tuple-element.40), channel_id=1, source_target_pairs={{0,4},{1,5},{2,6},{3,7},{4,0},{5,1},{6,2},{7,3},{8,12},{9,13},{10,... | collective-permute-start | bytes 294920 | tf_op jit(solution)/shard_map/ppermute | solution.py:132
  26.0 2.0 %collective-permute-start.6 = (bf16[1,2,12,16,128]{4,3,2,1,0:T(8,128)(2,1)S(1)}, bf16[1,2,12,16,128]{4,3,2,1,0:T(8,128)(2,1)S(1)}, u32[]{:S(2)}, u32[]{:S(2)}) collective-permute-start(bf16[1,2,12,16,128]{4,3,2,1,0:T(8,128)(2,1)S(1)} %get-tuple-element.41), channel_id=1, source_target_pairs={{0,8},{1,9},{2,10},{3,11},{4,12},{5,13},{6,14},{7,15},{8,0},{9,1},... | collective-permute-start | bytes 294920 | tf_op jit(solution)/shard_map/ppermute | solution.py:132
  28.0 0.0 collective-permute-done.8.refs_4_
  28.0 1.4 %collective-permute-start.5 = (bf16[1,2,12,16,128]{4,3,2,1,0:T(8,128)(2,1)S(1)}, bf16[1,2,12,16,128]{4,3,2,1,0:T(8,128)(2,1)S(1)}, u32[]{:S(2)}, u32[]{:S(2)}) collective-permute-start(bf16[1,2,12,16,128]{4,3,2,1,0:T(8,128)(2,1)S(1)} %get-tuple-element.42), channel_id=1, source_target_pairs={{0,12},{1,13},{2,14},{3,15},{4,8},{5,9},{6,10},{7,11},{8,4},{9,5},... | collective-permute-start | bytes 294920 | tf_op jit(solution)/shard_map/ppermute | solution.py:132
  29.4 0.0 collective-permute-done.11
  29.4 0.7 %collective-permute-start.12 = (bf16[2,2,12,16,128]{4,3,2,1,0:T(8,128)(2,1)S(1)}, bf16[2,2,12,16,128]{4,3,2,1,0:T(8,128)(2,1)S(1)}, u32[]{:S(2)}, u32[]{:S(2)}) collective-permute-start(bf16[2,2,12,16,128]{4,3,2,1,0:T(8,128)(2,1)S(1)} %broadcast_select_fusion.refs_7_), channel_id=1, source_target_pairs={{0,2},{1,3},{2,0},{3,1},{4,6},{5,7},{6,4},{7,5},{8,10},{9,11},{10,... | collective-permute-start | bytes 589832 | tf_op jit(solution)/shard_map/ppermute | solution.py:132
  30.1 0.0 collective-permute-done.10.refs_6_
  30.1 0.0 collective-permute-done.7.refs_2_
  30.1 4.6 %collective-permute-done.6.refs_1_ = bf16[1,2,12,16,128]{4,3,2,1,0:T(8,128)(2,1)S(1)} collective-permute-done((bf16[1,2,12,16,128]{4,3,2,1,0:T(8,128)(2,1)S(1)}, bf16[1,2,12,16,128]{4,3,2,1,0:T(8,128)(2,1)S(1)}, u32[]{:S(2)}, u32[]{:S(2)}) %collective-permute-start.6) | collective-permute-done | bytes 98336 | tf_op jit(solution)/shard_map/ppermute | solution.py:132
  34.8 0.0 collective-permute-done.5.refs_0_
  34.8 0.4 shard_map.52
  35.1 0.1 collective-permute-done.12.refs_0_
  35.2 1.2 %shard_map.53 = (bf16[2,12,16,128]{3,2,1,0:T(8,128)(2,1)S(1)}, bf16[2,12,16,128]{3,2,1,0:T(8,128)(2,1)S(1)}, bf16[2,12,16,128]{3,2,1,0:T(8,128)(2,1)S(1)}, bf16[2,12,16,128]{3,2,1,0:T(8,128)(2,1)S(1)}) custom-call(bf16[16,96,128]{2,1,0:T(8,128)(2,1)S(1)} %get-tuple-element.16.q, bf16[2,2,12,16,128]{4,3,2,1,0:T(8,128)(2,1)S(1)} %collective-permute-done.12.refs_0_, ...), custom_call_target="tpu_custom_call" | custom-call | flops 2000000000 | bytes 6000000 | tf_op jit(solution)/shard_map/pallas_call | solution.py:200
  36.4 3.0 %collective-permute-start.13 = (bf16[2,12,16,128]{3,2,1,0:T(8,128)(2,1)S(1)}, bf16[2,12,16,128]{3,2,1,0:T(8,128)(2,1)S(1)}, u32[]{:S(2)}, u32[]{:S(2)}) collective-permute-start(bf16[2,12,16,128]{3,2,1,0:T(8,128)(2,1)S(1)} %get-tuple-element.21), channel_id=1, source_target_pairs={{0,12},{1,13},{2,14},{3,15},{4,8},{5,9},{6,10},{7,11},{8,4},{9,5},... | collective-permute-start | bytes 294920 | tf_op jit(solution)/shard_map/ppermute | solution.py:132
  39.3 0.1 collective-permute-start.14
  39.5 1.4 %collective-permute-start.15 = (bf16[2,12,16,128]{3,2,1,0:T(8,128)(2,1)S(1)}, bf16[2,12,16,128]{3,2,1,0:T(8,128)(2,1)S(1)}, u32[]{:S(2)}, u32[]{:S(2)}) collective-permute-start(bf16[2,12,16,128]{3,2,1,0:T(8,128)(2,1)S(1)} %get-tuple-element.23), channel_id=1, source_target_pairs={{0,4},{1,5},{2,6},{3,7},{4,0},{5,1},{6,2},{7,3},{8,12},{9,13},{10,... | collective-permute-start | bytes 294920 | tf_op jit(solution)/shard_map/ppermute | solution.py:132
  40.8 0.0 collective-permute-start.19
  40.8 3.2 %collective-permute-done.13 = bf16[2,12,16,128]{3,2,1,0:T(8,128)(2,1)S(1)} collective-permute-done((bf16[2,12,16,128]{3,2,1,0:T(8,128)(2,1)S(1)}, bf16[2,12,16,128]{3,2,1,0:T(8,128)(2,1)S(1)}, u32[]{:S(2)}, u32[]{:S(2)}) %collective-permute-start.13) | collective-permute-done | bytes 98336 | tf_op jit(solution)/shard_map/ppermute | solution.py:132
  44.0 0.0 collective-permute-start.16
  44.0 2.4 %collective-permute-done.14 = bf16[2,12,16,128]{3,2,1,0:T(8,128)(2,1)S(1)} collective-permute-done((bf16[2,12,16,128]{3,2,1,0:T(8,128)(2,1)S(1)}, bf16[2,12,16,128]{3,2,1,0:T(8,128)(2,1)S(1)}, u32[]{:S(2)}, u32[]{:S(2)}) %collective-permute-start.14) | collective-permute-done | bytes 98336 | tf_op jit(solution)/shard_map/ppermute | solution.py:132
  46.4 0.0 collective-permute-start.17
  46.4 0.0 collective-permute-done.15
  46.4 0.5 %collective-permute-start.18 = (bf16[2,12,16,128]{3,2,1,0:T(8,128)(2,1)S(1)}, bf16[2,12,16,128]{3,2,1,0:T(8,128)(2,1)S(1)}, u32[]{:S(2)}, u32[]{:S(2)}) collective-permute-start(bf16[2,12,16,128]{3,2,1,0:T(8,128)(2,1)S(1)} %collective-permute-done.15), channel_id=1, source_target_pairs={{0,1},{1,0},{2,3},{3,2},{4,5},{5,4},{6,7},{7,6},{8,9},{9,8},{10,11... | collective-permute-start | bytes 294920 | tf_op jit(solution)/shard_map/ppermute | solution.py:132
  46.9 0.0 collective-permute-done.19
  46.9 0.0 collective-permute-done.16
  46.9 0.8 %collective-permute-done.17 = bf16[2,12,16,128]{3,2,1,0:T(8,128)(2,1)S(1)} collective-permute-done((bf16[2,12,16,128]{3,2,1,0:T(8,128)(2,1)S(1)}, bf16[2,12,16,128]{3,2,1,0:T(8,128)(2,1)S(1)}, u32[]{:S(2)}, u32[]{:S(2)}) %collective-permute-start.17) | collective-permute-done | bytes 98336 | tf_op jit(solution)/shard_map/ppermute | solution.py:132
  47.7 0.2 collective-permute-done.18
  47.8 0.8 %shard_map.54 = bf16[12,32,4,128]{3,2,1,0:T(4,128)(2,1)} custom-call(bf16[2,12,4,4,128]{4,3,2,1,0:T(4,128)(2,1)S(1)} %bitcast.44, bf16[2,12,4,4,128]{4,3,2,1,0:T(4,128)(2,1)S(1)} %bitcast.45, bf16[2,12,4,4,128]{4,3,2,1,0:T(4,128)(2,1)S(1)} %bitcast.46, bf16[2,12,4,4,128]{4,3,2,1,0:T(4,128)(2,1)S(1)} %bitcast.42, bf16[2,12,4,4,128]{4,3,2,1,0:T(4,128)(2,1)S(1)} %bitcast.48, ...), custom_call_target="tpu_custom_call" | custom-call | tf_op jit(solution)/shard_map/pallas_call | solution.py:209
  (15 shorter events, 0.3 us)
Async XLA Ops:
  0.0 2.3 %copy-start = (bf16[12,4,4096]{2,1,0:T(4,128)(2,1)S(1)}, bf16[12,4,4096]{2,1,0:T(4,128)(2,1)}, u32[]{:S(2)}) copy-start(bf16[12,4,4096]{2,1,0:T(4,128)(2,1)} %param.5) | copy-start | bytes 1179652
  0.0 2.3 %copy-start.1 = (bf16[12,4,4096]{2,1,0:T(4,128)(2,1)S(1)}, bf16[12,4,4096]{2,1,0:T(4,128)(2,1)}, u32[]{:S(2)}) copy-start(bf16[12,4,4096]{2,1,0:T(4,128)(2,1)} %param.6) | copy-start | bytes 1179652
  1.8 1.0 %copy-start.2 = (bf16[12,4,4096]{2,1,0:T(4,128)(2,1)S(1)}, bf16[12,4,4096]{2,1,0:T(4,128)(2,1)}, u32[]{:S(2)}) copy-start(bf16[12,4,4096]{2,1,0:T(4,128)(2,1)} %param.4) | copy-start | bytes 1179652
  1.8 1.9 %collective-permute-start = (bf16[2,3,12,16,128]{4,3,2,1,0:T(8,128)(2,1)}, bf16[2,3,12,16,128]{4,3,2,1,0:T(8,128)(2,1)S(1)}, u32[]{:S(2)}, u32[]{:S(2)}) collective-permute-start(bf16[2,3,12,16,128]{4,3,2,1,0:T(8,128)(2,1)} %bitcast.51), channel_id=1, source_target_pairs={{0,1},{1,0},{2,3},{3,2},{4,5},{5,4},{6,7},{7,6},{8,9},{9,8},{10,11... | collective-permute-start | bytes 884744 | tf_op jit(solution)/shard_map/ppermute | solution.py:132
  2.4 9.7 %collective-permute-start.2 = (bf16[2,1,12,16,128]{4,3,2,1,0:T(8,128)(2,1)S(1)}, bf16[2,1,12,16,128]{4,3,2,1,0:T(8,128)(2,1)S(1)}, u32[]{:S(2)}, u32[]{:S(2)}) collective-permute-start(bf16[2,1,12,16,128]{4,3,2,1,0:T(8,128)(2,1)S(1)} %bitcast.43), channel_id=1, source_target_pairs={{0,1},{1,0},{2,3},{3,2},{4,5},{5,4},{6,7},{7,6},{8,9},{9,8},{10,11... | collective-permute-start | bytes 294920 | tf_op jit(solution)/shard_map/ppermute | solution.py:132
  2.8 10.9 %collective-permute-start.4 = (bf16[1,4,12,16,128]{4,3,2,1,0:T(8,128)(2,1)S(1)}, bf16[1,4,12,16,128]{4,3,2,1,0:T(8,128)(2,1)S(1)}, u32[]{:S(2)}, u32[]{:S(2)}) collective-permute-start(bf16[1,4,12,16,128]{4,3,2,1,0:T(8,128)(2,1)S(1)} %bitcast.41), channel_id=1, source_target_pairs={{0,1},{1,0},{2,3},{3,2},{4,5},{5,4},{6,7},{7,6},{8,9},{9,8},{10,11... | collective-permute-start | bytes 589832 | tf_op jit(solution)/shard_map/ppermute | solution.py:132
  3.8 8.3 %collective-permute-start.1 = (bf16[2,2,12,16,128]{4,3,2,1,0:T(8,128)(2,1)S(1)}, bf16[2,2,12,16,128]{4,3,2,1,0:T(8,128)(2,1)S(1)}, u32[]{:S(2)}, u32[]{:S(2)}) collective-permute-start(bf16[2,2,12,16,128]{4,3,2,1,0:T(8,128)(2,1)S(1)} %pad_maximum_fusion), channel_id=1, source_target_pairs={{0,4},{1,5},{2,6},{3,7},{4,0},{5,1},{6,2},{7,3},{8,12},{9,13},{10,... | collective-permute-start | bytes 589832 | tf_op jit(solution)/shard_map/ppermute | solution.py:132
  6.8 12.5 %collective-permute-start.9 = (bf16[2,2,12,16,128]{4,3,2,1,0:T(8,128)(2,1)S(1)}, bf16[2,2,12,16,128]{4,3,2,1,0:T(8,128)(2,1)S(1)}, u32[]{:S(2)}, u32[]{:S(2)}) collective-permute-start(bf16[2,2,12,16,128]{4,3,2,1,0:T(8,128)(2,1)S(1)} %pad_maximum_fusion.1), channel_id=1, source_target_pairs={{0,12},{1,13},{2,14},{3,15},{4,8},{5,9},{6,10},{7,11},{8,4},{9,5},... | collective-permute-start | bytes 589832 | tf_op jit(solution)/shard_map/ppermute | solution.py:132
  12.1 8.7 %collective-permute-start.3 = (bf16[2,2,12,16,128]{4,3,2,1,0:T(8,128)(2,1)S(1)}, bf16[2,2,12,16,128]{4,3,2,1,0:T(8,128)(2,1)S(1)}, u32[]{:S(2)}, u32[]{:S(2)}) collective-permute-start(bf16[2,2,12,16,128]{4,3,2,1,0:T(8,128)(2,1)S(1)} %maximum_select_fusion.refs_0_), channel_id=1, source_target_pairs={{0,2},{1,3},{2,0},{3,1},{4,6},{5,7},{6,4},{7,5},{8,10},{9,11},{10,... | collective-permute-start | bytes 589832 | tf_op jit(solution)/shard_map/ppermute | solution.py:132
  13.8 7.0 %copy-start.3 = (s32[4]{0:T(128)S(1)}, s32[4]{0:T(128)}, u32[]{:S(2)}) copy-start(s32[4]{0:T(128)} %frames_ref.1) | copy-start | bytes 52
  13.8 15.6 %collective-permute-start.11 = (bf16[2,2,12,16,128]{4,3,2,1,0:T(8,128)(2,1)S(1)}, bf16[2,2,12,16,128]{4,3,2,1,0:T(8,128)(2,1)S(1)}, u32[]{:S(2)}, u32[]{:S(2)}) collective-permute-start(bf16[2,2,12,16,128]{4,3,2,1,0:T(8,128)(2,1)S(1)} %pad_maximum_fusion.2), channel_id=1, source_target_pairs={{0,8},{1,9},{2,10},{3,11},{4,12},{5,13},{6,14},{7,15},{8,0},{9,1},... | collective-permute-start | bytes 589832 | tf_op jit(solution)/shard_map/ppermute | solution.py:132
  17.3 10.8 %collective-permute-start.8 = (bf16[2,2,12,16,128]{4,3,2,1,0:T(8,128)(2,1)S(1)}, bf16[2,2,12,16,128]{4,3,2,1,0:T(8,128)(2,1)S(1)}, u32[]{:S(2)}, u32[]{:S(2)}) collective-permute-start(bf16[2,2,12,16,128]{4,3,2,1,0:T(8,128)(2,1)S(1)} %collective-permute-done.1.refs_2_), channel_id=1, source_target_pairs={{0,2},{1,3},{2,0},{3,1},{4,6},{5,7},{6,4},{7,5},{8,10},{9,11},{10,... | collective-permute-start | bytes 589832 | tf_op jit(solution)/shard_map/ppermute | solution.py:132
  19.3 10.8 %collective-permute-start.10 = (bf16[2,2,12,16,128]{4,3,2,1,0:T(8,128)(2,1)S(1)}, bf16[2,2,12,16,128]{4,3,2,1,0:T(8,128)(2,1)S(1)}, u32[]{:S(2)}, u32[]{:S(2)}) collective-permute-start(bf16[2,2,12,16,128]{4,3,2,1,0:T(8,128)(2,1)S(1)} %collective-permute-done.9.refs_5_), channel_id=1, source_target_pairs={{0,2},{1,3},{2,0},{3,1},{4,6},{5,7},{6,4},{7,5},{8,10},{9,11},{10,... | collective-permute-start | bytes 589832 | tf_op jit(solution)/shard_map/ppermute | solution.py:132
  21.5 8.7 %collective-permute-start.7 = (bf16[1,2,12,16,128]{4,3,2,1,0:T(8,128)(2,1)S(1)}, bf16[1,2,12,16,128]{4,3,2,1,0:T(8,128)(2,1)S(1)}, u32[]{:S(2)}, u32[]{:S(2)}) collective-permute-start(bf16[1,2,12,16,128]{4,3,2,1,0:T(8,128)(2,1)S(1)} %get-tuple-element.40), channel_id=1, source_target_pairs={{0,4},{1,5},{2,6},{3,7},{4,0},{5,1},{6,2},{7,3},{8,12},{9,13},{10,... | collective-permute-start | bytes 294920 | tf_op jit(solution)/shard_map/ppermute | solution.py:132
  26.0 8.7 %collective-permute-start.6 = (bf16[1,2,12,16,128]{4,3,2,1,0:T(8,128)(2,1)S(1)}, bf16[1,2,12,16,128]{4,3,2,1,0:T(8,128)(2,1)S(1)}, u32[]{:S(2)}, u32[]{:S(2)}) collective-permute-start(bf16[1,2,12,16,128]{4,3,2,1,0:T(8,128)(2,1)S(1)} %get-tuple-element.41), channel_id=1, source_target_pairs={{0,8},{1,9},{2,10},{3,11},{4,12},{5,13},{6,14},{7,15},{8,0},{9,1},... | collective-permute-start | bytes 294920 | tf_op jit(solution)/shard_map/ppermute | solution.py:132
  28.0 6.7 %collective-permute-start.5 = (bf16[1,2,12,16,128]{4,3,2,1,0:T(8,128)(2,1)S(1)}, bf16[1,2,12,16,128]{4,3,2,1,0:T(8,128)(2,1)S(1)}, u32[]{:S(2)}, u32[]{:S(2)}) collective-permute-start(bf16[1,2,12,16,128]{4,3,2,1,0:T(8,128)(2,1)S(1)} %get-tuple-element.42), channel_id=1, source_target_pairs={{0,12},{1,13},{2,14},{3,15},{4,8},{5,9},{6,10},{7,11},{8,4},{9,5},... | collective-permute-start | bytes 294920 | tf_op jit(solution)/shard_map/ppermute | solution.py:132
  29.4 5.7 %collective-permute-start.12 = (bf16[2,2,12,16,128]{4,3,2,1,0:T(8,128)(2,1)S(1)}, bf16[2,2,12,16,128]{4,3,2,1,0:T(8,128)(2,1)S(1)}, u32[]{:S(2)}, u32[]{:S(2)}) collective-permute-start(bf16[2,2,12,16,128]{4,3,2,1,0:T(8,128)(2,1)S(1)} %broadcast_select_fusion.refs_7_), channel_id=1, source_target_pairs={{0,2},{1,3},{2,0},{3,1},{4,6},{5,7},{6,4},{7,5},{8,10},{9,11},{10,... | collective-permute-start | bytes 589832 | tf_op jit(solution)/shard_map/ppermute | solution.py:132
  36.4 7.6 %collective-permute-start.13 = (bf16[2,12,16,128]{3,2,1,0:T(8,128)(2,1)S(1)}, bf16[2,12,16,128]{3,2,1,0:T(8,128)(2,1)S(1)}, u32[]{:S(2)}, u32[]{:S(2)}) collective-permute-start(bf16[2,12,16,128]{3,2,1,0:T(8,128)(2,1)S(1)} %get-tuple-element.21), channel_id=1, source_target_pairs={{0,12},{1,13},{2,14},{3,15},{4,8},{5,9},{6,10},{7,11},{8,4},{9,5},... | collective-permute-start | bytes 294920 | tf_op jit(solution)/shard_map/ppermute | solution.py:132
  39.3 7.0 %collective-permute-start.14 = (bf16[2,12,16,128]{3,2,1,0:T(8,128)(2,1)S(1)}, bf16[2,12,16,128]{3,2,1,0:T(8,128)(2,1)S(1)}, u32[]{:S(2)}, u32[]{:S(2)}) collective-permute-start(bf16[2,12,16,128]{3,2,1,0:T(8,128)(2,1)S(1)} %get-tuple-element.22), channel_id=1, source_target_pairs={{0,8},{1,9},{2,10},{3,11},{4,12},{5,13},{6,14},{7,15},{8,0},{9,1},... | collective-permute-start | bytes 294920 | tf_op jit(solution)/shard_map/ppermute | solution.py:132
  39.5 6.9 %collective-permute-start.15 = (bf16[2,12,16,128]{3,2,1,0:T(8,128)(2,1)S(1)}, bf16[2,12,16,128]{3,2,1,0:T(8,128)(2,1)S(1)}, u32[]{:S(2)}, u32[]{:S(2)}) collective-permute-start(bf16[2,12,16,128]{3,2,1,0:T(8,128)(2,1)S(1)} %get-tuple-element.23), channel_id=1, source_target_pairs={{0,4},{1,5},{2,6},{3,7},{4,0},{5,1},{6,2},{7,3},{8,12},{9,13},{10,... | collective-permute-start | bytes 294920 | tf_op jit(solution)/shard_map/ppermute | solution.py:132
  40.8 6.1 %collective-permute-start.19 = (bf16[2,12,16,128]{3,2,1,0:T(8,128)(2,1)S(1)}, bf16[2,12,16,128]{3,2,1,0:T(8,128)(2,1)S(1)}, u32[]{:S(2)}, u32[]{:S(2)}) collective-permute-start(bf16[2,12,16,128]{3,2,1,0:T(8,128)(2,1)S(1)} %get-tuple-element.24), channel_id=1, source_target_pairs={{0,1},{1,0},{2,3},{3,2},{4,5},{5,4},{6,7},{7,6},{8,9},{9,8},{10,11... | collective-permute-start | bytes 294920 | tf_op jit(solution)/shard_map/ppermute | solution.py:132
  44.0 2.9 %collective-permute-start.16 = (bf16[2,12,16,128]{3,2,1,0:T(8,128)(2,1)S(1)}, bf16[2,12,16,128]{3,2,1,0:T(8,128)(2,1)S(1)}, u32[]{:S(2)}, u32[]{:S(2)}) collective-permute-start(bf16[2,12,16,128]{3,2,1,0:T(8,128)(2,1)S(1)} %collective-permute-done.13), channel_id=1, source_target_pairs={{0,1},{1,0},{2,3},{3,2},{4,5},{5,4},{6,7},{7,6},{8,9},{9,8},{10,11... | collective-permute-start | bytes 294920 | tf_op jit(solution)/shard_map/ppermute | solution.py:132
  46.4 1.3 %collective-permute-start.17 = (bf16[2,12,16,128]{3,2,1,0:T(8,128)(2,1)S(1)}, bf16[2,12,16,128]{3,2,1,0:T(8,128)(2,1)S(1)}, u32[]{:S(2)}, u32[]{:S(2)}) collective-permute-start(bf16[2,12,16,128]{3,2,1,0:T(8,128)(2,1)S(1)} %collective-permute-done.14), channel_id=1, source_target_pairs={{0,1},{1,0},{2,3},{3,2},{4,5},{5,4},{6,7},{7,6},{8,9},{9,8},{10,11... | collective-permute-start | bytes 294920 | tf_op jit(solution)/shard_map/ppermute | solution.py:132
  46.4 1.5 %collective-permute-start.18 = (bf16[2,12,16,128]{3,2,1,0:T(8,128)(2,1)S(1)}, bf16[2,12,16,128]{3,2,1,0:T(8,128)(2,1)S(1)}, u32[]{:S(2)}, u32[]{:S(2)}) collective-permute-start(bf16[2,12,16,128]{3,2,1,0:T(8,128)(2,1)S(1)} %collective-permute-done.15), channel_id=1, source_target_pairs={{0,1},{1,0},{2,3},{3,2},{4,5},{5,4},{6,7},{7,6},{8,9},{9,8},{10,11... | collective-permute-start | bytes 294920 | tf_op jit(solution)/shard_map/ppermute | solution.py:132

commit v8 on v6

--- a/solution.py
+++ b/solution.py
@@ -90,7 +90,7 @@
     s = lax.dot_general(q[...], k, (((2,), (2,)), ((0,), (0,))), preferred_element_type=jnp.float32)
     s = s * (1.0 / math.sqrt(HDIM)) + jnp.concatenate([bias[...]] * (slots // clips), axis=0)[:, None, :]
     e = jnp.exp(s - jnp.max(s, axis=2, keepdims=True))
-    w = (e / jnp.sum(e, axis=2, keepdims=True)).astype(jnp.bfloat16)
+    w = (e * (1.0 / jnp.sum(e, axis=2, keepdims=True))).astype(jnp.bfloat16)
     o = lax.dot_general(w, v, (((2,), (1,)), ((0,), (0,))), preferred_element_type=jnp.float32)
     o = jnp.swapaxes(o.astype(jnp.bfloat16), 0, 1)
     tokens = outs[0].shape[1]
@@ -188,7 +188,7 @@
         crossed[a] = across(after(kv[a], crossed[near[0]][1]))
     q = pl.pallas_call(
         query_kernel, out_shape=jax.ShapeDtypeStruct((slots, outer * 2 * tokens, HDIM), bf),
-        in_specs=[VM] * outer, out_specs=VM, compiler_params=SMALL, cost_estimate=cost(1.3),
+        in_specs=[VM] * outer, out_specs=VM, compiler_params=SMALL, cost_estimate=cost(0.9),
     )(*[qs[a] for a in parts])
     piece = jax.ShapeDtypeStruct((2, tokens, slots, HDIM), bf)
     res = pl.pallas_call(

time: 48.7 us -> 48.7 us (level)
  no operation moved by 1% of the time
where the time goes in v8:
time: 48.7 us; the launch traced here: 48.5 us
  starting transfers between devices  27.4 us (56%)
  waiting for transfers between devices  15.4 us (32%)
  Pallas kernels  4.97 us (10%)
    ppermute x20, starting transfers between devices, swap(): return lax.ppermute(x, 'seq', [(i, i ^ mask) for i in range(devices)])  27.4 us
    ppermute x20, waiting for transfers between devices, swap(): return lax.ppermute(x, 'seq', [(i, i ^ mask) for i in range(devices)])  15.4 us
    pallas_call x5, Pallas kernels, pack(): pl.pallas_call(functools.partial(pack_kernel, outer, len(srcs), partners,...  2.11 us
    pallas_call x1, Pallas kernels, body(): pl.pallas_call(functools.partial(attend_kernel, len(rest)), out_shape=[pi...  1.33 us
  transfers between devices with their start and end apart: 20, of which 9 were waited for; matrix products, arithmetic and copies ran while one was open for 1% of the time, Pallas kernels for 2%

profile of v8, /device:TPU:0, one launch (start us, length us, event | category | flops | bytes accessed | tf_op | source)
XLA Modules:
  0.0 48.5 jit_solution(7492583058639483435)
XLA Ops:
  0.0 0.0 copy-start
  0.0 0.0 copy-start.1
  0.0 1.8 %shard_map.47 = bf16[2,3,12,4,4,128]{5,4,3,2,1,0:T(4,128)(2,1)} custom-call(bf16[12,32,4,128]{3,2,1,0:T(4,128)(2,1)} %bitcast.31, bf16[12,32,4,128]{3,2,1,0:T(4,128)(2,1)} %bitcast.34), custom_call_target="tpu_custom_call" | custom-call | tf_op jit(solution)/shard_map/pallas_call | solution.py:50
  1.8 0.0 copy-start.2
  1.8 0.5 %collective-permute-start = (bf16[2,3,12,16,128]{4,3,2,1,0:T(8,128)(2,1)}, bf16[2,3,12,16,128]{4,3,2,1,0:T(8,128)(2,1)S(1)}, u32[]{:S(2)}, u32[]{:S(2)}) collective-permute-start(bf16[2,3,12,16,128]{4,3,2,1,0:T(8,128)(2,1)} %bitcast.51), channel_id=1, source_target_pairs={{0,1},{1,0},{2,3},{3,2},{4,5},{5,4},{6,7},{7,6},{8,9},{9,8},{10,11... | collective-permute-start | bytes 884744 | tf_op jit(solution)/shard_map/ppermute | solution.py:130
  2.3 0.0 copy-done
  2.3 0.0 copy-done.1
  2.4 0.1 collective-permute-start.2
  2.5 0.3 copy-done.2
  2.8 0.1 shard_map.51
  2.8 0.5 %collective-permute-start.4 = (bf16[1,4,12,16,128]{4,3,2,1,0:T(8,128)(2,1)S(1)}, bf16[1,4,12,16,128]{4,3,2,1,0:T(8,128)(2,1)S(1)}, u32[]{:S(2)}, u32[]{:S(2)}) collective-permute-start(bf16[1,4,12,16,128]{4,3,2,1,0:T(8,128)(2,1)S(1)} %bitcast.41), channel_id=1, source_target_pairs={{0,1},{1,0},{2,3},{3,2},{4,5},{5,4},{6,7},{7,6},{8,9},{9,8},{10,11... | collective-permute-start | bytes 589832 | tf_op jit(solution)/shard_map/ppermute | solution.py:130
  3.4 0.1 shard_map.50
  3.4 0.2 shard_map.46
  3.7 0.1 collective-permute-done
  3.8 3.0 %collective-permute-start.1 = (bf16[2,2,12,16,128]{4,3,2,1,0:T(8,128)(2,1)S(1)}, bf16[2,2,12,16,128]{4,3,2,1,0:T(8,128)(2,1)S(1)}, u32[]{:S(2)}, u32[]{:S(2)}) collective-permute-start(bf16[2,2,12,16,128]{4,3,2,1,0:T(8,128)(2,1)S(1)} %pad_maximum_fusion), channel_id=1, source_target_pairs={{0,4},{1,5},{2,6},{3,7},{4,0},{5,1},{6,2},{7,3},{8,12},{9,13},{10,... | collective-permute-start | bytes 589832 | tf_op jit(solution)/shard_map/ppermute | solution.py:130
  6.8 2.5 %collective-permute-start.9 = (bf16[2,2,12,16,128]{4,3,2,1,0:T(8,128)(2,1)S(1)}, bf16[2,2,12,16,128]{4,3,2,1,0:T(8,128)(2,1)S(1)}, u32[]{:S(2)}, u32[]{:S(2)}) collective-permute-start(bf16[2,2,12,16,128]{4,3,2,1,0:T(8,128)(2,1)S(1)} %pad_maximum_fusion.1), channel_id=1, source_target_pairs={{0,12},{1,13},{2,14},{3,15},{4,8},{5,9},{6,10},{7,11},{8,4},{9,5},... | collective-permute-start | bytes 589832 | tf_op jit(solution)/shard_map/ppermute | solution.py:130
  9.4 2.7 %collective-permute-done.1.refs_2_ = bf16[2,2,12,16,128]{4,3,2,1,0:T(8,128)(2,1)S(1)} collective-permute-done((bf16[2,2,12,16,128]{4,3,2,1,0:T(8,128)(2,1)S(1)}, bf16[2,2,12,16,128]{4,3,2,1,0:T(8,128)(2,1)S(1)}, u32[]{:S(2)}, u32[]{:S(2)}) %collective-permute-start.1) | collective-permute-done | bytes 196640 | tf_op jit(solution)/shard_map/ppermute | solution.py:130
  12.1 0.0 collective-permute-done.2
  12.1 1.7 %collective-permute-start.3 = (bf16[2,2,12,16,128]{4,3,2,1,0:T(8,128)(2,1)S(1)}, bf16[2,2,12,16,128]{4,3,2,1,0:T(8,128)(2,1)S(1)}, u32[]{:S(2)}, u32[]{:S(2)}) collective-permute-start(bf16[2,2,12,16,128]{4,3,2,1,0:T(8,128)(2,1)S(1)} %maximum_select_fusion.refs_0_), channel_id=1, source_target_pairs={{0,2},{1,3},{2,0},{3,1},{4,6},{5,7},{6,4},{7,5},{8,10},{9,11},{10,... | collective-permute-start | bytes 589832 | tf_op jit(solution)/shard_map/ppermute | solution.py:130
  13.8 0.0 collective-permute-done.4
  13.8 0.0 copy-start.3
  13.8 3.5 %collective-permute-start.11 = (bf16[2,2,12,16,128]{4,3,2,1,0:T(8,128)(2,1)S(1)}, bf16[2,2,12,16,128]{4,3,2,1,0:T(8,128)(2,1)S(1)}, u32[]{:S(2)}, u32[]{:S(2)}) collective-permute-start(bf16[2,2,12,16,128]{4,3,2,1,0:T(8,128)(2,1)S(1)} %pad_maximum_fusion.2), channel_id=1, source_target_pairs={{0,8},{1,9},{2,10},{3,11},{4,12},{5,13},{6,14},{7,15},{8,0},{9,1},... | collective-permute-start | bytes 589832 | tf_op jit(solution)/shard_map/ppermute | solution.py:130
  17.3 0.5 %collective-permute-start.8 = (bf16[2,2,12,16,128]{4,3,2,1,0:T(8,128)(2,1)S(1)}, bf16[2,2,12,16,128]{4,3,2,1,0:T(8,128)(2,1)S(1)}, u32[]{:S(2)}, u32[]{:S(2)}) collective-permute-start(bf16[2,2,12,16,128]{4,3,2,1,0:T(8,128)(2,1)S(1)} %collective-permute-done.1.refs_2_), channel_id=1, source_target_pairs={{0,2},{1,3},{2,0},{3,1},{4,6},{5,7},{6,4},{7,5},{8,10},{9,11},{10,... | collective-permute-start | bytes 589832 | tf_op jit(solution)/shard_map/ppermute | solution.py:130
  17.8 1.5 %collective-permute-done.9.refs_1_ = bf16[2,2,12,16,128]{4,3,2,1,0:T(8,128)(2,1)S(1)} collective-permute-done((bf16[2,2,12,16,128]{4,3,2,1,0:T(8,128)(2,1)S(1)}, bf16[2,2,12,16,128]{4,3,2,1,0:T(8,128)(2,1)S(1)}, u32[]{:S(2)}, u32[]{:S(2)}) %collective-permute-start.9) | collective-permute-done | bytes 196640 | tf_op jit(solution)/shard_map/ppermute | solution.py:130
  19.3 1.5 %collective-permute-start.10 = (bf16[2,2,12,16,128]{4,3,2,1,0:T(8,128)(2,1)S(1)}, bf16[2,2,12,16,128]{4,3,2,1,0:T(8,128)(2,1)S(1)}, u32[]{:S(2)}, u32[]{:S(2)}) collective-permute-start(bf16[2,2,12,16,128]{4,3,2,1,0:T(8,128)(2,1)S(1)} %collective-permute-done.9.refs_1_), channel_id=1, source_target_pairs={{0,2},{1,3},{2,0},{3,1},{4,6},{5,7},{6,4},{7,5},{8,10},{9,11},{10,... | collective-permute-start | bytes 589832 | tf_op jit(solution)/shard_map/ppermute | solution.py:130
  20.8 0.0 collective-permute-done.3.refs_1_
  20.8 0.0 copy-done.3
  20.8 0.6 %shard_map.49 = (bf16[16,72,128]{2,1,0:T(8,128)(2,1)S(1)}, bf16[16,72,128]{2,1,0:T(8,128)(2,1)S(1)}, f32[4,192]{1,0:T(4,128)S(1)}) custom-call(s32[4]{0:T(128)S(1)} %copy-done.3, bf16[2,2,12,16,128]{4,3,2,1,0:T(8,128)(2,1)S(1)} %maximum_select_fusion.refs_0_, bf16[2,2,12,16,128]{4,3,2,1,0:T(8,128)(2,1)S(1)} %collective-permute-done.3.refs_1_, ...), custom_call_target="tpu_custom_call" | custom-call | flops 10000000 | bytes 30000 | tf_op jit(solution)/shard_map/pallas_call | solution.py:172
  21.5 4.6 %collective-permute-start.7 = (bf16[1,2,12,16,128]{4,3,2,1,0:T(8,128)(2,1)S(1)}, bf16[1,2,12,16,128]{4,3,2,1,0:T(8,128)(2,1)S(1)}, u32[]{:S(2)}, u32[]{:S(2)}) collective-permute-start(bf16[1,2,12,16,128]{4,3,2,1,0:T(8,128)(2,1)S(1)} %get-tuple-element.34), channel_id=1, source_target_pairs={{0,4},{1,5},{2,6},{3,7},{4,0},{5,1},{6,2},{7,3},{8,12},{9,13},{10,... | collective-permute-start | bytes 294920 | tf_op jit(solution)/shard_map/ppermute | solution.py:130
  26.0 2.0 %collective-permute-start.6 = (bf16[1,2,12,16,128]{4,3,2,1,0:T(8,128)(2,1)S(1)}, bf16[1,2,12,16,128]{4,3,2,1,0:T(8,128)(2,1)S(1)}, u32[]{:S(2)}, u32[]{:S(2)}) collective-permute-start(bf16[1,2,12,16,128]{4,3,2,1,0:T(8,128)(2,1)S(1)} %get-tuple-element.35), channel_id=1, source_target_pairs={{0,8},{1,9},{2,10},{3,11},{4,12},{5,13},{6,14},{7,15},{8,0},{9,1},... | collective-permute-start | bytes 294920 | tf_op jit(solution)/shard_map/ppermute | solution.py:130
  28.0 0.0 collective-permute-done.8.refs_0_
  28.0 1.4 %collective-permute-start.5 = (bf16[1,2,12,16,128]{4,3,2,1,0:T(8,128)(2,1)S(1)}, bf16[1,2,12,16,128]{4,3,2,1,0:T(8,128)(2,1)S(1)}, u32[]{:S(2)}, u32[]{:S(2)}) collective-permute-start(bf16[1,2,12,16,128]{4,3,2,1,0:T(8,128)(2,1)S(1)} %get-tuple-element.36), channel_id=1, source_target_pairs={{0,12},{1,13},{2,14},{3,15},{4,8},{5,9},{6,10},{7,11},{8,4},{9,5},... | collective-permute-start | bytes 294920 | tf_op jit(solution)/shard_map/ppermute | solution.py:130
  29.4 0.0 collective-permute-done.11
  29.4 0.7 %collective-permute-start.12 = (bf16[2,2,12,16,128]{4,3,2,1,0:T(8,128)(2,1)S(1)}, bf16[2,2,12,16,128]{4,3,2,1,0:T(8,128)(2,1)S(1)}, u32[]{:S(2)}, u32[]{:S(2)}) collective-permute-start(bf16[2,2,12,16,128]{4,3,2,1,0:T(8,128)(2,1)S(1)} %broadcast_select_fusion.refs_3_), channel_id=1, source_target_pairs={{0,2},{1,3},{2,0},{3,1},{4,6},{5,7},{6,4},{7,5},{8,10},{9,11},{10,... | collective-permute-start | bytes 589832 | tf_op jit(solution)/shard_map/ppermute | solution.py:130
  30.1 0.0 collective-permute-done.7.refs_2_
  30.1 4.6 %collective-permute-done.6.refs_1_ = bf16[1,2,12,16,128]{4,3,2,1,0:T(8,128)(2,1)S(1)} collective-permute-done((bf16[1,2,12,16,128]{4,3,2,1,0:T(8,128)(2,1)S(1)}, bf16[1,2,12,16,128]{4,3,2,1,0:T(8,128)(2,1)S(1)}, u32[]{:S(2)}, u32[]{:S(2)}) %collective-permute-start.6) | collective-permute-done | bytes 98336 | tf_op jit(solution)/shard_map/ppermute | solution.py:130
  34.8 0.0 collective-permute-done.5.refs_0_
  34.8 0.1 shard_map.52.q
  34.9 0.0 collective-permute-done.10.refs_2_
  34.9 0.3 collective-permute-done.12.refs_4_
  35.2 1.3 %shard_map.53 = (bf16[2,12,16,128]{3,2,1,0:T(8,128)(2,1)S(1)}, bf16[2,12,16,128]{3,2,1,0:T(8,128)(2,1)S(1)}, bf16[2,12,16,128]{3,2,1,0:T(8,128)(2,1)S(1)}, bf16[2,12,16,128]{3,2,1,0:T(8,128)(2,1)S(1)}) custom-call(bf16[16,96,128]{2,1,0:T(8,128)(2,1)S(1)} %shard_map.52.q, bf16[2,2,12,16,128]{4,3,2,1,0:T(8,128)(2,1)S(1)} %collective-permute-done.8.refs_0_, ...), custom_call_target="tpu_custom_call" | custom-call | flops 2000000000 | bytes 6000000 | tf_op jit(solution)/shard_map/pallas_call | solution.py:194
  36.5 3.0 %collective-permute-start.13 = (bf16[2,12,16,128]{3,2,1,0:T(8,128)(2,1)S(1)}, bf16[2,12,16,128]{3,2,1,0:T(8,128)(2,1)S(1)}, u32[]{:S(2)}, u32[]{:S(2)}) collective-permute-start(bf16[2,12,16,128]{3,2,1,0:T(8,128)(2,1)S(1)} %get-tuple-element.15), channel_id=1, source_target_pairs={{0,12},{1,13},{2,14},{3,15},{4,8},{5,9},{6,10},{7,11},{8,4},{9,5},... | collective-permute-start | bytes 294920 | tf_op jit(solution)/shard_map/ppermute | solution.py:130
  39.5 0.0 collective-permute-start.14
  39.5 1.5 %collective-permute-start.15 = (bf16[2,12,16,128]{3,2,1,0:T(8,128)(2,1)S(1)}, bf16[2,12,16,128]{3,2,1,0:T(8,128)(2,1)S(1)}, u32[]{:S(2)}, u32[]{:S(2)}) collective-permute-start(bf16[2,12,16,128]{3,2,1,0:T(8,128)(2,1)S(1)} %get-tuple-element.17), channel_id=1, source_target_pairs={{0,4},{1,5},{2,6},{3,7},{4,0},{5,1},{6,2},{7,3},{8,12},{9,13},{10,... | collective-permute-start | bytes 294920 | tf_op jit(solution)/shard_map/ppermute | solution.py:130
  41.0 0.0 collective-permute-start.19
  41.0 3.0 %collective-permute-done.13 = bf16[2,12,16,128]{3,2,1,0:T(8,128)(2,1)S(1)} collective-permute-done((bf16[2,12,16,128]{3,2,1,0:T(8,128)(2,1)S(1)}, bf16[2,12,16,128]{3,2,1,0:T(8,128)(2,1)S(1)}, u32[]{:S(2)}, u32[]{:S(2)}) %collective-permute-start.13) | collective-permute-done | bytes 98336 | tf_op jit(solution)/shard_map/ppermute | solution.py:130
  43.9 0.0 collective-permute-start.16
  43.9 2.3 %collective-permute-done.14 = bf16[2,12,16,128]{3,2,1,0:T(8,128)(2,1)S(1)} collective-permute-done((bf16[2,12,16,128]{3,2,1,0:T(8,128)(2,1)S(1)}, bf16[2,12,16,128]{3,2,1,0:T(8,128)(2,1)S(1)}, u32[]{:S(2)}, u32[]{:S(2)}) %collective-permute-start.14) | collective-permute-done | bytes 98336 | tf_op jit(solution)/shard_map/ppermute | solution.py:130
  46.3 0.0 collective-permute-start.17
  46.3 0.0 collective-permute-done.15
  46.3 0.5 %collective-permute-start.18 = (bf16[2,12,16,128]{3,2,1,0:T(8,128)(2,1)S(1)}, bf16[2,12,16,128]{3,2,1,0:T(8,128)(2,1)S(1)}, u32[]{:S(2)}, u32[]{:S(2)}) collective-permute-start(bf16[2,12,16,128]{3,2,1,0:T(8,128)(2,1)S(1)} %collective-permute-done.15), channel_id=1, source_target_pairs={{0,1},{1,0},{2,3},{3,2},{4,5},{5,4},{6,7},{7,6},{8,9},{9,8},{10,11... | collective-permute-start | bytes 294920 | tf_op jit(solution)/shard_map/ppermute | solution.py:130
  46.8 0.0 collective-permute-done.19
  46.8 0.0 collective-permute-done.16
  46.8 0.8 %collective-permute-done.17 = bf16[2,12,16,128]{3,2,1,0:T(8,128)(2,1)S(1)} collective-permute-done((bf16[2,12,16,128]{3,2,1,0:T(8,128)(2,1)S(1)}, bf16[2,12,16,128]{3,2,1,0:T(8,128)(2,1)S(1)}, u32[]{:S(2)}, u32[]{:S(2)}) %collective-permute-start.17) | collective-permute-done | bytes 98336 | tf_op jit(solution)/shard_map/ppermute | solution.py:130
  47.6 0.2 collective-permute-done.18
  47.8 0.8 %shard_map.54 = bf16[12,32,4,128]{3,2,1,0:T(4,128)(2,1)} custom-call(bf16[2,12,4,4,128]{4,3,2,1,0:T(4,128)(2,1)S(1)} %bitcast.44, bf16[2,12,4,4,128]{4,3,2,1,0:T(4,128)(2,1)S(1)} %bitcast.45, bf16[2,12,4,4,128]{4,3,2,1,0:T(4,128)(2,1)S(1)} %bitcast.46, bf16[2,12,4,4,128]{4,3,2,1,0:T(4,128)(2,1)S(1)} %bitcast.42, bf16[2,12,4,4,128]{4,3,2,1,0:T(4,128)(2,1)S(1)} %bitcast.48, ...), custom_call_target="tpu_custom_call" | custom-call | tf_op jit(solution)/shard_map/pallas_call | solution.py:203
  (15 shorter events, 0.3 us)
Async XLA Ops:
  0.0 2.3 %copy-start = (bf16[12,4,4096]{2,1,0:T(4,128)(2,1)S(1)}, bf16[12,4,4096]{2,1,0:T(4,128)(2,1)}, u32[]{:S(2)}) copy-start(bf16[12,4,4096]{2,1,0:T(4,128)(2,1)} %param.5) | copy-start | bytes 1179652
  0.0 2.3 %copy-start.1 = (bf16[12,4,4096]{2,1,0:T(4,128)(2,1)S(1)}, bf16[12,4,4096]{2,1,0:T(4,128)(2,1)}, u32[]{:S(2)}) copy-start(bf16[12,4,4096]{2,1,0:T(4,128)(2,1)} %param.6) | copy-start | bytes 1179652
  1.8 1.0 %copy-start.2 = (bf16[12,4,4096]{2,1,0:T(4,128)(2,1)S(1)}, bf16[12,4,4096]{2,1,0:T(4,128)(2,1)}, u32[]{:S(2)}) copy-start(bf16[12,4,4096]{2,1,0:T(4,128)(2,1)} %param.4) | copy-start | bytes 1179652
  1.8 1.9 %collective-permute-start = (bf16[2,3,12,16,128]{4,3,2,1,0:T(8,128)(2,1)}, bf16[2,3,12,16,128]{4,3,2,1,0:T(8,128)(2,1)S(1)}, u32[]{:S(2)}, u32[]{:S(2)}) collective-permute-start(bf16[2,3,12,16,128]{4,3,2,1,0:T(8,128)(2,1)} %bitcast.51), channel_id=1, source_target_pairs={{0,1},{1,0},{2,3},{3,2},{4,5},{5,4},{6,7},{7,6},{8,9},{9,8},{10,11... | collective-permute-start | bytes 884744 | tf_op jit(solution)/shard_map/ppermute | solution.py:130
  2.4 9.7 %collective-permute-start.2 = (bf16[2,1,12,16,128]{4,3,2,1,0:T(8,128)(2,1)S(1)}, bf16[2,1,12,16,128]{4,3,2,1,0:T(8,128)(2,1)S(1)}, u32[]{:S(2)}, u32[]{:S(2)}) collective-permute-start(bf16[2,1,12,16,128]{4,3,2,1,0:T(8,128)(2,1)S(1)} %bitcast.43), channel_id=1, source_target_pairs={{0,1},{1,0},{2,3},{3,2},{4,5},{5,4},{6,7},{7,6},{8,9},{9,8},{10,11... | collective-permute-start | bytes 294920 | tf_op jit(solution)/shard_map/ppermute | solution.py:130
  2.8 10.9 %collective-permute-start.4 = (bf16[1,4,12,16,128]{4,3,2,1,0:T(8,128)(2,1)S(1)}, bf16[1,4,12,16,128]{4,3,2,1,0:T(8,128)(2,1)S(1)}, u32[]{:S(2)}, u32[]{:S(2)}) collective-permute-start(bf16[1,4,12,16,128]{4,3,2,1,0:T(8,128)(2,1)S(1)} %bitcast.41), channel_id=1, source_target_pairs={{0,1},{1,0},{2,3},{3,2},{4,5},{5,4},{6,7},{7,6},{8,9},{9,8},{10,11... | collective-permute-start | bytes 589832 | tf_op jit(solution)/shard_map/ppermute | solution.py:130
  3.8 8.3 %collective-permute-start.1 = (bf16[2,2,12,16,128]{4,3,2,1,0:T(8,128)(2,1)S(1)}, bf16[2,2,12,16,128]{4,3,2,1,0:T(8,128)(2,1)S(1)}, u32[]{:S(2)}, u32[]{:S(2)}) collective-permute-start(bf16[2,2,12,16,128]{4,3,2,1,0:T(8,128)(2,1)S(1)} %pad_maximum_fusion), channel_id=1, source_target_pairs={{0,4},{1,5},{2,6},{3,7},{4,0},{5,1},{6,2},{7,3},{8,12},{9,13},{10,... | collective-permute-start | bytes 589832 | tf_op jit(solution)/shard_map/ppermute | solution.py:130
  6.8 12.5 %collective-permute-start.9 = (bf16[2,2,12,16,128]{4,3,2,1,0:T(8,128)(2,1)S(1)}, bf16[2,2,12,16,128]{4,3,2,1,0:T(8,128)(2,1)S(1)}, u32[]{:S(2)}, u32[]{:S(2)}) collective-permute-start(bf16[2,2,12,16,128]{4,3,2,1,0:T(8,128)(2,1)S(1)} %pad_maximum_fusion.1), channel_id=1, source_target_pairs={{0,12},{1,13},{2,14},{3,15},{4,8},{5,9},{6,10},{7,11},{8,4},{9,5},... | collective-permute-start | bytes 589832 | tf_op jit(solution)/shard_map/ppermute | solution.py:130
  12.1 8.7 %collective-permute-start.3 = (bf16[2,2,12,16,128]{4,3,2,1,0:T(8,128)(2,1)S(1)}, bf16[2,2,12,16,128]{4,3,2,1,0:T(8,128)(2,1)S(1)}, u32[]{:S(2)}, u32[]{:S(2)}) collective-permute-start(bf16[2,2,12,16,128]{4,3,2,1,0:T(8,128)(2,1)S(1)} %maximum_select_fusion.refs_0_), channel_id=1, source_target_pairs={{0,2},{1,3},{2,0},{3,1},{4,6},{5,7},{6,4},{7,5},{8,10},{9,11},{10,... | collective-permute-start | bytes 589832 | tf_op jit(solution)/shard_map/ppermute | solution.py:130
  13.8 7.0 %copy-start.3 = (s32[4]{0:T(128)S(1)}, s32[4]{0:T(128)}, u32[]{:S(2)}) copy-start(s32[4]{0:T(128)} %frames_ref.1) | copy-start | bytes 52
  13.8 15.6 %collective-permute-start.11 = (bf16[2,2,12,16,128]{4,3,2,1,0:T(8,128)(2,1)S(1)}, bf16[2,2,12,16,128]{4,3,2,1,0:T(8,128)(2,1)S(1)}, u32[]{:S(2)}, u32[]{:S(2)}) collective-permute-start(bf16[2,2,12,16,128]{4,3,2,1,0:T(8,128)(2,1)S(1)} %pad_maximum_fusion.2), channel_id=1, source_target_pairs={{0,8},{1,9},{2,10},{3,11},{4,12},{5,13},{6,14},{7,15},{8,0},{9,1},... | collective-permute-start | bytes 589832 | tf_op jit(solution)/shard_map/ppermute | solution.py:130
  17.3 10.8 %collective-permute-start.8 = (bf16[2,2,12,16,128]{4,3,2,1,0:T(8,128)(2,1)S(1)}, bf16[2,2,12,16,128]{4,3,2,1,0:T(8,128)(2,1)S(1)}, u32[]{:S(2)}, u32[]{:S(2)}) collective-permute-start(bf16[2,2,12,16,128]{4,3,2,1,0:T(8,128)(2,1)S(1)} %collective-permute-done.1.refs_2_), channel_id=1, source_target_pairs={{0,2},{1,3},{2,0},{3,1},{4,6},{5,7},{6,4},{7,5},{8,10},{9,11},{10,... | collective-permute-start | bytes 589832 | tf_op jit(solution)/shard_map/ppermute | solution.py:130
  19.3 15.6 %collective-permute-start.10 = (bf16[2,2,12,16,128]{4,3,2,1,0:T(8,128)(2,1)S(1)}, bf16[2,2,12,16,128]{4,3,2,1,0:T(8,128)(2,1)S(1)}, u32[]{:S(2)}, u32[]{:S(2)}) collective-permute-start(bf16[2,2,12,16,128]{4,3,2,1,0:T(8,128)(2,1)S(1)} %collective-permute-done.9.refs_1_), channel_id=1, source_target_pairs={{0,2},{1,3},{2,0},{3,1},{4,6},{5,7},{6,4},{7,5},{8,10},{9,11},{10,... | collective-permute-start | bytes 589832 | tf_op jit(solution)/shard_map/ppermute | solution.py:130
  21.5 8.7 %collective-permute-start.7 = (bf16[1,2,12,16,128]{4,3,2,1,0:T(8,128)(2,1)S(1)}, bf16[1,2,12,16,128]{4,3,2,1,0:T(8,128)(2,1)S(1)}, u32[]{:S(2)}, u32[]{:S(2)}) collective-permute-start(bf16[1,2,12,16,128]{4,3,2,1,0:T(8,128)(2,1)S(1)} %get-tuple-element.34), channel_id=1, source_target_pairs={{0,4},{1,5},{2,6},{3,7},{4,0},{5,1},{6,2},{7,3},{8,12},{9,13},{10,... | collective-permute-start | bytes 294920 | tf_op jit(solution)/shard_map/ppermute | solution.py:130
  26.0 8.7 %collective-permute-start.6 = (bf16[1,2,12,16,128]{4,3,2,1,0:T(8,128)(2,1)S(1)}, bf16[1,2,12,16,128]{4,3,2,1,0:T(8,128)(2,1)S(1)}, u32[]{:S(2)}, u32[]{:S(2)}) collective-permute-start(bf16[1,2,12,16,128]{4,3,2,1,0:T(8,128)(2,1)S(1)} %get-tuple-element.35), channel_id=1, source_target_pairs={{0,8},{1,9},{2,10},{3,11},{4,12},{5,13},{6,14},{7,15},{8,0},{9,1},... | collective-permute-start | bytes 294920 | tf_op jit(solution)/shard_map/ppermute | solution.py:130
  28.0 6.7 %collective-permute-start.5 = (bf16[1,2,12,16,128]{4,3,2,1,0:T(8,128)(2,1)S(1)}, bf16[1,2,12,16,128]{4,3,2,1,0:T(8,128)(2,1)S(1)}, u32[]{:S(2)}, u32[]{:S(2)}) collective-permute-start(bf16[1,2,12,16,128]{4,3,2,1,0:T(8,128)(2,1)S(1)} %get-tuple-element.36), channel_id=1, source_target_pairs={{0,12},{1,13},{2,14},{3,15},{4,8},{5,9},{6,10},{7,11},{8,4},{9,5},... | collective-permute-start | bytes 294920 | tf_op jit(solution)/shard_map/ppermute | solution.py:130
  29.4 5.7 %collective-permute-start.12 = (bf16[2,2,12,16,128]{4,3,2,1,0:T(8,128)(2,1)S(1)}, bf16[2,2,12,16,128]{4,3,2,1,0:T(8,128)(2,1)S(1)}, u32[]{:S(2)}, u32[]{:S(2)}) collective-permute-start(bf16[2,2,12,16,128]{4,3,2,1,0:T(8,128)(2,1)S(1)} %broadcast_select_fusion.refs_3_), channel_id=1, source_target_pairs={{0,2},{1,3},{2,0},{3,1},{4,6},{5,7},{6,4},{7,5},{8,10},{9,11},{10,... | collective-permute-start | bytes 589832 | tf_op jit(solution)/shard_map/ppermute | solution.py:130
  36.5 7.4 %collective-permute-start.13 = (bf16[2,12,16,128]{3,2,1,0:T(8,128)(2,1)S(1)}, bf16[2,12,16,128]{3,2,1,0:T(8,128)(2,1)S(1)}, u32[]{:S(2)}, u32[]{:S(2)}) collective-permute-start(bf16[2,12,16,128]{3,2,1,0:T(8,128)(2,1)S(1)} %get-tuple-element.15), channel_id=1, source_target_pairs={{0,12},{1,13},{2,14},{3,15},{4,8},{5,9},{6,10},{7,11},{8,4},{9,5},... | collective-permute-start | bytes 294920 | tf_op jit(solution)/shard_map/ppermute | solution.py:130
  39.5 6.8 %collective-permute-start.14 = (bf16[2,12,16,128]{3,2,1,0:T(8,128)(2,1)S(1)}, bf16[2,12,16,128]{3,2,1,0:T(8,128)(2,1)S(1)}, u32[]{:S(2)}, u32[]{:S(2)}) collective-permute-start(bf16[2,12,16,128]{3,2,1,0:T(8,128)(2,1)S(1)} %get-tuple-element.16), channel_id=1, source_target_pairs={{0,8},{1,9},{2,10},{3,11},{4,12},{5,13},{6,14},{7,15},{8,0},{9,1},... | collective-permute-start | bytes 294920 | tf_op jit(solution)/shard_map/ppermute | solution.py:130
  39.5 6.8 %collective-permute-start.15 = (bf16[2,12,16,128]{3,2,1,0:T(8,128)(2,1)S(1)}, bf16[2,12,16,128]{3,2,1,0:T(8,128)(2,1)S(1)}, u32[]{:S(2)}, u32[]{:S(2)}) collective-permute-start(bf16[2,12,16,128]{3,2,1,0:T(8,128)(2,1)S(1)} %get-tuple-element.17), channel_id=1, source_target_pairs={{0,4},{1,5},{2,6},{3,7},{4,0},{5,1},{6,2},{7,3},{8,12},{9,13},{10,... | collective-permute-start | bytes 294920 | tf_op jit(solution)/shard_map/ppermute | solution.py:130
  41.0 5.8 %collective-permute-start.19 = (bf16[2,12,16,128]{3,2,1,0:T(8,128)(2,1)S(1)}, bf16[2,12,16,128]{3,2,1,0:T(8,128)(2,1)S(1)}, u32[]{:S(2)}, u32[]{:S(2)}) collective-permute-start(bf16[2,12,16,128]{3,2,1,0:T(8,128)(2,1)S(1)} %get-tuple-element.18), channel_id=1, source_target_pairs={{0,1},{1,0},{2,3},{3,2},{4,5},{5,4},{6,7},{7,6},{8,9},{9,8},{10,11... | collective-permute-start | bytes 294920 | tf_op jit(solution)/shard_map/ppermute | solution.py:130
  43.9 2.9 %collective-permute-start.16 = (bf16[2,12,16,128]{3,2,1,0:T(8,128)(2,1)S(1)}, bf16[2,12,16,128]{3,2,1,0:T(8,128)(2,1)S(1)}, u32[]{:S(2)}, u32[]{:S(2)}) collective-permute-start(bf16[2,12,16,128]{3,2,1,0:T(8,128)(2,1)S(1)} %collective-permute-done.13), channel_id=1, source_target_pairs={{0,1},{1,0},{2,3},{3,2},{4,5},{5,4},{6,7},{7,6},{8,9},{9,8},{10,11... | collective-permute-start | bytes 294920 | tf_op jit(solution)/shard_map/ppermute | solution.py:130
  46.3 1.3 %collective-permute-start.17 = (bf16[2,12,16,128]{3,2,1,0:T(8,128)(2,1)S(1)}, bf16[2,12,16,128]{3,2,1,0:T(8,128)(2,1)S(1)}, u32[]{:S(2)}, u32[]{:S(2)}) collective-permute-start(bf16[2,12,16,128]{3,2,1,0:T(8,128)(2,1)S(1)} %collective-permute-done.14), channel_id=1, source_target_pairs={{0,1},{1,0},{2,3},{3,2},{4,5},{5,4},{6,7},{7,6},{8,9},{9,8},{10,11... | collective-permute-start | bytes 294920 | tf_op jit(solution)/shard_map/ppermute | solution.py:130
  46.3 1.5 %collective-permute-start.18 = (bf16[2,12,16,128]{3,2,1,0:T(8,128)(2,1)S(1)}, bf16[2,12,16,128]{3,2,1,0:T(8,128)(2,1)S(1)}, u32[]{:S(2)}, u32[]{:S(2)}) collective-permute-start(bf16[2,12,16,128]{3,2,1,0:T(8,128)(2,1)S(1)} %collective-permute-done.15), channel_id=1, source_target_pairs={{0,1},{1,0},{2,3},{3,2},{4,5},{5,4},{6,7},{7,6},{8,9},{9,8},{10,11... | collective-permute-start | bytes 294920 | tf_op jit(solution)/shard_map/ppermute | solution.py:130
